TPU v7x, 32 devices: a whole 2x2x4 slice. The times are simulated.
32 devices in a mesh: seq: 4 (over z), batch: 8 (over y, x, core).
Axes of the slice: x: 2, y: 2, z: 4, core: 2. Of those that a mesh axis runs over, the one named last changes fastest.
Arguments:
- tokens: bfloat16 [64, 1024, 512], P('batch', 'seq'), may hold values from -6 to 6
- cotangent: bfloat16 [64, 1024, 512], P('batch', 'seq'), may hold values from -6 to 6
- expert_index: int32 [64, 1024, 2], P('batch', 'seq'), may hold values from 0 to 7, all different within a row
- segments: int32 [64, 1024], P('batch'), may hold values from 0 to 32, as said below
- ln1_gain: bfloat16 [512], P(('seq', 'batch')), may hold values from 0.5 to 1.5
- ln1_bias: bfloat16 [512], P(('seq', 'batch')), may hold values from -4 to 4
- w_router: bfloat16 [512, 8], P(('seq', 'batch')), may hold values from -0.1875 to 0.1875
- w_query: bfloat16 [512, 512], P(('seq', 'batch')), may hold values from -0.25 to 0.25
- b_query: bfloat16 [512], P(('seq', 'batch')), may hold values from -4 to 4
- w_keyval: bfloat16 [512, 128], P(('seq', 'batch')), may hold values from -0.25 to 0.25
- w_out: bfloat16 [512, 512], P(('seq', 'batch')), may hold values from -2 to 2
- b_out: bfloat16 [512], P(('seq', 'batch')), may hold values from -4 to 4
- ln2_gain: bfloat16 [512], P(('seq', 'batch')), may hold values from 0.5 to 1.5
- ln2_bias: bfloat16 [512], P(('seq', 'batch')), may hold values from -4 to 4
- w_up: bfloat16 [512, 2048], P(('seq', 'batch')), may hold values from -0.25 to 0.25
- b_up: bfloat16 [2048], P(('seq', 'batch')), may hold values from -4 to 4
- w_down: bfloat16 [2048, 512], P(('seq', 'batch')), may hold values from -0.125 to 0.125
- b_down: bfloat16 [512], P(('seq', 'batch')), may hold values from -4 to 4
Outputs:
- output: bfloat16 [64, 1024, 512], P('batch', 'seq')
- grad_tokens: bfloat16 [64, 1024, 512], P('batch', 'seq')
- grad_ln1_gain: float32 [512], P(('seq', 'batch'))
- grad_ln1_bias: float32 [512], P(('seq', 'batch'))
- grad_w_router: float32 [512, 8], P(('seq', 'batch'))
- grad_w_query: float32 [512, 512], P(('seq', 'batch'))
- grad_b_query: float32 [512], P(('seq', 'batch'))
- grad_w_keyval: float32 [512, 128], P(('seq', 'batch'))
- grad_w_out: float32 [512, 512], P(('seq', 'batch'))
- grad_b_out: float32 [512], P(('seq', 'batch'))
- grad_ln2_gain: float32 [512], P(('seq', 'batch'))
- grad_ln2_bias: float32 [512], P(('seq', 'batch'))
- grad_w_up: float32 [512, 2048], P(('seq', 'batch'))
- grad_b_up: float32 [2048], P(('seq', 'batch'))
- grad_w_down: float32 [2048, 512], P(('seq', 'batch'))
- grad_b_down: float32 [512], P(('seq', 'batch'))
Inputs may be any that keep to these rules, and one draw needn't show every extreme that they name: `segments`: each row's segment numbers start at 0, rise by 0 or 1 from one position to the next and end at 32; in one row of each aligned group of 8 rows one segment covers positions 128 to 895.
All inputs are finite; a program needn't handle non-finite values.
Results may differ from a plain program's by a relative error of at most 0.012.
Values may be sent and summed in bfloat16 or wider, within the bound.
No kernel may reach another device: no remote copies, remote signals or barrier semaphores. Data moves between devices by JAX's collectives and lax.ppermute only.
A program may use at most 128 MiB of HBM per device.

v0:
```python
import jax
import jax.numpy as jnp
from jax import lax
from jax.sharding import PartitionSpec as P

epsilon = 1e-05
neg_large = -1e30


def normalize(values, gain, shift):
    centered = values - jnp.mean(values, axis=-1, keepdims=True)
    spread = jnp.mean(centered * centered, axis=-1, keepdims=True)
    return centered * lax.rsqrt(spread + epsilon) * gain + shift


def masked_scores(row_query, key_part, seg_query, seg_keys, scale):
    scores = (
        jnp.einsum("ceh,kh->eck", row_query, key_part, preferred_element_type=jnp.float32) * scale
    )
    matches = seg_query[:, None] == seg_keys[None, :]
    return jnp.where(matches[None], scores, neg_large)


def spread_slots(picked_one_hot, slot_values):
    return jnp.sum(picked_one_hot[..., None] * slot_values[:, :, :, None, :], axis=2)


def body(
    tokens,
    cotangent,
    expert_index,
    segments,
    ln1_gain,
    ln1_bias,
    w_router,
    w_query,
    b_query,
    w_keyval,
    w_out,
    b_out,
    ln2_gain,
    ln2_bias,
    w_up,
    b_up,
    w_down,
    b_down,
):
    every_full = (
        lax.all_gather(ln1_gain, ("seq", "batch"), axis=0, tiled=True),
        lax.all_gather(ln1_bias, ("seq", "batch"), axis=0, tiled=True),
        lax.all_gather(w_router, ("seq", "batch"), axis=0, tiled=True),
        lax.all_gather(w_query, ("seq", "batch"), axis=0, tiled=True),
        lax.all_gather(b_query, ("seq", "batch"), axis=0, tiled=True),
        lax.all_gather(w_keyval, ("seq", "batch"), axis=0, tiled=True),
        lax.all_gather(w_out, ("seq", "batch"), axis=0, tiled=True),
        lax.all_gather(b_out, ("seq", "batch"), axis=0, tiled=True),
        lax.all_gather(ln2_gain, ("seq", "batch"), axis=0, tiled=True),
        lax.all_gather(ln2_bias, ("seq", "batch"), axis=0, tiled=True),
        lax.all_gather(w_up, ("seq", "batch"), axis=0, tiled=True),
        lax.all_gather(b_up, ("seq", "batch"), axis=0, tiled=True),
        lax.all_gather(w_down, ("seq", "batch"), axis=0, tiled=True),
        lax.all_gather(b_down, ("seq", "batch"), axis=0, tiled=True),
    )
    attn_full = every_full[:8]
    (
        gain_first,
        shift_first,
        router_full,
        query_full,
        query_bias,
        keyval_full,
        out_full,
        out_bias,
    ) = attn_full
    gain_first = gain_first.astype(jnp.float32)
    shift_first = shift_first.astype(jnp.float32)
    rows_dev, local_len, model_width = tokens.shape
    experts = router_full.shape[1]
    heads = query_full.shape[1]
    head_size = keyval_full.shape[1] // 2
    scale = head_size ** (-0.5)
    inputs = tokens.astype(jnp.float32)
    normed = normalize(inputs, gain_first, shift_first)
    normed_low = normed.astype(jnp.bfloat16)
    logits = jnp.einsum("rcd,de->rce", normed_low, router_full, preferred_element_type=jnp.float32)
    one_hot = (expert_index[..., None] == jnp.arange(experts, dtype=jnp.int32)).astype(jnp.float32)
    chosen = jnp.sum(one_hot, axis=2)
    shifted = jnp.exp(logits - jnp.max(logits, axis=-1, keepdims=True)) * chosen
    gates = shifted / jnp.sum(shifted, axis=-1, keepdims=True)
    gate_slots = jnp.take_along_axis(gates, expert_index, axis=2)
    queries = (
        jnp.einsum("rcd,df->rcf", normed_low, query_full, preferred_element_type=jnp.float32)
        + query_bias.astype(jnp.float32)
    ).astype(jnp.bfloat16)
    queries = queries.reshape(rows_dev, local_len, experts, head_size)
    query_slots = jnp.take_along_axis(queries, expert_index[..., None], axis=2)
    keyval_local = jnp.einsum(
        "rcd,df->rcf", normed_low, keyval_full, preferred_element_type=jnp.float32
    ).astype(jnp.bfloat16)
    keyval_row = lax.all_gather(keyval_local, "seq", axis=1, tiled=True)
    offset = lax.axis_index("seq") * local_len
    query_seg = lax.dynamic_slice_in_dim(segments, offset, local_len, 1)

    def attend_row(operands):
        row_query, row_keyval, seg_query, seg_keys = operands
        scores = masked_scores(row_query, row_keyval[:, :head_size], seg_query, seg_keys, scale)
        highest = jnp.max(scores, axis=-1, keepdims=True)
        numerator = jnp.exp(scores - highest)
        total = jnp.sum(numerator, axis=-1, keepdims=True)
        attention = (numerator / total).astype(jnp.bfloat16)
        context_row = jnp.einsum(
            "eck,kh->ceh", attention, row_keyval[:, head_size:], preferred_element_type=jnp.float32
        )
        return (context_row, highest[..., 0] + jnp.log(total[..., 0]))

    context_slots, logsum = lax.map(attend_row, (query_slots, keyval_row, query_seg, segments))
    mixed_slots = gate_slots[..., None] * context_slots
    mixed = (
        spread_slots(one_hot, mixed_slots).astype(jnp.bfloat16).reshape(rows_dev, local_len, heads)
    )
    attended = jnp.einsum(
        "rcf,fd->rcd", mixed, out_full, preferred_element_type=jnp.float32
    ) + out_bias.astype(jnp.float32)
    middle = inputs + attended
    ffn_full = every_full[8:]
    gain_second, shift_second, up_full, up_bias, down_full, down_bias = ffn_full
    gain_second = gain_second.astype(jnp.float32)
    shift_second = shift_second.astype(jnp.float32)
    normed_two = normalize(middle, gain_second, shift_second)
    normed_two_low = normed_two.astype(jnp.bfloat16)
    hidden = jnp.einsum(
        "rcd,df->rcf", normed_two_low, up_full, preferred_element_type=jnp.float32
    ) + up_bias.astype(jnp.float32)
    active, gelu_pull = jax.vjp(jax.nn.gelu, hidden)
    active_low = active.astype(jnp.bfloat16)
    output = middle + (
        jnp.einsum("rcf,fd->rcd", active_low, down_full, preferred_element_type=jnp.float32)
        + down_bias.astype(jnp.float32)
    )
    grad_out = cotangent.astype(jnp.float32)
    grad_down_bias = jnp.sum(grad_out, axis=(0, 1))
    grad_down = jnp.einsum("rcf,rcd->fd", active_low, cotangent, preferred_element_type=jnp.float32)
    grad_active = jnp.einsum(
        "rcd,fd->rcf", cotangent, down_full, preferred_element_type=jnp.float32
    )
    grad_hidden = gelu_pull(grad_active)[0].astype(jnp.bfloat16)
    grad_up_bias = jnp.sum(grad_hidden.astype(jnp.float32), axis=(0, 1))
    grad_up = jnp.einsum(
        "rcd,rcf->df", normed_two_low, grad_hidden, preferred_element_type=jnp.float32
    )
    grad_normed_two = jnp.einsum(
        "rcf,df->rcd", grad_hidden, up_full, preferred_element_type=jnp.float32
    )
    unused_two, second_pull = jax.vjp(normalize, middle, gain_second, shift_second)
    grad_middle_part, grad_gain_second, grad_shift_second = second_pull(grad_normed_two)
    grad_middle = grad_out + grad_middle_part
    grad_att_low = grad_middle.astype(jnp.bfloat16)
    grad_out_bias = jnp.sum(grad_att_low.astype(jnp.float32), axis=(0, 1))
    grad_out_w = jnp.einsum("rcf,rcd->fd", mixed, grad_att_low, preferred_element_type=jnp.float32)
    grad_mixed = jnp.einsum(
        "rcd,fd->rcf", grad_att_low, out_full, preferred_element_type=jnp.float32
    )
    grad_mixed = grad_mixed.reshape(rows_dev, local_len, experts, head_size)
    grad_mixed_slots = jnp.take_along_axis(grad_mixed, expert_index[..., None], axis=2)
    grad_gate_slots = jnp.sum(grad_mixed_slots * context_slots, axis=-1)
    grad_context = (gate_slots[..., None] * grad_mixed_slots).astype(jnp.bfloat16)

    def back_row(operands):
        row_query, row_keyval, seg_query, seg_keys, row_logsum, row_grad = operands
        key_part = row_keyval[:, :head_size]
        value_part = row_keyval[:, head_size:]
        scores = masked_scores(row_query, key_part, seg_query, seg_keys, scale)
        probs = jnp.exp(scores - row_logsum[..., None])
        probs_low = probs.astype(jnp.bfloat16)
        grad_value = jnp.einsum(
            "eck,ceh->kh", probs_low, row_grad, preferred_element_type=jnp.float32
        )
        grad_probs = jnp.einsum(
            "ceh,kh->eck", row_grad, value_part, preferred_element_type=jnp.float32
        )
        inner = jnp.sum(probs * grad_probs, axis=-1, keepdims=True)
        grad_scores = (probs * (grad_probs - inner)).astype(jnp.bfloat16)
        grad_query = (
            jnp.einsum("eck,kh->ceh", grad_scores, key_part, preferred_element_type=jnp.float32)
            * scale
        )
        grad_key = (
            jnp.einsum("eck,ceh->kh", grad_scores, row_query, preferred_element_type=jnp.float32)
            * scale
        )
        return (grad_query, jnp.concatenate([grad_key, grad_value], axis=1))

    grad_query_slots, grad_keyval_row = lax.map(
        back_row, (query_slots, keyval_row, query_seg, segments, logsum, grad_context)
    )
    grad_keyval = lax.psum_scatter(
        grad_keyval_row.astype(jnp.bfloat16), "seq", scatter_dimension=1, tiled=True
    )
    grad_query_low = (
        spread_slots(one_hot, grad_query_slots)
        .reshape(rows_dev, local_len, heads)
        .astype(jnp.bfloat16)
    )
    grad_query_bias = jnp.sum(grad_query_low.astype(jnp.float32), axis=(0, 1))
    grad_query_w = jnp.einsum(
        "rcd,rcf->df", normed_low, grad_query_low, preferred_element_type=jnp.float32
    )
    grad_keyval_w = jnp.einsum(
        "rcd,rcf->df", normed_low, grad_keyval, preferred_element_type=jnp.float32
    )
    logit_slots = gate_slots * (
        grad_gate_slots - jnp.sum(gate_slots * grad_gate_slots, axis=-1, keepdims=True)
    )
    grad_logits = jnp.sum(one_hot * logit_slots[..., None], axis=2).astype(jnp.bfloat16)
    grad_router = jnp.einsum(
        "rcd,rce->de", normed_low, grad_logits, preferred_element_type=jnp.float32
    )
    grad_normed = jnp.einsum(
        "rcf,df->rcd", grad_query_low, query_full, preferred_element_type=jnp.float32
    )
    grad_normed = grad_normed + jnp.einsum(
        "rcf,df->rcd", grad_keyval, keyval_full, preferred_element_type=jnp.float32
    )
    grad_normed = grad_normed + jnp.einsum(
        "rce,de->rcd", grad_logits, router_full, preferred_element_type=jnp.float32
    )
    unused_one, first_pull = jax.vjp(normalize, inputs, gain_first, shift_first)
    grad_input_part, grad_gain_first, grad_shift_first = first_pull(grad_normed)
    grad_input = (grad_middle + grad_input_part).astype(jnp.bfloat16)
    shards = tuple(
        (
            lax.psum_scatter(grad_gain_first, ("seq", "batch"), scatter_dimension=0, tiled=True),
            lax.psum_scatter(grad_shift_first, ("seq", "batch"), scatter_dimension=0, tiled=True),
            lax.psum_scatter(grad_router, ("seq", "batch"), scatter_dimension=0, tiled=True),
            lax.psum_scatter(grad_query_w, ("seq", "batch"), scatter_dimension=0, tiled=True),
            lax.psum_scatter(grad_query_bias, ("seq", "batch"), scatter_dimension=0, tiled=True),
            lax.psum_scatter(grad_keyval_w, ("seq", "batch"), scatter_dimension=0, tiled=True),
            lax.psum_scatter(grad_out_w, ("seq", "batch"), scatter_dimension=0, tiled=True),
            lax.psum_scatter(grad_out_bias, ("seq", "batch"), scatter_dimension=0, tiled=True),
            lax.psum_scatter(grad_gain_second, ("seq", "batch"), scatter_dimension=0, tiled=True),
            lax.psum_scatter(grad_shift_second, ("seq", "batch"), scatter_dimension=0, tiled=True),
            lax.psum_scatter(grad_up, ("seq", "batch"), scatter_dimension=0, tiled=True),
            lax.psum_scatter(grad_up_bias, ("seq", "batch"), scatter_dimension=0, tiled=True),
            lax.psum_scatter(grad_down, ("seq", "batch"), scatter_dimension=0, tiled=True),
            lax.psum_scatter(grad_down_bias, ("seq", "batch"), scatter_dimension=0, tiled=True),
        )
    )
    return (output.astype(jnp.bfloat16), grad_input) + shards


def solution(mesh):
    in_specs = (
        P("batch", "seq", None),
        P("batch", "seq", None),
        P("batch", "seq", None),
        P("batch", None),
        P(("seq", "batch")),
        P(("seq", "batch")),
        P(("seq", "batch"), None),
        P(("seq", "batch"), None),
        P(("seq", "batch")),
        P(("seq", "batch"), None),
        P(("seq", "batch"), None),
        P(("seq", "batch")),
        P(("seq", "batch")),
        P(("seq", "batch")),
        P(("seq", "batch"), None),
        P(("seq", "batch")),
        P(("seq", "batch"), None),
        P(("seq", "batch")),
    )
    out_specs = (
        P("batch", "seq", None),
        P("batch", "seq", None),
        P(("seq", "batch")),
        P(("seq", "batch")),
        P(("seq", "batch"), None),
        P(("seq", "batch"), None),
        P(("seq", "batch")),
        P(("seq", "batch"), None),
        P(("seq", "batch"), None),
        P(("seq", "batch")),
        P(("seq", "batch")),
        P(("seq", "batch")),
        P(("seq", "batch"), None),
        P(("seq", "batch")),
        P(("seq", "batch"), None),
        P(("seq", "batch")),
    )
    return jax.shard_map(body, mesh=mesh, in_specs=in_specs, out_specs=out_specs, check_vma=False)
```

profile of v0, /device:TPU:0, one launch (start us, length us, event | category | flops | bytes accessed | tf_op | source)
XLA Modules:
  0.0 1434.7 jit_solution(12338625134393793286)
XLA Ops:
  14.2 42.2 %all-reduce.17 = (bf16[512]{0:T(512)(128)(2,1)S(1)}, bf16[512]{0:T(512)(128)(2,1)S(1)}, bf16[512]{0:T(512)(128)(2,1)S(1)}, bf16[512]{0:T(512)(128)(2,1)}, bf16[5...) all-reduce(bf16[512]{0:T(512)(128)(2,1)S(1)} %dynamic-update-slice., ...), channel_id=1, replica_groups=mesh['seq'=4,'batch'=8] {'seq','batch'}, use_global_device_ids=true, to_apply=%add.1 | all-reduce | flops 5632 | bytes 22528
  60.9 41.0 %all_gather.48 = bf16[512,128]{1,0:T(8,128)(2,1)S(1)} all-gather(bf16[16,128]{1,0:T(8,128)(2,1)S(1)} %copy-done.37), channel_id=1, replica_groups=mesh['seq'=4,'batch'=8] {'seq','batch'}, dimensions={0}, use_global_device_ids=true | all-gather | bytes 135168 | tf_op jit(solution)/shard_map/all_gather | solution.py:54
  106.7 40.6 %all_gather.50 = bf16[512,512]{1,0:T(8,128)(2,1)S(1)} all-gather(bf16[16,512]{1,0:T(8,128)(2,1)S(1)} %copy-done.35), channel_id=1, replica_groups=mesh['seq'=4,'batch'=8] {'seq','batch'}, dimensions={0}, use_global_device_ids=true | all-gather | bytes 540672 | tf_op jit(solution)/shard_map/all_gather | solution.py:52
  150.6 3.9 copy.150
  154.5 5.1 copy.151
  160.5 53.7 %gather_fusion.1 = bf16[4096,64]{1,0:T(8,128)(2,1)S(1)} fusion(bf16[8,256,8,64]{3,2,1,0:T(8,128)(2,1)} %copy.151, s32[4096]{0:T(1024)S(1)} %reshape.233), kind=kCustom, calls=%fused_computation.1 | custom fusion | bytes 1097728 | tf_op jit(solution)/shard_map/jit(take_along_axis)/gather | solution.py:96
  216.0 37.8 %all-gather = bf16[32,16,8]{1,2,0:T(8,128)(2,1)S(1)} all-gather(bf16[1,16,8]{1,2,0:T(8,128)(2,1)S(1)} %bitcast.235), channel_id=1, replica_groups=mesh['seq'=4,'batch'=8] {'seq','batch'}, dimensions={0}, use_global_device_ids=true | all-gather | bytes 8448 | tf_op jit(solution)/shard_map/all_gather | solution.py:51
  255.1 31.9 %gather_fusion = f32[4096]{0:T(1024)S(1)} fusion(f32[8,256,8]{1,2,0:T(8,128)S(1)} %fusion.61, s32[4096]{0:T(1024)S(1)} %reshape.233), kind=kCustom, calls=%fused_computation | custom fusion | bytes 81920 | tf_op jit(solution)/shard_map/jit(take_along_axis)/gather | solution.py:90
  288.5 41.3 %all_gather.52 = bf16[512,512]{1,0:T(8,128)(2,1)} all-gather(bf16[16,512]{1,0:T(8,128)(2,1)S(1)} %copy-done.36), channel_id=1, replica_groups=mesh['seq'=4,'batch'=8] {'seq','batch'}, dimensions={0}, use_global_device_ids=true | all-gather | bytes 540672 | tf_op jit(solution)/shard_map/all_gather | solution.py:55
  330.7 3.9 copy.153
  334.7 31.4 %while.24 = (s32[]{:T(128)}, f32[8,256,2,64]{1,3,2,0:T(8,128)S(1)}, f32[8,2,256]{2,1,0:T(2,128)}, bf16[8,1024,128]{1,2,0:T(8,128)(2,1)}, s32[8,256]{1,0:T(8,128)...) while((s32[]{:T(128)}, f32[8,256,2,64]{1,3,2,0:T(8,128)S(1)}, ...), condition=%wide.region_8.9_spmd, body=%wide.region_5.8_spmd.sunk | while | flops 138673664 | bytes 7831653 | solution.py:116
  372.1 14.6 %multiply_convert_fusion = (bf16[8,256,2048]{2,1,0:T(8,128)(2,1)}, f32[8,256,2048]{2,1,0:T(8,128)}) fusion(f32[2048]{0:T(1024)S(1)} %convert_element_type.120, bf16[512,2048]{1,0:T(8,128)(2,1)} %all-gather.7.cloned.1.call-done, f32[8,256,512]{2,1,0:T(8,128)} %copy-done.4, f32[512]{0:T(512)S(1)} %convert_element_type.118, f32[512]{0:T(512)S(1)} %convert_element_type.117, ...), kind=kOutput, calls=%fused_computation.69 | convolution fusion | flops 4342153216 | bytes 31485952 | tf_op jit(solution)/shard_map/rcd,df->rcf/dot_general | solution.py:131
  386.7 18.9 %convert_reduce_fusion = (f32[2048]{0:T(1024)S(1)}, bf16[8,256,2048]{2,1,0:T(8,128)(2,1)S(1)}) fusion(f32[8,256,2048]{2,1,0:T(8,128)} %get-tuple-element.258, f32[2048]{0:T(1024)S(1)} %convert_element_type.120, bf16[8,256,512]{2,1,0:T(8,128)(2,1)} %param.23, bf16[2048,512]{1,0:T(8,128)(2,1)} %all-gather.9.cloned.1.call-done), kind=kOutput, calls=%fused_computation.68 | convolution fusion | flops 4391434240 | bytes 29376512 | tf_op jit(solution)/shard_map/rcd,fd->rcf/dot_general | solution.py:143
  405.6 9.2 multiply_reduce_fusion.2
  423.3 6.9 copy.156
  430.2 65.4 %gather_fusion.2 = f32[4096,64]{1,0:T(8,128)} fusion(f32[8,256,8,64]{3,2,1,0:T(8,128)} %copy.156, s32[4096]{0:T(1024)S(1)} %reshape.233), kind=kCustom, calls=%fused_computation.2 | custom fusion | bytes 2146304 | tf_op jit(solution)/shard_map/jit(take_along_axis)/gather | solution.py:164
  495.6 3.9 copy.157
  501.9 70.6 %while.25 = (s32[]{:T(128)}, f32[8,256,2,64]{1,3,2,0:T(8,128)S(1)}, bf16[8,1024,128]{1,2,0:T(8,128)(2,1)}, bf16[8,1024,128]{1,2,0:T(8,128)(2,1)}, s32[8,256]{1,0...) while((s32[]{:T(128)}, f32[8,256,2,64]{1,3,2,0:T(8,128)S(1)}, ...), condition=%wide.region_16.17_spmd, body=%wide.region_14.16_spmd.sunk | while | flops 341212672 | bytes 18378360 | solution.py:193
  577.3 4.5 convolution_bitcast_fusion.6
  581.9 4.5 convolution_bitcast_fusion.5
  586.5 27.2 %reduce-scatter.10.cloned.1.call-done = bf16[8,256,128]{1,2,0:T(8,128)(2,1)} async-done(((bf16[8,1024,128]{1,2,0:T(8,128)(2,1)}), bf16[8,256,128]{1,2,0:T(8,128)(2,1)}) %reduce-scatter.10.cloned.1.call-update) | async-done | bytes 524304 | tf_op jit(solution)/shard_map/reduce_scatter | solution.py:196
  617.0 11.4 convolution_bitcast_fusion.4
  628.7 10.5 convolution_bitcast_fusion.3
  641.9 5.0 fusion.67
  646.9 9.3 add_convert_fusion.1
  656.2 92.4 %reduce-scatter.22.cloned.1.call-done = f32[16,8]{1,0:T(8,128)} async-done(((f32[512,8]{1,0:T(8,128)}), f32[16,8]{1,0:T(8,128)}) %reduce-scatter.22.cloned.1.call-update) | async-done | bytes 528
  759.9 37.2 %all-reduce.16 = (f32[512]{0:T(512)S(1)}, f32[512]{0:T(512)S(1)}, f32[512]{0:T(512)S(1)}, f32[512]{0:T(512)S(1)}, f32[512]{0:T(512)S(1)}, /*index=5*/f32[512]{0:T(512)S(1)}, f32[2048]{0:T(1024)S(1)}, f32[512]{0:T(512)S(1)}) all-reduce(f32[512]{0:T(512)S(1)} %get-tuple-element.188, ...), channel_id=3, replica_groups=mesh['seq'=4,'batch'=8] {'seq','batch'}, use_global_device_ids=true, to_apply=%region_25.26.clone | all-reduce | flops 5632 | bytes 45056
  801.8 80.2 %reduce-scatter.12.cloned.1.call-done = f32[16,512]{1,0:T(8,128)} async-done(((f32[512,512]{1,0:T(8,128)}), f32[16,512]{1,0:T(8,128)}) %reduce-scatter.12.cloned.1.call-update) | async-done | bytes 32784 | tf_op jit(solution)/shard_map/reduce_scatter | solution.py:235
  882.1 133.8 %reduce-scatter.16.cloned.1.call-done = f32[16,512]{1,0:T(8,128)} async-done(((f32[512,512]{1,0:T(8,128)}), f32[16,512]{1,0:T(8,128)}) %reduce-scatter.16.cloned.1.call-update) | async-done | bytes 32784 | tf_op jit(solution)/shard_map/reduce_scatter | solution.py:238
  1015.9 132.2 %reduce-scatter.14.cloned.1.call-done = f32[16,128]{1,0:T(8,128)} async-done(((f32[512,128]{1,0:T(8,128)}), f32[16,128]{1,0:T(8,128)}) %reduce-scatter.14.cloned.1.call-update) | async-done | bytes 8208 | tf_op jit(solution)/shard_map/reduce_scatter | solution.py:237
  1148.0 139.8 %reduce-scatter.18.cloned.1.call-done = f32[16,2048]{1,0:T(8,128)} async-done(((f32[512,2048]{1,0:T(8,128)}), f32[16,2048]{1,0:T(8,128)}) %reduce-scatter.18.cloned.1.call-update) | async-done | bytes 131088 | tf_op jit(solution)/shard_map/reduce_scatter | solution.py:242
  1287.9 139.6 %reduce-scatter.20.cloned.1.call-done = f32[64,512]{1,0:T(8,128)} async-done(((f32[2048,512]{1,0:T(8,128)}), f32[64,512]{1,0:T(8,128)}) %reduce-scatter.20.cloned.1.call-update) | async-done | bytes 131088 | tf_op jit(solution)/shard_map/reduce_scatter | solution.py:244
  (363 shorter events, 170.4 us)
Async XLA Ops:
  7.2 95.3 %copy-start = (bf16[8,256,512]{2,1,0:T(8,128)(2,1)S(1)}, bf16[8,256,512]{2,1,0:T(8,128)(2,1)}, u32[]{:S(2)}) copy-start(bf16[8,256,512]{2,1,0:T(8,128)(2,1)} %param.22) | copy-start | bytes 6291460
  7.2 53.6 %copy-start.37 = (bf16[16,128]{1,0:T(8,128)(2,1)S(1)}, bf16[16,128]{1,0:T(8,128)(2,1)}, u32[]{:S(2)}) copy-start(bf16[16,128]{1,0:T(8,128)(2,1)} %param.31) | copy-start | bytes 12292
  7.2 323.5 %all-gather.5.cloned.1.call-start = ((), (), s32[]{:S(2)}) async-start(), calls=%async_computation.7 | async-start | bytes 2621440 | tf_op jit(solution)/shard_map/all_gather | solution.py:100
  56.4 197.6 %copy-start.33 = (f32[512]{0:T(512)}, f32[512]{0:T(512)S(1)}, u32[]{:S(2)}) copy-start(f32[512]{0:T(512)S(1)} %convert_element_type.108) | copy-start | bytes 6148
  56.4 197.6 %copy-start.40 = (f32[512]{0:T(512)}, f32[512]{0:T(512)S(1)}, u32[]{:S(2)}) copy-start(f32[512]{0:T(512)S(1)} %convert_element_type.109) | copy-start | bytes 6148
  58.4 195.6 %copy-start.24 = (f32[8,256]{1,0:T(8,128)}, f32[8,256]{1,0:T(8,128)S(1)}, u32[]{:S(2)}) copy-start(f32[8,256]{1,0:T(8,128)S(1)} %broadcast_multiply_fusion.2) | copy-start | bytes 24580
  58.4 47.6 %copy-start.22 = (s32[8,256,2]{1,2,0:T(2,128)S(1)}, s32[8,256,2]{1,2,0:T(2,128)}, u32[]{:S(2)}) copy-start(s32[8,256,2]{1,2,0:T(2,128)} %param.24) | copy-start | bytes 49156
  60.8 89.8 %copy-start.28 = (f32[8,256]{1,0:T(8,128)}, f32[8,256]{1,0:T(8,128)S(1)}, u32[]{:S(2)}) copy-start(f32[8,256]{1,0:T(8,128)S(1)} %fusion.47) | copy-start | bytes 24580
  60.8 45.9 %copy-start.35 = (bf16[16,512]{1,0:T(8,128)(2,1)S(1)}, bf16[16,512]{1,0:T(8,128)(2,1)}, u32[]{:S(2)}) copy-start(bf16[16,512]{1,0:T(8,128)(2,1)} %param.29) | copy-start | bytes 49156
  60.8 193.1 %copy-start.26 = (f32[8,256]{1,0:T(8,128)}, f32[8,256]{1,0:T(8,128)S(1)}, u32[]{:S(2)}) copy-start(f32[8,256]{1,0:T(8,128)S(1)} %fusion.77) | copy-start | bytes 24580
  104.4 267.7 %all-gather.7.cloned.1.call-start = ((), (), s32[]{:S(2)}) async-start(), calls=%async_computation.8 | async-start | bytes 2162688 | tf_op jit(solution)/shard_map/all_gather | solution.py:59
  105.2 281.5 %all-gather.9.cloned.1.call-start = ((), (), s32[]{:S(2)}) async-start(), calls=%async_computation.9 | async-start | bytes 2162688 | tf_op jit(solution)/shard_map/all_gather | solution.py:61
  105.9 507.8 %reduce-scatter.10.cloned.1.call-start = ((), (), s32[]{:S(2)}) async-start(), calls=%async_computation.10 | async-start | bytes 2621440 | tf_op jit(solution)/shard_map/reduce_scatter | solution.py:196
  160.5 55.5 %copy-start.39 = (bf16[16,8]{0,1:T(8,128)(2,1)S(1)}, bf16[16,8]{0,1:T(8,128)(2,1)}, u32[]{:S(2)}) copy-start(bf16[16,8]{0,1:T(8,128)(2,1)} %param.28) | copy-start | bytes 772
  254.0 33.1 %copy-start.31 = (bf16[512,8,1]{0,1,2:T(8,128)(2,1)}, bf16[512,8,1]{0,1,2:T(8,128)(2,1)S(1)}, u32[]{:S(2)}) copy-start(bf16[512,8,1]{0,1,2:T(8,128)(2,1)S(1)} %reshape.280) | copy-start | bytes 24580
  255.0 33.4 %copy-start.23 = (s32[8,256,2]{1,2,0:T(2,128)S(1)}, s32[8,256,2]{1,2,0:T(2,128)}, u32[]{:S(2)}) copy-start(s32[8,256,2]{1,2,0:T(2,128)} %param.24) | copy-start | bytes 49156
  255.0 33.4 %copy-start.45 = (bf16[512]{0:T(512)(128)(2,1)S(1)}, bf16[512]{0:T(512)(128)(2,1)}, u32[]{:S(2)}) copy-start(bf16[512]{0:T(512)(128)(2,1)} %get-tuple-element.236) | copy-start | bytes 3076
  255.0 33.4 %copy-start.36 = (bf16[16,512]{1,0:T(8,128)(2,1)S(1)}, bf16[16,512]{1,0:T(8,128)(2,1)}, u32[]{:S(2)}) copy-start(bf16[16,512]{1,0:T(8,128)(2,1)} %param.32) | copy-start | bytes 49156
  255.1 74.7 %copy-start.44 = (bf16[512]{0:T(512)(128)(2,1)S(1)}, bf16[512]{0:T(512)(128)(2,1)}, u32[]{:S(2)}) copy-start(bf16[512]{0:T(512)(128)(2,1)} %get-tuple-element.239) | copy-start | bytes 3076
  255.1 74.7 %copy-start.38 = (bf16[2048]{0:T(1024)(128)(2,1)S(1)}, bf16[2048]{0:T(1024)(128)(2,1)}, u32[]{:S(2)}) copy-start(bf16[2048]{0:T(1024)(128)(2,1)} %get-tuple-element.240) | copy-start | bytes 12292
  255.1 74.7 %copy-start.43 = (bf16[512]{0:T(512)(128)(2,1)S(1)}, bf16[512]{0:T(512)(128)(2,1)}, u32[]{:S(2)}) copy-start(bf16[512]{0:T(512)(128)(2,1)} %get-tuple-element.238) | copy-start | bytes 3076
  255.1 74.7 %copy-start.12 = (bf16[8,256,2,64]{1,3,2,0:T(8,128)(2,1)S(1)}, bf16[8,256,2,64]{1,3,2,0:T(8,128)(2,1)}, u32[]{:S(2)}) copy-start(bf16[8,256,2,64]{1,3,2,0:T(8,128)(2,1)} %copy.152) | copy-start | bytes 1572868
  255.1 75.6 %copy-start.30 = (s32[8,1024]{1,0:T(8,128)S(1)}, s32[8,1024]{1,0:T(8,128)}, u32[]{:S(2)}) copy-start(s32[8,1024]{1,0:T(8,128)} %param.25) | copy-start | bytes 98308
  572.6 176.1 %reduce-scatter.22.cloned.1.call-start = ((), (), s32[]{:S(2)}) async-start(), calls=%async_computation.16 | async-start | bytes 270336
  577.2 304.8 %reduce-scatter.12.cloned.1.call-start = ((), (), s32[]{:S(2)}) async-start(), calls=%async_computation.11 | async-start | bytes 1081344 | tf_op jit(solution)/shard_map/reduce_scatter | solution.py:235
  581.8 434.0 %reduce-scatter.16.cloned.1.call-start = ((), (), s32[]{:S(2)}) async-start(), calls=%async_computation.13 | async-start | bytes 1081344 | tf_op jit(solution)/shard_map/reduce_scatter | solution.py:238
  586.4 561.6 %reduce-scatter.14.cloned.1.call-start = ((), (), s32[]{:S(2)}) async-start(), calls=%async_computation.12 | async-start | bytes 270336 | tf_op jit(solution)/shard_map/reduce_scatter | solution.py:237
  616.9 670.9 %reduce-scatter.18.cloned.1.call-start = ((), (), s32[]{:S(2)}) async-start(), calls=%async_computation.14 | async-start | bytes 4325376 | tf_op jit(solution)/shard_map/reduce_scatter | solution.py:242
  628.4 799.1 %reduce-scatter.20.cloned.1.call-start = ((), (), s32[]{:S(2)}) async-start(), calls=%async_computation.15 | async-start | bytes 4325376 | tf_op jit(solution)/shard_map/reduce_scatter | solution.py:244
  646.9 103.1 %copy-start.19 = (bf16[8,256,128]{1,2,0:T(8,128)(2,1)S(1)}, bf16[8,256,128]{1,2,0:T(8,128)(2,1)}, u32[]{:S(2)}) copy-start(bf16[8,256,128]{1,2,0:T(8,128)(2,1)} %reduce-scatter.10.cloned.1.call-done) | copy-start | bytes 1572868
  646.9 103.1 %copy-start.21 = (bf16[512,128]{1,0:T(8,128)(2,1)S(1)}, bf16[512,128]{1,0:T(8,128)(2,1)}, u32[]{:S(2)}) copy-start(bf16[512,128]{1,0:T(8,128)(2,1)} %copy-done.20) | copy-start | bytes 393220
  656.2 94.5 %copy-start.32 = (bf16[512,8,1]{0,1,2:T(8,128)(2,1)S(1)}, bf16[512,8,1]{0,1,2:T(8,128)(2,1)}, u32[]{:S(2)}) copy-start(bf16[512,8,1]{0,1,2:T(8,128)(2,1)} %copy-done.31) | copy-start | bytes 24580
  (25 other events, 109.4 us)
Sparse Core Ops, SparseCore 0:
  104.5 43.1 all-gather.4
  150.5 56.4 all-gather.6
  209.9 55.2 all-gather.8
  572.7 40.9 reduce-scatter.9
  615.9 132.7 reduce-scatter.21
  751.3 130.7 reduce-scatter.11
  885.0 130.8 reduce-scatter.15
  1018.7 129.3 reduce-scatter.13
  1151.0 136.8 reduce-scatter.17
  1290.7 136.8 reduce-scatter.19
where the time goes:
time: 1450 us; the launch traced here: 1430 us
  waiting for transfers between devices  747 us (52%)
  blocking collectives  240 us (17%)
  local copies, waits for them, and re-layouts  223 us (15%)
  matrix products  167 us (12%)
  other arithmetic  41.3 us (3%)
  between operations  15.3 us (1%)
    reduce_scatter x1, waiting for transfers between devices, body(): lax.psum_scatter(grad_up, ('seq', 'batch'), scatter_dimension=0, tiled=True)  140 us
    reduce_scatter x1, waiting for transfers between devices, body(): lax.psum_scatter(grad_down, ('seq', 'batch'), scatter_dimension=0, tiled=...  140 us
    reduce_scatter x1, waiting for transfers between devices, body(): lax.psum_scatter(grad_out_w, ('seq', 'batch'), scatter_dimension=0, tiled...  134 us
    reduce_scatter x1, waiting for transfers between devices, body(): lax.psum_scatter(grad_keyval_w, ('seq', 'batch'), scatter_dimension=0, ti...  132 us
    unnamed x11, waiting for transfers between devices  93.9 us
    reduce_scatter x1, waiting for transfers between devices, body(): lax.psum_scatter(grad_query_w, ('seq', 'batch'), scatter_dimension=0, til...  80.2 us
    unnamed x2, blocking collectives  79.4 us
    gather x2, local copies, waits for them, and re-layouts, body(): jnp.take_along_axis(grad_mixed, expert_index[..., None], axis=2)  69.3 us
  transfers between devices with their start and end apart: 10, of which 7 were waited for; matrix products, arithmetic and copies ran while one was open for 16% of the time, Pallas kernels for 0%

commit v1 on v0

v1 whole, which is shorter than its diff:
```python
import functools

import jax
import jax.numpy as jnp
from jax import lax
from jax.experimental import pallas as pl
from jax.experimental.pallas import tpu as pltpu
from jax.sharding import PartitionSpec as P

EPS = 1e-05
NEG = -1e30
C0 = 0.7978845608028654
C1 = 0.7978845608028654 * 0.044715
PARTS = (8,)
R = 2
VMEM_LIMIT = 60 * 1024 * 1024
F32 = jnp.float32
BF16 = jnp.bfloat16


def mm(a, b):
    return lax.dot_general(a, b, (((1,), (0,)), ((), ())), preferred_element_type=F32)


def mmt(a, b):
    return lax.dot_general(a, b, (((1,), (1,)), ((), ())), preferred_element_type=F32)


def fold8(v):
    return jnp.sum(v.reshape(v.shape[0] // 8, 8, v.shape[1]), axis=0)


def norm_parts(x):
    mean = jnp.mean(x, axis=-1, keepdims=True)
    xc = x - mean
    rstd = lax.rsqrt(jnp.mean(xc * xc, axis=-1, keepdims=True) + EPS)
    return xc * rstd, rstd


def norm_back(d, xhat, rstd):
    return rstd * (
        d
        - jnp.mean(d, axis=-1, keepdims=True)
        - xhat * jnp.mean(d * xhat, axis=-1, keepdims=True)
    )


def rel(bits, v):
    j = 0
    for src, dst in bits:
        j = j | (((v >> src) & 1) << dst)
    return j


def spread_matrix():
    m = lax.broadcasted_iota(jnp.int32, (128, 512), 0)
    lane = lax.broadcasted_iota(jnp.int32, (128, 512), 1)
    return jnp.where(m == (lane >> 6) * 16 + (lane & 15), 1.0, 0.0).astype(BF16)


def spread_rows():
    row = lax.broadcasted_iota(jnp.int32, (16, 512), 0)
    lane = lax.broadcasted_iota(jnp.int32, (16, 512), 1)
    return ((lane >> 4) & 3) + 8 == row


def kernel_a(bits, nblk, parts, sc, pack, tok, can, vec, bup, *kvs):
    me = sc[0]
    for b in range(nblk):
        can[b * 16 : (b + 1) * 16, :] = pack[rel(bits, me ^ b)]
    turned = jnp.transpose(can[:, 640:768].astype(F32))
    rows = turned[8:24]
    vec[...] = rows
    ex = spread_matrix()
    pick = spread_rows()
    width = can.shape[0]
    for b in range(4):
        wide = mm(rows[:, b * 128 : (b + 1) * 128].astype(BF16), ex)
        line = jnp.sum(jnp.where(pick, wide, 0.0), axis=0, keepdims=True)
        bup[:, b * width : (b + 1) * width] = jnp.broadcast_to(line, (8, width))
    gain = vec[0:1, :]
    shift = vec[1:2, :]
    row = 0
    for kv, count in zip(kvs, parts):
        for r in range(count):
            xhat, unused = norm_parts(tok[row].astype(F32))
            normed = (xhat * gain + shift).astype(BF16)
            kv[r] = mm(normed, can[:, 512:640]).astype(BF16)
            row += 1


def kernel_b(cfg, *refs):
    first, last, steps, bits_u, bits_d, gbits_u, gbits_d, nblk, nseq = cfg
    refs = list(refs)

    def take(n):
        got = refs[:n]
        del refs[:n]
        return got

    sc, tok, cot, idx, seg = take(5)
    kvs = take(nseq)
    can, vec, bup = take(3)
    u_own, u_got, d_own, d_got = take(4)
    acc_in = []
    if not first:
        acc_in = take(6)
        take(2)
    out_ref, part_ref = take(2)
    dkvs = take(nseq)
    (vacc,) = take(1)
    if last:
        gu_ref, gd_ref = take(2)
        acc_up, acc_dn, acc_wo, acc_wq, acc_r = take(5)
    else:
        acc_up, acc_dn, acc_wo, acc_wq, acc_r = take(5)
    (
        wup,
        wdn,
        wo,
        xn,
        q_s,
        qp,
        dp,
        idx_b,
        gate_b,
        cd,
        inner,
        prob,
        score,
        wide1,
        wide2,
        mid,
        xh2,
        rs2,
        n2,
        mix,
        hid,
        gac,
        act,
        ghd,
        low1,
        gl,
        wsem,
        asem,
    ) = refs

    me = sc[0]
    place = sc[1]
    step = pl.program_id(0)
    tile = tok.shape[0]
    local = tile // R
    ch = 64
    nch = tile // ch
    lane128 = lax.broadcasted_iota(jnp.int32, (ch, 128), 1)
    upper = lane128 >= 64
    half = lane128 >> 6
    accs = (acc_up, acc_dn, acc_wo, acc_wq, acc_r, vacc)

    @pl.when(step == 0)
    def _():
        for piece, base in ((u_own, 0), (u_got, u_own.shape[0])):
            for c in range(piece.shape[0]):
                blk = me ^ sum(((base + c) >> dst & 1) << src for src, dst in bits_u)
                pltpu.make_async_copy(
                    piece.at[c], wup.at[pl.ds(pl.multiple_of(blk * 16, 16), 16), :], wsem.at[0]
                ).start()
        for piece, base in ((d_own, 0), (d_got, d_own.shape[0])):
            for c in range(piece.shape[0]):
                blk = me ^ sum(((base + c) >> dst & 1) << src for src, dst in bits_d)
                pltpu.make_async_copy(
                    piece.at[c, pl.ds(0, 64), :],
                    wdn.at[pl.ds(pl.multiple_of(blk * 64, 64), 64), :],
                    wsem.at[1],
                ).start()
                pltpu.make_async_copy(
                    piece.at[c, pl.ds(64, 16), :],
                    wo.at[pl.ds(pl.multiple_of(blk * 16, 16), 16), :],
                    wsem.at[2],
                ).start()
        if first:
            for a in accs:
                a[...] = jnp.zeros_like(a)
        else:
            for n, a in enumerate(accs):
                pltpu.make_async_copy(acc_in[n], a, asem.at[n]).start()

    gain1 = vec[0:1, :]
    shift1 = vec[1:2, :]
    bias_q = vec[2:3, :]
    bias_o = vec[3:4, :]
    gain2 = vec[4:5, :]
    shift2 = vec[5:6, :]
    bias_d = vec[6:7, :]

    def norm_chunk(c, carry):
        sl = pl.ds(pl.multiple_of(c * ch, ch), ch)
        xhat, unused = norm_parts(tok[sl, :].astype(F32))
        xn[sl, :] = (xhat * gain1 + shift1).astype(BF16)
        return carry

    lax.fori_loop(0, nch, norm_chunk, 0)
    q_s[...] = mm(xn[...], can[:, 0:512])
    low1[...] = mm(xn[...], can[:, 640:768])
    for r in range(R):
        for s in range(2):
            line = idx[r, s : s + 1, :].astype(F32)
            idx_b[s, r * local : (r + 1) * local, :] = jnp.transpose(
                jnp.broadcast_to(line, (128, local))
            ).astype(jnp.int32)

    def gate_chunk(c, carry):
        sl = pl.ds(pl.multiple_of(c * ch, ch), ch)
        logits = low1[sl, :]
        i0 = idx_b[0, sl, :]
        i1 = idx_b[1, sl, :]
        top = jnp.max(jnp.where(lane128 < 8, logits, -jnp.inf), axis=-1, keepdims=True)
        e0 = jnp.exp(jnp.sum(jnp.where(lane128 == i0, logits, 0.0), axis=-1, keepdims=True) - top)
        e1 = jnp.exp(jnp.sum(jnp.where(lane128 == i1, logits, 0.0), axis=-1, keepdims=True) - top)
        total = e0 + e1
        gate_b[0, sl, :] = jnp.broadcast_to(e0 / total, (ch, 128))
        gate_b[1, sl, :] = jnp.broadcast_to(e1 / total, (ch, 128))
        r = c // (local // ch)
        at = pl.multiple_of((c % (local // ch)) * ch, ch)
        f0 = jnp.zeros((ch, 128), F32)
        f1 = jnp.zeros((ch, 128), F32)
        for b in range(4):
            q = (q_s[sl, b * 128 : (b + 1) * 128] + bias_q[:, b * 128 : (b + 1) * 128]) * 0.125
            f0 = f0 + jnp.where(half + 2 * b == i0, q, 0.0)
            f1 = f1 + jnp.where(half + 2 * b == i1, q, 0.0)
        f0 = f0 + pltpu.roll(f0, 64, 1)
        f1 = f1 + pltpu.roll(f1, 64, 1)
        qp[r, pl.ds(at, ch), :] = jnp.where(upper, 0.0, f0).astype(BF16)
        qp[r, pl.ds(local + at, ch), :] = jnp.where(upper, 0.0, f1).astype(BF16)
        return carry

    lax.fori_loop(0, nch, gate_chunk, 0)

    for r in range(R):
        for m in range(nseq):
            score[:, m * local : (m + 1) * local] = mmt(qp[r], kvs[m][r])
        seg_k = jnp.concatenate(
            [
                seg[r, :, pl.ds(pl.multiple_of((place ^ m) * local, 128), local)]
                for m in range(nseq)
            ],
            axis=1,
        )
        own = seg[r, :, pl.ds(pl.multiple_of(place * local, 128), local)].astype(F32)
        inner[0:local, :] = jnp.transpose(jnp.broadcast_to(own, (128, local)))

        def soft_chunk(c, carry, r=r, seg_k=seg_k):
            at = pl.multiple_of(c * 16, 16)
            match = inner[pl.ds(at, 16), 0:1].astype(jnp.int32) == seg_k
            for s in range(2):
                sl = pl.ds(pl.multiple_of(s * local + at, 16), 16)
                sc_ = jnp.where(match, score[sl, :], NEG)
                num = jnp.exp(sc_ - jnp.max(sc_, axis=-1, keepdims=True))
                total = jnp.sum(num, axis=-1, keepdims=True)
                prob[r, sl, :] = (num / total).astype(BF16)
            return carry

        lax.fori_loop(0, local // 16, soft_chunk, 0, unroll=2)
        ctx = jnp.zeros((2 * local, 128), F32)
        for m in range(nseq):
            ctx = ctx + mm(prob[r, :, m * local : (m + 1) * local], kvs[m][r])
        up2 = lax.broadcasted_iota(jnp.int32, ctx.shape, 1) >= 64
        ctx = jnp.where(up2, ctx, 0.0)
        ctx = ctx + pltpu.roll(ctx, 64, 1)
        cd[0, r * local : (r + 1) * local, :] = ctx[:local]
        cd[1, r * local : (r + 1) * local, :] = ctx[local:]

    @pl.when(step == 0)
    def _():
        for n, w in enumerate((wup, wdn, wo)):
            pltpu.make_async_copy(w, w, wsem.at[n]).wait()
        if not first:
            for n, a in enumerate(accs):
                pltpu.make_async_copy(acc_in[n], a, asem.at[n]).wait()

    def mix_chunk(c, carry):
        sl = pl.ds(pl.multiple_of(c * ch, ch), ch)
        i0 = idx_b[0, sl, :]
        i1 = idx_b[1, sl, :]
        m0 = gate_b[0, sl, :] * cd[0, sl, :]
        m1 = gate_b[1, sl, :] * cd[1, sl, :]
        for b in range(4):
            mix[sl, b * 128 : (b + 1) * 128] = jnp.where(
                half + 2 * b == i0, m0, jnp.where(half + 2 * b == i1, m1, 0.0)
            ).astype(BF16)
        return carry

    lax.fori_loop(0, nch, mix_chunk, 0)
    wide1[...] = mm(mix[...], wo[...])

    def mid_chunk(c, carry):
        sl = pl.ds(pl.multiple_of(c * ch, ch), ch)
        middle = tok[sl, :].astype(F32) + (wide1[sl, :] + bias_o)
        mid[sl, :] = middle
        xhat, rstd = norm_parts(middle)
        xh2[sl, :] = xhat
        rs2[sl, :] = jnp.broadcast_to(rstd, (ch, 128))
        n2[sl, :] = (xhat * gain2 + shift2).astype(BF16)
        return carry

    lax.fori_loop(0, nch, mid_chunk, 0)

    n2_t = jnp.transpose(n2[...])
    cot_t = jnp.transpose(cot[...])
    width = hid.shape[2]
    for j in range(wup.shape[1] // width):
        k = j % 2
        js = slice(j * width, (j + 1) * width)
        hid[k] = mm(n2[...], wup[:, js])
        gac[k] = mmt(cot[...], wdn[js, :])
        bias = bup[0:1, js]
        total = jnp.zeros((8, width), F32)
        for c in range(tile // 32):
            sl = slice(c * 32, (c + 1) * 32)
            h = hid[k, sl, :] + bias
            h2 = h * h
            t = jnp.tanh(h * (C0 + C1 * h2))
            hh = 0.5 * h
            act[k, sl, :] = (hh + hh * t).astype(BF16)
            slope = (0.5 + 0.5 * t) + hh * (1.0 - t * t) * (C0 + (3.0 * C1) * h2)
            g = (gac[k, sl, :] * slope).astype(BF16)
            ghd[k, sl, :] = g
            total = total + fold8(g.astype(F32))
        vacc[(7 + j) * 8 : (8 + j) * 8, :] += total
        o = mm(act[k], wdn[js, :])
        g2 = mmt(ghd[k], wup[:, js])
        if j == 0:
            wide1[...] = o
            wide2[...] = g2
        else:
            wide1[...] += o
            wide2[...] += g2
        acc_up[:, js] += mm(n2_t, ghd[k])
        acc_dn[:, js] += mm(cot_t, act[k])

    def out_chunk(c, carry):
        sl = pl.ds(pl.multiple_of(c * ch, ch), ch)
        out_ref[sl, :] = (mid[sl, :] + (wide1[sl, :] + bias_d)).astype(BF16)
        ct = cot[sl, :].astype(F32)
        g = wide2[sl, :]
        xhat = xh2[sl, :]
        gm = ct + norm_back(g * gain2, xhat, rs2[sl, 0:1])
        mid[sl, :] = gm
        low = gm.astype(BF16)
        n2[sl, :] = low
        vacc[24:32, :] += fold8(low.astype(F32))
        vacc[32:40, :] += fold8(g * xhat)
        vacc[40:48, :] += fold8(g)
        vacc[48:56, :] += fold8(ct)
        return carry

    lax.fori_loop(0, nch, out_chunk, 0)

    acc_wo[...] += mm(jnp.transpose(mix[...]), n2[...])
    wide1[...] = mmt(n2[...], wo[...])

    def gate_back_chunk(c, carry):
        sl = pl.ds(pl.multiple_of(c * ch, ch), ch)
        i0 = idx_b[0, sl, :]
        i1 = idx_b[1, sl, :]
        f0 = jnp.zeros((ch, 128), F32)
        f1 = jnp.zeros((ch, 128), F32)
        for b in range(4):
            g = wide1[sl, b * 128 : (b + 1) * 128]
            f0 = f0 + jnp.where(half + 2 * b == i0, g, 0.0)
            f1 = f1 + jnp.where(half + 2 * b == i1, g, 0.0)
        f0 = jnp.where(upper, f0 + pltpu.roll(f0, 64, 1), 0.0)
        f1 = jnp.where(upper, f1 + pltpu.roll(f1, 64, 1), 0.0)
        c0 = cd[0, sl, :]
        c1 = cd[1, sl, :]
        g0 = gate_b[0, sl, :]
        g1 = gate_b[1, sl, :]
        gg0 = jnp.sum(f0 * c0, axis=-1, keepdims=True)
        gg1 = jnp.sum(f1 * c1, axis=-1, keepdims=True)
        both = g0 * gg0 + g1 * gg1
        gl[sl, :] = jnp.where(
            lane128 == i0, g0 * (gg0 - both), jnp.where(lane128 == i1, g1 * (gg1 - both), 0.0)
        ).astype(BF16)
        d0 = (g0 * f0).astype(BF16)
        d1 = (g1 * f1).astype(BF16)
        r = c // (local // ch)
        at = pl.multiple_of((c % (local // ch)) * ch, ch)
        s0 = pl.ds(r * 2 * local + at, ch)
        s1 = pl.ds(r * 2 * local + local + at, ch)
        dp[r, pl.ds(at, ch), :] = d0
        dp[r, pl.ds(local + at, ch), :] = d1
        inner[s0, :] = jnp.broadcast_to(
            jnp.sum(d0.astype(F32) * c0, axis=-1, keepdims=True), (ch, 128)
        )
        inner[s1, :] = jnp.broadcast_to(
            jnp.sum(d1.astype(F32) * c1, axis=-1, keepdims=True), (ch, 128)
        )
        return carry

    lax.fori_loop(0, nch, gate_back_chunk, 0)

    for r in range(R):
        for m in range(nseq):
            score[:, m * local : (m + 1) * local] = mmt(dp[r], kvs[m][r])
        dsc = act

        def score_chunk(c, carry, r=r):
            at = pl.multiple_of(c * 16, 16)
            sl = pl.ds(at, 16)
            inn = inner[pl.ds(pl.multiple_of(r * 2 * local + at, 16), 16), 0:1]
            for k in range(2):
                ks = slice(k * width, (k + 1) * width)
                dsc[k, sl, :] = (prob[r, sl, ks].astype(F32) * (score[sl, ks] - inn)).astype(BF16)
            return carry

        lax.fori_loop(0, 2 * local // 16, score_chunk, 0, unroll=2)
        q_t = jnp.transpose(qp[r])
        d_t = jnp.transpose(dp[r])
        dq = jnp.zeros((2 * local, 128), F32)
        for m in range(nseq):
            k = m * local // width
            ks = slice(m * local - k * width, m * local - k * width + local)
            ds_m = dsc[k, :, ks]
            dq = dq + mm(ds_m, kvs[m][r])
            dkv_t = mm(q_t, ds_m) + mm(d_t, prob[r, :, m * local : (m + 1) * local])
            dkvs[m][r] = jnp.transpose(dkv_t).astype(BF16)
        up2 = lax.broadcasted_iota(jnp.int32, dq.shape, 1) >= 64
        dq = jnp.where(up2, 0.0, dq) * 0.125
        dq = dq + pltpu.roll(dq, 64, 1)
        cd[0, r * local : (r + 1) * local, :] = dq[:local]
        cd[1, r * local : (r + 1) * local, :] = dq[local:]

    def query_chunk(c, carry):
        sl = pl.ds(pl.multiple_of(c * ch, ch), ch)
        i0 = idx_b[0, sl, :]
        i1 = idx_b[1, sl, :]
        m0 = cd[0, sl, :]
        m1 = cd[1, sl, :]
        for b in range(4):
            low = jnp.where(
                half + 2 * b == i0, m0, jnp.where(half + 2 * b == i1, m1, 0.0)
            ).astype(BF16)
            mix[sl, b * 128 : (b + 1) * 128] = low
            vacc[16:24, b * 128 : (b + 1) * 128] += fold8(low.astype(F32))
        return carry

    lax.fori_loop(0, nch, query_chunk, 0)
    xn_t = jnp.transpose(xn[...])
    acc_wq[...] += mm(xn_t, mix[...])
    acc_r[...] += mm(xn_t, gl[...])
    wide1[...] = mmt(mix[...], can[:, 0:512]) + mmt(gl[...], can[:, 640:768])

    def part_chunk(c, carry):
        sl = pl.ds(pl.multiple_of(c * ch, ch), ch)
        xhat, rstd = norm_parts(tok[sl, :].astype(F32))
        g = wide1[sl, :]
        part_ref[sl, :] = mid[sl, :] + norm_back(g * gain1, xhat, rstd)
        vacc[0:8, :] += fold8(g * xhat)
        vacc[8:16, :] += fold8(g)
        return carry

    lax.fori_loop(0, nch, part_chunk, 0)

    if last:

        @pl.when(step == steps - 1)
        def _():
            for b in range(nblk):
                j = rel(gbits_u, me ^ b)
                rows = slice(b * 16, (b + 1) * 16)
                gu_ref[j, :, 0:2048] = acc_up[rows, :].astype(BF16)
                gu_ref[j, :, 2048:2176] = acc_r[rows, :].astype(BF16)
                j = rel(gbits_d, me ^ b)
                gd_ref[j, 64:80, :] = acc_wo[rows, :].astype(BF16)
                gd_ref[j, 80:96, :] = acc_wq[rows, :].astype(BF16)
            for c in range(nblk // 2):
                both = jnp.transpose(acc_dn[:, c * 128 : (c + 1) * 128]).astype(BF16)
                gd_ref[rel(gbits_d, me ^ (2 * c)), 0:64, :] = both[:64]
                gd_ref[rel(gbits_d, me ^ (2 * c + 1)), 0:64, :] = both[64:]


def kernel_e(cfg, *refs):
    first, last, steps, gbits, nblk, nseq = cfg
    refs = list(refs)

    def take(n):
        got = refs[:n]
        del refs[:n]
        return got

    sc, part, tok = take(3)
    dkvs = take(nseq)
    can, vec, vacc = take(3)
    acc_in = []
    if not first:
        acc_in = take(2)
        take(1)
    (out_ref,) = take(1)
    if last:
        (gs_ref,) = take(1)
    acc_kv, acc_l = take(2)
    wide, xh, xn, dk = refs
    me = sc[0]
    step = pl.program_id(0)
    tile = tok.shape[0]
    local = tile // R
    ch = 64
    nch = tile // ch
    gain = vec[0:1, :]
    shift = vec[1:2, :]

    @pl.when(step == 0)
    def _():
        if first:
            acc_kv[...] = jnp.zeros_like(acc_kv)
            acc_l[...] = jnp.zeros_like(acc_l)
        else:
            acc_kv[...] = acc_in[0][...]
            acc_l[...] = acc_in[1][...]

    for r in range(R):
        total = dkvs[0][r].astype(F32)
        for m in range(1, nseq):
            total = total + dkvs[m][r].astype(F32)
        dk[r * local : (r + 1) * local, :] = total.astype(BF16)
    wide[...] = mmt(dk[...], can[:, 512:640])

    def chunk(c, carry):
        sl = pl.ds(pl.multiple_of(c * ch, ch), ch)
        xhat, rstd = norm_parts(tok[sl, :].astype(F32))
        xn[sl, :] = (xhat * gain + shift).astype(BF16)
        g = wide[sl, :]
        out_ref[sl, :] = (part[sl, :] + norm_back(g * gain, xhat, rstd)).astype(BF16)
        acc_l[0:8, :] += fold8(g * xhat)
        acc_l[8:16, :] += fold8(g)
        return carry

    lax.fori_loop(0, nch, chunk, 0)
    acc_kv[...] += mm(jnp.transpose(xn[...]), dk[...])

    if last:

        @pl.when(step == steps - 1)
        def _():
            row = lax.broadcasted_iota(jnp.int32, (16, 512), 0)
            table = jnp.zeros((16, 512), F32)
            for v in range(7):
                line = vacc[v * 8 : (v + 1) * 8, :]
                if v < 2:
                    line = line + acc_l[v * 8 : (v + 1) * 8, :]
                table = jnp.where(row == v, jnp.sum(line, axis=0, keepdims=True), table)
            ex = spread_matrix()
            pick = spread_rows()
            ups = []
            for b in range(4):
                line = jnp.sum(vacc[(7 + b) * 8 : (8 + b) * 8, :], axis=0, keepdims=True)
                ups.append(mmt(jnp.where(pick, line, 0.0).astype(BF16), ex))
            table = table + jnp.concatenate(ups, axis=1)
            table = jnp.concatenate([table, jnp.zeros((112, 512), F32)], axis=0)
            cols = jnp.transpose(table)
            for b in range(nblk):
                j = rel(gbits, me ^ b)
                rows = slice(b * 16, (b + 1) * 16)
                gs_ref[j, :, 0:128] = acc_kv[rows, :].astype(BF16)
                gs_ref[j, :, 128:256] = cols[rows, :].astype(BF16)


def swap(x, hop, sizes):
    axis, mask = hop
    return lax.ppermute(x, axis, [(i, i ^ mask) for i in range(sizes[axis])])


def widen(x, order, sizes):
    for hop in order[:-1]:
        x = jnp.concatenate([x, swap(x, hop, sizes)], axis=0)
    return x, swap(x, order[-1], sizes)


def narrow(x, order, sizes):
    for n, hop in enumerate(order):
        h = x.shape[0] // 2
        got = swap(x[h:], hop, sizes)
        x = x[:h].astype(F32) + got.astype(F32)
        if n < len(order) - 1:
            x = x.astype(BF16)
    return x[0]


def whole(shape):
    zeros = (0,) * len(shape)
    return pl.BlockSpec(shape, lambda i: zeros, pipeline_mode=pl.Buffered(1))


def body(
    sizes,
    tokens,
    cotangent,
    expert_index,
    segments,
    ln1_gain,
    ln1_bias,
    w_router,
    w_query,
    b_query,
    w_keyval,
    w_out,
    b_out,
    ln2_gain,
    ln2_bias,
    w_up,
    b_up,
    w_down,
    b_down,
):
    nseq, nbatch = sizes["seq"], sizes["batch"]
    rows_dev, local, d = tokens.shape
    ff = w_up.shape[1]
    experts = w_router.shape[1]
    group = max(1, 16 // w_query.shape[0])
    high = nbatch // group
    nblk = nseq * high
    bidx = lax.axis_index("batch")
    sidx = lax.axis_index("seq")
    blk = sidx * high + bidx // group
    sc = jnp.stack([blk, sidx]).astype(jnp.int32)

    groups = [[g * group + i for i in range(group)] for g in range(high)]

    def near(w):
        if group == 1:
            return w
        return lax.all_gather(w, "batch", axis=0, tiled=True, axis_index_groups=groups)

    def near_sum(g):
        if group == 1:
            return g
        return lax.psum_scatter(
            g, "batch", scatter_dimension=0, tiled=True, axis_index_groups=groups
        )

    bb = [("batch", group << i) for i in range((high - 1).bit_length())]
    zz = [("seq", 1 << i) for i in range((nseq - 1).bit_length())]
    core, xy = bb[0], bb[1:]

    def bit_of(hop):
        axis, mask = hop
        step = mask // group if axis == "batch" else mask * high
        return step.bit_length() - 1

    def gather_bits(order):
        return tuple((bit_of(hop), i) for i, hop in enumerate(order))

    def scatter_bits(order):
        return tuple((bit_of(hop), len(order) - 1 - i) for i, hop in enumerate(order))

    def weave(a, b):
        out = []
        for i in range(max(len(a), len(b))):
            out += list(a[i : i + 1]) + list(b[i : i + 1])
        return out

    order_a = zz[::-1] + xy + [core]
    order_u = weave(zz[::-1], xy) + [core]
    order_d = weave(xy, zz[::-1]) + [core]
    back_u = [core] + xy[::-1] + zz
    back_d = [core] + xy + zz
    back_s = [core] + xy[::-1] + zz

    cols = [near(v)[:, None] for v in (ln1_gain, ln1_bias, b_query, b_out, ln2_gain, ln2_bias, b_down)]
    bu = jnp.transpose(near(b_up).reshape(-1, 16))
    pad0 = jnp.zeros((16, 1), BF16)
    pad1 = jnp.zeros((16, 128 - 20), BF16)
    pack = jnp.concatenate(
        [near(w_query), near(w_keyval), near(w_router)] + cols + [pad0, bu, pad1], axis=1
    )[None]
    own, got = widen(pack, order_a, sizes)
    pack = jnp.concatenate([own, got], axis=0)
    u_own, u_got = widen(near(w_up)[None], order_u, sizes)
    d_own, d_got = widen(
        jnp.concatenate([near(w_down), near(w_out)], axis=0)[None], order_d, sizes
    )

    smem = pl.BlockSpec(memory_space=pltpu.SMEM)
    anywhere = pl.BlockSpec(memory_space=pl.ANY)
    params = pltpu.CompilerParams(vmem_limit_bytes=VMEM_LIMIT)
    shape = jax.ShapeDtypeStruct

    can, vec, bup, *kv_parts = pl.pallas_call(
        functools.partial(kernel_a, gather_bits(order_a), nblk, PARTS),
        out_shape=(
            shape((d, 768), BF16),
            shape((16, d), F32),
            shape((8, ff), F32),
        )
        + tuple(shape((n, local, 128), BF16) for n in PARTS),
        in_specs=[smem, pl.BlockSpec(memory_space=pltpu.VMEM), pl.BlockSpec(memory_space=pltpu.VMEM)],
        out_specs=tuple(pl.BlockSpec(memory_space=pltpu.VMEM) for unused in range(3 + len(PARTS))),
        compiler_params=params,
        name="project",
    )(sc, pack, tokens)

    flat = (rows_dev * local, d)
    tok = tokens.reshape(flat)
    cot = cotangent.reshape(flat)
    idx = jnp.transpose(expert_index, (0, 2, 1))
    seg = segments[:, None, :]
    tile = R * local

    kv_all = [
        [kv] + [swap(kv, ("seq", m), sizes) for m in range(1, nseq)] for kv in kv_parts
    ]
    acc_shapes = (
        shape((d, ff), F32),
        shape((d, ff), F32),
        shape((d, d), F32),
        shape((d, d), F32),
        shape((d, 128), F32),
    )
    vacc_shape = shape((88, d), F32)
    row0 = 0
    acc = None
    out = part = vacc = None
    dkv_all = []
    for p, count in enumerate(PARTS):
        first, last = p == 0, p == len(PARTS) - 1
        steps = count // R
        base = row0 // R
        rowspec = pl.BlockSpec((tile, d), lambda i, base=base: (base + i, 0))
        kvspec = pl.BlockSpec((R, local, 128), lambda i: (i, 0, 0))
        ins = [sc, tok, cot, idx, seg] + kv_all[p] + [can, vec, bup, u_own, u_got, d_own, d_got]
        specs = [
            smem,
            rowspec,
            rowspec,
            pl.BlockSpec((R, 2, local), lambda i, base=base: (base + i, 0, 0)),
            pl.BlockSpec((R, 1, local * nseq), lambda i, base=base: (base + i, 0, 0)),
        ]
        specs += [kvspec] * nseq
        specs += [whole(can.shape), whole(vec.shape), whole(bup.shape)] + [anywhere] * 4
        alias = {}
        if not first:
            ins += list(acc) + [vacc, out, part]
            specs += [anywhere] * 8
            alias = {len(ins) - 2: 0, len(ins) - 1: 1}
        outs = [shape(flat, BF16), shape(flat, F32)]
        outs += [shape((count, local, 128), BF16)] * nseq + [vacc_shape]
        ospecs = [rowspec, rowspec] + [kvspec] * nseq + [whole(vacc_shape.shape)]
        scratch = []
        if last:
            outs += [shape((nblk, 16, ff + 128), BF16), shape((nblk, 96, d), BF16)]
            ospecs += [whole((nblk, 16, ff + 128)), whole((nblk, 96, d))]
            scratch += [pltpu.VMEM(a.shape, F32) for a in acc_shapes]
        else:
            outs += list(acc_shapes)
            ospecs += [whole(a.shape) for a in acc_shapes]
        wide = (tile, d)
        scratch += [
            pltpu.VMEM((d, ff), BF16),
            pltpu.VMEM((ff, d), BF16),
            pltpu.VMEM((d, d), BF16),
            pltpu.VMEM(wide, BF16),
            pltpu.VMEM(wide, F32),
            pltpu.VMEM((R, 2 * local, 128), BF16),
            pltpu.VMEM((R, 2 * local, 128), BF16),
            pltpu.VMEM((2, tile, 128), jnp.int32),
            pltpu.VMEM((2, tile, 128), F32),
            pltpu.VMEM((2, tile, 128), F32),
            pltpu.VMEM((2 * tile, 128), F32),
            pltpu.VMEM((R, 2 * local, nseq * local), BF16),
            pltpu.VMEM((2 * local, nseq * local), F32),
            pltpu.VMEM(wide, F32),
            pltpu.VMEM(wide, F32),
            pltpu.VMEM(wide, F32),
            pltpu.VMEM(wide, F32),
            pltpu.VMEM((tile, 128), F32),
            pltpu.VMEM(wide, BF16),
            pltpu.VMEM(wide, BF16),
            pltpu.VMEM((2, tile, 512), F32),
            pltpu.VMEM((2, tile, 512), F32),
            pltpu.VMEM((2, tile, 512), BF16),
            pltpu.VMEM((2, tile, 512), BF16),
            pltpu.VMEM((tile, 128), F32),
            pltpu.VMEM((tile, 128), BF16),
            pltpu.SemaphoreType.DMA((3,)),
            pltpu.SemaphoreType.DMA((6,)),
        ]
        cfg = (
            first,
            last,
            steps,
            gather_bits(order_u),
            gather_bits(order_d),
            scatter_bits(back_u),
            scatter_bits(back_d),
            nblk,
            nseq,
        )
        got = pl.pallas_call(
            functools.partial(kernel_b, cfg),
            grid=(steps,),
            out_shape=tuple(outs),
            in_specs=specs,
            out_specs=tuple(ospecs),
            scratch_shapes=scratch,
            input_output_aliases=alias,
            compiler_params=params,
            name="layer",
        )(*ins)
        out, part = got[0], got[1]
        dkv = got[2 : 2 + nseq]
        dkv_all.append(
            [dkv[0]] + [swap(dkv[m], ("seq", m), sizes) for m in range(1, nseq)]
        )
        vacc = got[2 + nseq]
        acc = got[3 + nseq :]
        row0 += count

    gu, gd = acc
    gu = narrow(gu, back_u, sizes)
    gd = narrow(gd, back_d, sizes)

    row0 = 0
    grad = None
    eacc = None
    for p, count in enumerate(PARTS):
        first, last = p == 0, p == len(PARTS) - 1
        steps = count // R
        base = row0 // R
        rowspec = pl.BlockSpec((tile, d), lambda i, base=base: (base + i, 0))
        kvspec = pl.BlockSpec((R, local, 128), lambda i: (i, 0, 0))
        ins = [sc, part, tok] + dkv_all[p] + [can, vec, vacc]
        specs = [smem, rowspec, rowspec] + [kvspec] * nseq
        specs += [whole(can.shape), whole(vec.shape), whole(vacc.shape)]
        alias = {}
        if not first:
            ins += list(eacc) + [grad]
            specs += [whole((d, 128)), whole((16, d)), anywhere]
            alias = {len(ins) - 1: 0}
        outs = [shape(flat, BF16)]
        ospecs = [rowspec]
        scratch = []
        if last:
            outs += [shape((nblk, 16, 256), BF16)]
            ospecs += [whole((nblk, 16, 256))]
            scratch += [pltpu.VMEM((d, 128), F32), pltpu.VMEM((16, d), F32)]
        else:
            outs += [shape((d, 128), F32), shape((16, d), F32)]
            ospecs += [whole((d, 128)), whole((16, d))]
        scratch += [
            pltpu.VMEM((tile, d), F32),
            pltpu.VMEM((8, 128), F32),
            pltpu.VMEM((tile, d), BF16),
            pltpu.VMEM((tile, 128), BF16),
        ]
        cfg = (first, last, steps, scatter_bits(back_s), nblk, nseq)
        got = pl.pallas_call(
            functools.partial(kernel_e, cfg),
            grid=(steps,),
            out_shape=tuple(outs),
            in_specs=specs,
            out_specs=tuple(ospecs),
            scratch_shapes=scratch,
            input_output_aliases=alias,
            compiler_params=params,
            name="finish",
        )(*ins)
        grad = got[0]
        eacc = got[1:]
        row0 += count
    gs = narrow(eacc[0], back_s, sizes)

    def vector(v):
        return near_sum(gs[:, 128 + v])

    grad_b_up = near_sum(jnp.transpose(gs[:, 136:140]).reshape(-1))
    return (
        out.reshape(tokens.shape),
        grad.reshape(tokens.shape),
        vector(0),
        vector(1),
        near_sum(gu[:, ff : ff + experts]),
        near_sum(gd[80:96]),
        vector(2),
        near_sum(gs[:, :128]),
        near_sum(gd[64:80]),
        vector(3),
        vector(4),
        vector(5),
        near_sum(gu[:, :ff]),
        grad_b_up,
        near_sum(gd[:64]),
        vector(6),
    )


def solution(mesh):
    sizes = {name: mesh.shape[name] for name in ("seq", "batch")}
    both = ("seq", "batch")
    row = P("batch", "seq", None)
    vector, matrix = P(both), P(both, None)
    in_specs = (
        row,
        row,
        row,
        P("batch", None),
        vector,
        vector,
        matrix,
        matrix,
        vector,
        matrix,
        matrix,
        vector,
        vector,
        vector,
        matrix,
        vector,
        matrix,
        vector,
    )
    out_specs = (
        row,
        row,
        vector,
        vector,
        matrix,
        matrix,
        vector,
        matrix,
        matrix,
        vector,
        vector,
        vector,
        matrix,
        vector,
        matrix,
        vector,
    )
    return jax.shard_map(
        functools.partial(body, sizes),
        mesh=mesh,
        in_specs=in_specs,
        out_specs=out_specs,
        check_vma=False,
    )
```

time: 1450 us -> 385 us (0.27)
  waiting for transfers between devices: 747 us -> 134 us
  blocking collectives: 240 us -> 0 us
  local copies, waits for them, and re-layouts: 223 us -> 27.9 us
  matrix products: 167 us -> 0 us
  Pallas kernels: 0 us -> 159 us
  starting transfers between devices: 0.62 us -> 54.3 us
  other arithmetic: 41.3 us -> 8.02 us
    reduce_scatter x6 -> x0, waiting for transfers between devices: 653 us -> none  [the longest x1 140 us: body(): lax.psum_scatter(grad_up, ('seq', 'batch'), scatter_dimension=0, tiled=True)]
    dot_general x73 -> x0, matrix products: 166 us -> none  [the longest x16 23.5 us: masked_scores(): jnp.einsum('ceh,kh->eck', row_query, key_part, preferred_element_type=jnp...]
    all_gather x4 -> x0, blocking collectives: 161 us -> none  [the longest x1 41.3 us: body(): lax.all_gather(w_out, ('seq', 'batch'), axis=0, tiled=True)]
    gather x9 -> x0, local copies, waits for them, and re-layouts: 159 us -> none  [the longest x2 69.3 us: body(): jnp.take_along_axis(grad_mixed, expert_index[..., None], axis=2)]
    pallas_call x0 -> x3, Pallas kernels: none -> 159 us  [the longest x1 138 us: body(): pl.pallas_call(functools.partial(kernel_b, cfg), grid=(steps,), out_shape...]
    ppermute x0 -> x36, waiting for transfers between devices: none -> 134 us  [swap(): return lax.ppermute(x, axis, [(i, i ^ mask) for i in range(sizes[axis])])]
    unnamed x11 -> x0, waiting for transfers between devices: 93.9 us -> none
    unnamed x2 -> x0, blocking collectives: 79.4 us -> none
  transfers between devices with their start and end apart: 10 -> 36, of which waited for: 7 -> 20; matrix products, arithmetic and copies ran while one was open for 16% -> 6% of each run, Pallas kernels for 0% -> 1%
where the time goes in v1:
time: 385 us; the launch traced here: 384 us
  Pallas kernels  159 us (41%)
  waiting for transfers between devices  134 us (35%)
  starting transfers between devices  54.3 us (14%)
  local copies, waits for them, and re-layouts  27.9 us (7%)
  other arithmetic  8.02 us (2%)
    pallas_call x1, Pallas kernels, body(): pl.pallas_call(functools.partial(kernel_b, cfg), grid=(steps,), out_shape...  138 us
    ppermute x36, waiting for transfers between devices, swap(): return lax.ppermute(x, axis, [(i, i ^ mask) for i in range(sizes[axis])])  134 us
    ppermute x36, starting transfers between devices, swap(): return lax.ppermute(x, axis, [(i, i ^ mask) for i in range(sizes[axis])])  54.3 us
    pallas_call x1, Pallas kernels, body(): pl.pallas_call(functools.partial(kernel_e, cfg), grid=(steps,), out_shape...  15.8 us
    unnamed x41, local copies, waits for them, and re-layouts  11.2 us
  transfers between devices with their start and end apart: 36, of which 20 were waited for; matrix products, arithmetic and copies ran while one was open for 6% of the time, Pallas kernels for 1%

profile of v1, /device:TPU:0, one launch (start us, length us, event | category | flops | bytes accessed | tf_op | source)
XLA Modules:
  0.0 383.9 jit_solution(16533608949182266547)
XLA Ops:
  8.3 4.1 %collective-permute-start = (bf16[1,16,768]{2,1,0:T(8,128)(2,1)S(1)}, bf16[1,16,768]{2,1,0:T(8,128)(2,1)S(1)}, u32[]{:S(2)}, u32[]{:S(2)}) collective-permute-start(bf16[1,16,768]{2,1,0:T(8,128)(2,1)S(1)} %bitcast.43), channel_id=1, source_target_pairs={{0,16},{8,24},{16,0},{24,8},{1,17},{9,25},{17,1},{25,9},{2,18},{10... | collective-permute-start | bytes 73736 | tf_op jit(solution)/shard_map/ppermute | solution.py:570
  13.3 1.7 collective-permute-start.13
  18.0 1.6 collective-permute-start.1
  24.6 2.7 collective-permute-start.14
  29.7 3.5 collective-permute-done.14
  35.6 6.2 %collective-permute-done.15 = bf16[4,80,512]{2,1,0:T(8,128)(2,1)S(1)} collective-permute-done((bf16[4,80,512]{2,1,0:T(8,128)(2,1)S(1)}, bf16[4,80,512]{2,1,0:T(8,128)(2,1)S(1)}, u32[]{:S(2)}, u32[]{:S(2)}) %collective-permute-start.15) | collective-permute-done | bytes 327712 | tf_op jit(solution)/shard_map/ppermute | solution.py:570
  44.4 12.2 %collective-permute-done.16 = bf16[8,80,512]{2,1,0:T(8,128)(2,1)S(1)} collective-permute-done((bf16[8,80,512]{2,1,0:T(8,128)(2,1)S(1)}, bf16[8,80,512]{2,1,0:T(8,128)(2,1)S(1)}, u32[]{:S(2)}, u32[]{:S(2)}) %collective-permute-start.16) | collective-permute-done | bytes 655392 | tf_op jit(solution)/shard_map/ppermute | solution.py:570
  59.6 2.6 collective-permute-done.4
  64.1 4.6 %project.1 = (bf16[512,768]{1,0:T(8,128)(2,1)}, f32[16,512]{1,0:T(8,128)}, f32[8,2048]{1,0:T(8,128)}, bf16[8,256,128]{2,1,0:T(8,128)(2,1)}) custom-call(s32[2]{0:T(128)} %pad_add_fusion.sc.refs_0_, bf16[32,16,768]{2,1,0:T(8,128)(2,1)} %copy-done.6, bf16[8,256,512]{2,1,0:T(8,128)(2,1)} %tok.1), custom_call_target="tpu_custom_call" | custom-call | tf_op jit(solution)/shard_map/project/pallas_call | solution.py:688
  68.7 2.6 collective-permute-start.7
  71.4 1.8 collective-permute-start.5
  73.8 11.9 %collective-permute-done.7.refs_8_ = bf16[8,256,128]{2,1,0:T(8,128)(2,1)S(1)} collective-permute-done((bf16[8,256,128]{2,1,0:T(8,128)(2,1)}, bf16[8,256,128]{2,1,0:T(8,128)(2,1)S(1)}, u32[]{:S(2)}, u32[]{:S(2)}) %collective-permute-start.7) | collective-permute-done | bytes 524320 | tf_op jit(solution)/shard_map/ppermute | solution.py:570
  85.7 30.8 %collective-permute-done.6.refs_7_ = bf16[8,256,128]{2,1,0:T(8,128)(2,1)S(1)} collective-permute-done((bf16[8,256,128]{2,1,0:T(8,128)(2,1)}, bf16[8,256,128]{2,1,0:T(8,128)(2,1)S(1)}, u32[]{:S(2)}, u32[]{:S(2)}) %collective-permute-start.6) | collective-permute-done | bytes 524320 | tf_op jit(solution)/shard_map/ppermute | solution.py:570
  118.3 138.1 %layer.1 = (bf16[2048,512]{1,0:T(8,128)(2,1)}, f32[2048,512]{1,0:T(8,128)}, bf16[8,256,128]{2,1,0:T(8,128)(2,1)}, bf16[8,256,128]{2,1,0:T(8,128)(2,1)}, bf16[8,2...) custom-call(s32[2]{0:T(128)} %pad_add_fusion.sc.refs_0_, ...), custom_call_target="tpu_custom_call" | custom-call | tf_op jit(solution)/shard_map/layer/pallas_call | solution.py:798
  256.5 3.2 collective-permute-start.19
  260.9 19.3 %collective-permute-done.18.refs_4_ = bf16[8,256,128]{2,1,0:T(8,128)(2,1)S(1)} collective-permute-done((bf16[8,256,128]{2,1,0:T(8,128)(2,1)}, bf16[8,256,128]{2,1,0:T(8,128)(2,1)S(1)}, u32[]{:S(2)}, u32[]{:S(2)}) %collective-permute-start.18) | collective-permute-done | bytes 524320 | tf_op jit(solution)/shard_map/ppermute | solution.py:570
  280.2 15.0 %collective-permute-done.19.refs_5_ = bf16[8,256,128]{2,1,0:T(8,128)(2,1)S(1)} collective-permute-done((bf16[8,256,128]{2,1,0:T(8,128)(2,1)}, bf16[8,256,128]{2,1,0:T(8,128)(2,1)S(1)}, u32[]{:S(2)}, u32[]{:S(2)}) %collective-permute-start.19) | collective-permute-done | bytes 524320 | tf_op jit(solution)/shard_map/ppermute | solution.py:570
  296.2 15.8 %finish.1 = (bf16[2048,512]{1,0:T(8,128)(2,1)}, bf16[32,16,256]{2,1,0:T(8,128)(2,1)}) custom-call(s32[2]{0:T(128)} %pad_add_fusion.sc.refs_0_, f32[2048,512]{1,0:T(8,128)} %get-tuple-element.36.refs_1_, bf16[2048,512]{1,0:T(8,128)(2,1)} %bitcast.37, bf16[8,256,128]{2,1,0:T(8,128)(2,1)} %get-tuple-element.37.refs_3_, bf16[8,256,128]{2,1,0:T(8,128)(2,1)} %copy-done.10, ...), custom_call_target="tpu_custom_call" | custom-call | tf_op jit(solution)/shard_map/finish/pallas_call | solution.py:856
  315.5 1.6 collective-permute-start.22
  317.1 2.7 collective-permute-done.22
  320.9 3.0 collective-permute-done.23
  323.8 10.0 %collective-permute-start.24 = (bf16[2,16,256]{2,1,0:T(8,128)(2,1)S(1)}, bf16[2,16,256]{2,1,0:T(8,128)(2,1)S(1)}, u32[]{:S(2)}, u32[]{:S(2)}) collective-permute-start(bf16[2,16,256]{2,1,0:T(8,128)(2,1)S(1)} %slice.193), channel_id=1, source_target_pairs={{0,8},{8,0},{16,24},{24,16},{1,9},{9,1},{17,25},{25,17},{2,10},{10... | collective-permute-start | bytes 49160 | tf_op jit(solution)/shard_map/ppermute | solution.py:570
  333.8 1.7 collective-permute-done.24
  335.6 3.1 collective-permute-start.25
  338.6 1.6 collective-permute-done.25
  346.6 5.5 %collective-permute-done.27 = bf16[8,16,2176]{2,1,0:T(8,128)(2,1)} collective-permute-done((bf16[8,16,2176]{2,1,0:T(8,128)(2,1)}, bf16[8,16,2176]{2,1,0:T(8,128)(2,1)}, u32[]{:S(2)}, u32[]{:S(2)}) %collective-permute-start.27) | collective-permute-done | bytes 557088 | tf_op jit(solution)/shard_map/ppermute | solution.py:570
  354.4 7.4 %collective-permute-done.32 = bf16[8,96,512]{2,1,0:T(8,128)(2,1)} collective-permute-done((bf16[8,96,512]{2,1,0:T(8,128)(2,1)S(1)}, bf16[8,96,512]{2,1,0:T(8,128)(2,1)}, u32[]{:S(2)}, u32[]{:S(2)}) %collective-permute-start.32) | collective-permute-done | bytes 786464 | tf_op jit(solution)/shard_map/ppermute | solution.py:570
  364.8 1.7 collective-permute-start.29
  366.5 4.5 %collective-permute-done.33 = bf16[4,96,512]{2,1,0:T(8,128)(2,1)S(1)} collective-permute-done((bf16[4,96,512]{2,1,0:T(8,128)(2,1)S(1)}, bf16[4,96,512]{2,1,0:T(8,128)(2,1)S(1)}, u32[]{:S(2)}, u32[]{:S(2)}) %collective-permute-start.33) | collective-permute-done | bytes 393248 | tf_op jit(solution)/shard_map/ppermute | solution.py:570
  371.1 1.7 collective-permute-start.34
  374.2 2.6 collective-permute-done.34
  376.9 2.7 collective-permute-start.35
  (152 shorter events, 55.1 us)
Async XLA Ops:
  8.3 9.7 %collective-permute-start = (bf16[1,16,768]{2,1,0:T(8,128)(2,1)S(1)}, bf16[1,16,768]{2,1,0:T(8,128)(2,1)S(1)}, u32[]{:S(2)}, u32[]{:S(2)}) collective-permute-start(bf16[1,16,768]{2,1,0:T(8,128)(2,1)S(1)} %bitcast.43), channel_id=1, source_target_pairs={{0,16},{8,24},{16,0},{24,8},{1,17},{9,25},{17,1},{25,9},{2,18},{10... | collective-permute-start | bytes 73736 | tf_op jit(solution)/shard_map/ppermute | solution.py:570
  12.4 7.9 %collective-permute-start.8 = (bf16[1,16,2048]{2,1,0:T(8,128)(2,1)}, bf16[1,16,2048]{2,1,0:T(8,128)(2,1)S(1)}, u32[]{:S(2)}, u32[]{:S(2)}) collective-permute-start(bf16[1,16,2048]{2,1,0:T(8,128)(2,1)} %bitcast.39), channel_id=1, source_target_pairs={{0,16},{8,24},{16,0},{24,8},{1,17},{9,25},{17,1},{25,9},{2,18},{10... | collective-permute-start | bytes 196616 | tf_op jit(solution)/shard_map/ppermute | solution.py:570
  13.3 11.2 %collective-permute-start.13 = (bf16[1,80,512]{2,1,0:T(8,128)(2,1)S(1)}, bf16[1,80,512]{2,1,0:T(8,128)(2,1)S(1)}, u32[]{:S(2)}, u32[]{:S(2)}) collective-permute-start(bf16[1,80,512]{2,1,0:T(8,128)(2,1)S(1)} %maximum_bitcast_fusion), channel_id=1, source_target_pairs={{0,2},{1,3},{2,0},{3,1},{4,6},{5,7},{6,4},{7,5},{8,10},{9,11},{10,... | collective-permute-start | bytes 245768 | tf_op jit(solution)/shard_map/ppermute | solution.py:570
  18.0 4.3 %collective-permute-start.1 = (bf16[2,16,768]{2,1,0:T(8,128)(2,1)S(1)}, bf16[2,16,768]{2,1,0:T(8,128)(2,1)S(1)}, u32[]{:S(2)}, u32[]{:S(2)}) collective-permute-start(bf16[2,16,768]{2,1,0:T(8,128)(2,1)S(1)} %pad_maximum_fusion.8), channel_id=1, source_target_pairs={{0,8},{8,0},{16,24},{24,16},{1,9},{9,1},{17,25},{25,17},{2,10},{10... | collective-permute-start | bytes 147464 | tf_op jit(solution)/shard_map/ppermute | solution.py:570
  21.1 13.7 %collective-permute-start.9 = (bf16[2,16,2048]{2,1,0:T(8,128)(2,1)S(1)}, bf16[2,16,2048]{2,1,0:T(8,128)(2,1)S(1)}, u32[]{:S(2)}, u32[]{:S(2)}) collective-permute-start(bf16[2,16,2048]{2,1,0:T(8,128)(2,1)S(1)} %pad_maximum_fusion.6), channel_id=1, source_target_pairs={{0,2},{1,3},{2,0},{3,1},{4,6},{5,7},{6,4},{7,5},{8,10},{9,11},{10,... | collective-permute-start | bytes 393224 | tf_op jit(solution)/shard_map/ppermute | solution.py:570
  22.4 5.1 %collective-permute-start.2 = (bf16[4,16,768]{2,1,0:T(8,128)(2,1)S(1)}, bf16[4,16,768]{2,1,0:T(8,128)(2,1)S(1)}, u32[]{:S(2)}, u32[]{:S(2)}) collective-permute-start(bf16[4,16,768]{2,1,0:T(8,128)(2,1)S(1)} %pad_maximum_fusion.7), channel_id=1, source_target_pairs={{0,2},{1,3},{2,0},{3,1},{4,6},{5,7},{6,4},{7,5},{8,10},{9,11},{10,... | collective-permute-start | bytes 294920 | tf_op jit(solution)/shard_map/ppermute | solution.py:570
  24.6 8.6 %collective-permute-start.14 = (bf16[2,80,512]{2,1,0:T(8,128)(2,1)S(1)}, bf16[2,80,512]{2,1,0:T(8,128)(2,1)S(1)}, u32[]{:S(2)}, u32[]{:S(2)}) collective-permute-start(bf16[2,80,512]{2,1,0:T(8,128)(2,1)S(1)} %pad_maximum_fusion.5), channel_id=1, source_target_pairs={{0,16},{8,24},{16,0},{24,8},{1,17},{9,25},{17,1},{25,9},{2,18},{10... | collective-permute-start | bytes 491528 | tf_op jit(solution)/shard_map/ppermute | solution.py:570
  27.5 30.7 %collective-permute-start.3 = (bf16[8,16,768]{2,1,0:T(8,128)(2,1)S(1)}, bf16[8,16,768]{2,1,0:T(8,128)(2,1)S(1)}, u32[]{:S(2)}, u32[]{:S(2)}) collective-permute-start(bf16[8,16,768]{2,1,0:T(8,128)(2,1)S(1)} %pad_maximum_fusion.4), channel_id=1, source_target_pairs={{0,4},{1,5},{2,6},{3,7},{4,0},{5,1},{6,2},{7,3},{8,12},{9,13},{10,... | collective-permute-start | bytes 589832 | tf_op jit(solution)/shard_map/ppermute | solution.py:570
  33.3 8.6 %collective-permute-start.15 = (bf16[4,80,512]{2,1,0:T(8,128)(2,1)S(1)}, bf16[4,80,512]{2,1,0:T(8,128)(2,1)S(1)}, u32[]{:S(2)}, u32[]{:S(2)}) collective-permute-start(bf16[4,80,512]{2,1,0:T(8,128)(2,1)S(1)} %pad_maximum_fusion.2), channel_id=1, source_target_pairs={{0,4},{1,5},{2,6},{3,7},{4,0},{5,1},{6,2},{7,3},{8,12},{9,13},{10,... | collective-permute-start | bytes 983048 | tf_op jit(solution)/shard_map/ppermute | solution.py:570
  34.9 7.1 %collective-permute-start.10 = (bf16[4,16,2048]{2,1,0:T(8,128)(2,1)S(1)}, bf16[4,16,2048]{2,1,0:T(8,128)(2,1)S(1)}, u32[]{:S(2)}, u32[]{:S(2)}) collective-permute-start(bf16[4,16,2048]{2,1,0:T(8,128)(2,1)S(1)} %pad_maximum_fusion.3), channel_id=1, source_target_pairs={{0,8},{8,0},{16,24},{24,16},{1,9},{9,1},{17,25},{25,17},{2,10},{10... | collective-permute-start | bytes 786440 | tf_op jit(solution)/shard_map/ppermute | solution.py:570
  41.9 14.7 %collective-permute-start.16 = (bf16[8,80,512]{2,1,0:T(8,128)(2,1)S(1)}, bf16[8,80,512]{2,1,0:T(8,128)(2,1)S(1)}, u32[]{:S(2)}, u32[]{:S(2)}) collective-permute-start(bf16[8,80,512]{2,1,0:T(8,128)(2,1)S(1)} %pad_maximum_fusion), channel_id=1, source_target_pairs={{0,8},{8,0},{16,24},{24,16},{1,9},{9,1},{17,25},{25,17},{2,10},{10... | collective-permute-start | bytes 1966088 | tf_op jit(solution)/shard_map/ppermute | solution.py:570
  42.1 14.7 %collective-permute-start.11 = (bf16[8,16,2048]{2,1,0:T(8,128)(2,1)S(1)}, bf16[8,16,2048]{2,1,0:T(8,128)(2,1)S(1)}, u32[]{:S(2)}, u32[]{:S(2)}) collective-permute-start(bf16[8,16,2048]{2,1,0:T(8,128)(2,1)S(1)} %pad_maximum_fusion.1), channel_id=1, source_target_pairs={{0,4},{1,5},{2,6},{3,7},{4,0},{5,1},{6,2},{7,3},{8,12},{9,13},{10,... | collective-permute-start | bytes 1572872 | tf_op jit(solution)/shard_map/ppermute | solution.py:570
  56.7 59.8 %collective-permute-start.17 = (bf16[16,80,512]{2,1,0:T(8,128)(2,1)S(1)}, bf16[16,80,512]{2,1,0:T(8,128)(2,1)S(1)}, u32[]{:S(2)}, u32[]{:S(2)}) collective-permute-start(bf16[16,80,512]{2,1,0:T(8,128)(2,1)S(1)} %constant_dynamic-update-slice_fusion.16.refs_14_), channel_id=1, source_target_pairs={{0,1},{1,0},{2,3},{3,2},{4,5},{5,4},{6,7},{7,6},{8,9},{9,8},{10,11... | collective-permute-start | bytes 3932168 | tf_op jit(solution)/shard_map/ppermute | solution.py:570
  57.8 58.6 %collective-permute-start.12 = (bf16[16,16,2048]{2,1,0:T(8,128)(2,1)}, bf16[16,16,2048]{2,1,0:T(8,128)(2,1)}, u32[]{:S(2)}, u32[]{:S(2)}) collective-permute-start(bf16[16,16,2048]{2,1,0:T(8,128)(2,1)} %constant_dynamic-update-slice_fusion.11.refs_12_), channel_id=1, source_target_pairs={{0,1},{1,0},{2,3},{3,2},{4,5},{5,4},{6,7},{7,6},{8,9},{9,8},{10,11... | collective-permute-start | bytes 3145736 | tf_op jit(solution)/shard_map/ppermute | solution.py:570
  68.7 16.9 %collective-permute-start.7 = (bf16[8,256,128]{2,1,0:T(8,128)(2,1)}, bf16[8,256,128]{2,1,0:T(8,128)(2,1)S(1)}, u32[]{:S(2)}, u32[]{:S(2)}) collective-permute-start(bf16[8,256,128]{2,1,0:T(8,128)(2,1)} %get-tuple-element.31.refs_5_), channel_id=1, source_target_pairs={{0,24},{8,16},{16,8},{24,0},{1,25},{9,17},{17,9},{25,1},{2,26},{10... | collective-permute-start | bytes 1572872 | tf_op jit(solution)/shard_map/ppermute | solution.py:570
  71.3 45.1 %collective-permute-start.6 = (bf16[8,256,128]{2,1,0:T(8,128)(2,1)}, bf16[8,256,128]{2,1,0:T(8,128)(2,1)S(1)}, u32[]{:S(2)}, u32[]{:S(2)}) collective-permute-start(bf16[8,256,128]{2,1,0:T(8,128)(2,1)} %get-tuple-element.31.refs_5_), channel_id=1, source_target_pairs={{0,16},{8,24},{16,0},{24,8},{1,17},{9,25},{17,1},{25,9},{2,18},{10... | collective-permute-start | bytes 1572872 | tf_op jit(solution)/shard_map/ppermute | solution.py:570
  71.4 45.1 %collective-permute-start.5 = (bf16[8,256,128]{2,1,0:T(8,128)(2,1)}, bf16[8,256,128]{2,1,0:T(8,128)(2,1)S(1)}, u32[]{:S(2)}, u32[]{:S(2)}) collective-permute-start(bf16[8,256,128]{2,1,0:T(8,128)(2,1)} %get-tuple-element.31.refs_5_), channel_id=1, source_target_pairs={{0,8},{8,0},{16,24},{24,16},{1,9},{9,1},{17,25},{25,17},{2,10},{10... | collective-permute-start | bytes 1572872 | tf_op jit(solution)/shard_map/ppermute | solution.py:570
  256.4 23.8 %collective-permute-start.18 = (bf16[8,256,128]{2,1,0:T(8,128)(2,1)}, bf16[8,256,128]{2,1,0:T(8,128)(2,1)S(1)}, u32[]{:S(2)}, u32[]{:S(2)}) collective-permute-start(bf16[8,256,128]{2,1,0:T(8,128)(2,1)} %get-tuple-element.38), channel_id=1, source_target_pairs={{0,8},{8,0},{16,24},{24,16},{1,9},{9,1},{17,25},{25,17},{2,10},{10... | collective-permute-start | bytes 1572872 | tf_op jit(solution)/shard_map/ppermute | solution.py:570
  256.5 38.7 %collective-permute-start.19 = (bf16[8,256,128]{2,1,0:T(8,128)(2,1)}, bf16[8,256,128]{2,1,0:T(8,128)(2,1)S(1)}, u32[]{:S(2)}, u32[]{:S(2)}) collective-permute-start(bf16[8,256,128]{2,1,0:T(8,128)(2,1)} %get-tuple-element.39), channel_id=1, source_target_pairs={{0,16},{8,24},{16,0},{24,8},{1,17},{9,25},{17,1},{25,9},{2,18},{10... | collective-permute-start | bytes 1572872 | tf_op jit(solution)/shard_map/ppermute | solution.py:570
  259.7 35.5 %collective-permute-start.20 = (bf16[8,256,128]{2,1,0:T(8,128)(2,1)}, bf16[8,256,128]{2,1,0:T(8,128)(2,1)S(1)}, u32[]{:S(2)}, u32[]{:S(2)}) collective-permute-start(bf16[8,256,128]{2,1,0:T(8,128)(2,1)} %get-tuple-element.40), channel_id=1, source_target_pairs={{0,24},{8,16},{16,8},{24,0},{1,25},{9,17},{17,9},{25,1},{2,26},{10... | collective-permute-start | bytes 1572872 | tf_op jit(solution)/shard_map/ppermute | solution.py:570
  313.3 27.0 %collective-permute-start.26 = (bf16[16,16,2176]{2,1,0:T(8,128)(2,1)S(1)}, bf16[16,16,2176]{2,1,0:T(8,128)(2,1)S(1)}, u32[]{:S(2)}, u32[]{:S(2)}) collective-permute-start(bf16[16,16,2176]{2,1,0:T(8,128)(2,1)S(1)} %slice.154), channel_id=1, source_target_pairs={{0,1},{1,0},{2,3},{3,2},{4,5},{5,4},{6,7},{7,6},{8,9},{9,8},{10,11... | collective-permute-start | bytes 3342344 | tf_op jit(solution)/shard_map/ppermute | solution.py:570
  320.8 22.2 %collective-permute-start.31 = (bf16[16,96,512]{2,1,0:T(8,128)(2,1)S(1)}, bf16[16,96,512]{2,1,0:T(8,128)(2,1)S(1)}, u32[]{:S(2)}, u32[]{:S(2)}) collective-permute-start(bf16[16,96,512]{2,1,0:T(8,128)(2,1)S(1)} %slice.165), channel_id=1, source_target_pairs={{0,1},{1,0},{2,3},{3,2},{4,5},{5,4},{6,7},{7,6},{8,9},{9,8},{10,11... | collective-permute-start | bytes 4718600 | tf_op jit(solution)/shard_map/ppermute | solution.py:570
  323.8 11.7 %collective-permute-start.24 = (bf16[2,16,256]{2,1,0:T(8,128)(2,1)S(1)}, bf16[2,16,256]{2,1,0:T(8,128)(2,1)S(1)}, u32[]{:S(2)}, u32[]{:S(2)}) collective-permute-start(bf16[2,16,256]{2,1,0:T(8,128)(2,1)S(1)} %slice.193), channel_id=1, source_target_pairs={{0,8},{8,0},{16,24},{24,16},{1,9},{9,1},{17,25},{25,17},{2,10},{10... | collective-permute-start | bytes 49160 | tf_op jit(solution)/shard_map/ppermute | solution.py:570
  335.6 4.7 %collective-permute-start.25 = (bf16[1,16,256]{2,1,0:T(8,128)(2,1)S(1)}, bf16[1,16,256]{2,1,0:T(8,128)(2,1)S(1)}, u32[]{:S(2)}, u32[]{:S(2)}) collective-permute-start(bf16[1,16,256]{2,1,0:T(8,128)(2,1)S(1)} %slice.195), channel_id=1, source_target_pairs={{0,16},{8,24},{16,0},{24,8},{1,17},{9,25},{17,1},{25,9},{2,18},{10... | collective-permute-start | bytes 24584 | tf_op jit(solution)/shard_map/ppermute | solution.py:570
  341.4 10.7 %collective-permute-start.27 = (bf16[8,16,2176]{2,1,0:T(8,128)(2,1)}, bf16[8,16,2176]{2,1,0:T(8,128)(2,1)}, u32[]{:S(2)}, u32[]{:S(2)}) collective-permute-start(bf16[8,16,2176]{2,1,0:T(8,128)(2,1)} %slice.199), channel_id=1, source_target_pairs={{0,4},{1,5},{2,6},{3,7},{4,0},{5,1},{6,2},{7,3},{8,12},{9,13},{10,... | collective-permute-start | bytes 1671176 | tf_op jit(solution)/shard_map/ppermute | solution.py:570
  343.6 18.2 %collective-permute-start.32 = (bf16[8,96,512]{2,1,0:T(8,128)(2,1)S(1)}, bf16[8,96,512]{2,1,0:T(8,128)(2,1)}, u32[]{:S(2)}, u32[]{:S(2)}) collective-permute-start(bf16[8,96,512]{2,1,0:T(8,128)(2,1)S(1)} %slice.208), channel_id=1, source_target_pairs={{0,2},{1,3},{2,0},{3,1},{4,6},{5,7},{6,4},{7,5},{8,10},{9,11},{10,... | collective-permute-start | bytes 2359304 | tf_op jit(solution)/shard_map/ppermute | solution.py:570
  353.3 11.3 %collective-permute-start.28 = (bf16[4,16,2176]{2,1,0:T(8,128)(2,1)S(1)}, bf16[4,16,2176]{2,1,0:T(8,128)(2,1)S(1)}, u32[]{:S(2)}, u32[]{:S(2)}) collective-permute-start(bf16[4,16,2176]{2,1,0:T(8,128)(2,1)S(1)} %slice.201), channel_id=1, source_target_pairs={{0,2},{1,3},{2,0},{3,1},{4,6},{5,7},{6,4},{7,5},{8,10},{9,11},{10,... | collective-permute-start | bytes 835592 | tf_op jit(solution)/shard_map/ppermute | solution.py:570
  363.2 7.8 %collective-permute-start.33 = (bf16[4,96,512]{2,1,0:T(8,128)(2,1)S(1)}, bf16[4,96,512]{2,1,0:T(8,128)(2,1)S(1)}, u32[]{:S(2)}, u32[]{:S(2)}) collective-permute-start(bf16[4,96,512]{2,1,0:T(8,128)(2,1)S(1)} %slice.210), channel_id=1, source_target_pairs={{0,4},{1,5},{2,6},{3,7},{4,0},{5,1},{6,2},{7,3},{8,12},{9,13},{10,... | collective-permute-start | bytes 1179656 | tf_op jit(solution)/shard_map/ppermute | solution.py:570
  364.8 8.1 %collective-permute-start.29 = (bf16[2,16,2176]{2,1,0:T(8,128)(2,1)S(1)}, bf16[2,16,2176]{2,1,0:T(8,128)(2,1)S(1)}, u32[]{:S(2)}, u32[]{:S(2)}) collective-permute-start(bf16[2,16,2176]{2,1,0:T(8,128)(2,1)S(1)} %slice.203), channel_id=1, source_target_pairs={{0,8},{8,0},{16,24},{24,16},{1,9},{9,1},{17,25},{25,17},{2,10},{10... | collective-permute-start | bytes 417800 | tf_op jit(solution)/shard_map/ppermute | solution.py:570
  371.1 5.7 %collective-permute-start.34 = (bf16[2,96,512]{2,1,0:T(8,128)(2,1)S(1)}, bf16[2,96,512]{2,1,0:T(8,128)(2,1)S(1)}, u32[]{:S(2)}, u32[]{:S(2)}) collective-permute-start(bf16[2,96,512]{2,1,0:T(8,128)(2,1)S(1)} %slice.212), channel_id=1, source_target_pairs={{0,8},{8,0},{16,24},{24,16},{1,9},{9,1},{17,25},{25,17},{2,10},{10... | collective-permute-start | bytes 589832 | tf_op jit(solution)/shard_map/ppermute | solution.py:570
  372.9 6.7 %collective-permute-start.30 = (bf16[1,16,2176]{2,1,0:T(8,128)(2,1)S(1)}, bf16[1,16,2176]{2,1,0:T(8,128)(2,1)S(1)}, u32[]{:S(2)}, u32[]{:S(2)}) collective-permute-start(bf16[1,16,2176]{2,1,0:T(8,128)(2,1)S(1)} %slice.205), channel_id=1, source_target_pairs={{0,16},{8,24},{16,0},{24,8},{1,17},{9,25},{17,1},{25,9},{2,18},{10... | collective-permute-start | bytes 208904 | tf_op jit(solution)/shard_map/ppermute | solution.py:570
  376.9 5.6 %collective-permute-start.35 = (bf16[1,96,512]{2,1,0:T(8,128)(2,1)S(1)}, bf16[1,96,512]{2,1,0:T(8,128)(2,1)S(1)}, u32[]{:S(2)}, u32[]{:S(2)}) collective-permute-start(bf16[1,96,512]{2,1,0:T(8,128)(2,1)S(1)} %slice.214), channel_id=1, source_target_pairs={{0,16},{8,24},{16,0},{24,8},{1,17},{9,25},{17,1},{25,9},{2,18},{10... | collective-permute-start | bytes 294920 | tf_op jit(solution)/shard_map/ppermute | solution.py:570
  (18 other events, 146.7 us)

commit v2 on v1

--- a/solution.py
+++ b/solution.py
@@ -11,8 +11,17 @@
 NEG = -1e30
 C0 = 0.7978845608028654
 C1 = 0.7978845608028654 * 0.044715
-PARTS = (8,)
+PARTS = (4, 4)
 R = 2
+FC = 32
+FU = 4
+RU = 2
+CH = 32
+UN = 16
+SC = 64
+SU = 4
+SD = 64
+SV = 4
 VMEM_LIMIT = 60 * 1024 * 1024
 F32 = jnp.float32
 BF16 = jnp.bfloat16
@@ -52,32 +61,27 @@
     return j
 
 
-def spread_matrix():
-    m = lax.broadcasted_iota(jnp.int32, (128, 512), 0)
-    lane = lax.broadcasted_iota(jnp.int32, (128, 512), 1)
-    return jnp.where(m == (lane >> 6) * 16 + (lane & 15), 1.0, 0.0).astype(BF16)
-
-
-def spread_rows():
-    row = lax.broadcasted_iota(jnp.int32, (16, 512), 0)
-    lane = lax.broadcasted_iota(jnp.int32, (16, 512), 1)
-    return ((lane >> 4) & 3) + 8 == row
-
-
-def kernel_a(bits, nblk, parts, sc, pack, tok, can, vec, bup, *kvs):
+def kernel_a(bits, nblk, parts, sc, own, got, tok, can, vec, bup, *kvs):
+    *kvs, pack = kvs
     me = sc[0]
-    for b in range(nblk):
-        can[b * 16 : (b + 1) * 16, :] = pack[rel(bits, me ^ b)]
-    turned = jnp.transpose(can[:, 640:768].astype(F32))
-    rows = turned[8:24]
-    vec[...] = rows
-    ex = spread_matrix()
-    pick = spread_rows()
-    width = can.shape[0]
-    for b in range(4):
-        wide = mm(rows[:, b * 128 : (b + 1) * 128].astype(BF16), ex)
-        line = jnp.sum(jnp.where(pick, wide, 0.0), axis=0, keepdims=True)
-        bup[:, b * width : (b + 1) * width] = jnp.broadcast_to(line, (8, width))
+    pack[0 : nblk // 2] = own[...]
+    pack[nblk // 2 :] = got[...]
+    lane = lax.broadcasted_iota(jnp.int32, (16, 128), 1)
+    for g in range(nblk // 8):
+        rows = jnp.zeros((16, 128), F32)
+        for i in range(8):
+            b = g * 8 + i
+            block = pack[rel(bits, me ^ b)]
+            can[b * 16 : (b + 1) * 16, 0:640] = block[:, 0:640]
+            tail = block[:, 640:768].astype(F32)
+            rows = jnp.where(lane >> 4 == i, pltpu.roll(tail, i * 16, 1) if i else tail, rows)
+            line = pltpu.roll(tail, 112 if i % 2 == 0 else 48, 1)
+            wide = line if i % 2 == 0 else jnp.where(lane >= 64, line, wide)
+            if i % 2:
+                bup[:, (b // 2) * 128 : (b // 2 + 1) * 128] = wide[0:8]
+        vec[:, g * 128 : (g + 1) * 128] = rows
+    router = jnp.concatenate([vec[8:16, :], jnp.zeros((120, vec.shape[1]), F32)], axis=0)
+    can[:, 640:768] = jnp.transpose(router).astype(BF16)
     gain = vec[0:1, :]
     shift = vec[1:2, :]
     row = 0
@@ -104,16 +108,15 @@
     u_own, u_got, d_own, d_got = take(4)
     acc_in = []
     if not first:
-        acc_in = take(6)
+        acc_in = take(5)
         take(2)
     out_ref, part_ref = take(2)
     dkvs = take(nseq)
     (vacc,) = take(1)
     if last:
-        gu_ref, gd_ref = take(2)
-        acc_up, acc_dn, acc_wo, acc_wq, acc_r = take(5)
-    else:
-        acc_up, acc_dn, acc_wo, acc_wq, acc_r = take(5)
+        gu_refs = take(2)
+        gd_refs = take(2)
+    acc_up, acc_dn, acc_wo, acc_wq = take(4)
     (
         wup,
         wdn,
@@ -141,6 +144,8 @@
         ghd,
         low1,
         gl,
+        n2_t,
+        cot_t,
         wsem,
         asem,
     ) = refs
@@ -150,12 +155,12 @@
     step = pl.program_id(0)
     tile = tok.shape[0]
     local = tile // R
-    ch = 64
+    ch = CH
     nch = tile // ch
     lane128 = lax.broadcasted_iota(jnp.int32, (ch, 128), 1)
     upper = lane128 >= 64
     half = lane128 >> 6
-    accs = (acc_up, acc_dn, acc_wo, acc_wq, acc_r, vacc)
+    accs = (acc_up, acc_dn, acc_wo, acc_wq, vacc)
 
     @pl.when(step == 0)
     def _():
@@ -199,7 +204,7 @@
         xn[sl, :] = (xhat * gain1 + shift1).astype(BF16)
         return carry
 
-    lax.fori_loop(0, nch, norm_chunk, 0)
+    lax.fori_loop(0, nch, norm_chunk, 0, unroll=UN)
     q_s[...] = mm(xn[...], can[:, 0:512])
     low1[...] = mm(xn[...], can[:, 640:768])
     for r in range(R):
@@ -234,9 +239,9 @@
         qp[r, pl.ds(local + at, ch), :] = jnp.where(upper, 0.0, f1).astype(BF16)
         return carry
 
-    lax.fori_loop(0, nch, gate_chunk, 0)
-
-    for r in range(R):
+    lax.fori_loop(0, nch, gate_chunk, 0, unroll=UN)
+
+    def attend(r, outer):
         for m in range(nseq):
             score[:, m * local : (m + 1) * local] = mmt(qp[r], kvs[m][r])
         seg_k = jnp.concatenate(
@@ -249,26 +254,30 @@
         own = seg[r, :, pl.ds(pl.multiple_of(place * local, 128), local)].astype(F32)
         inner[0:local, :] = jnp.transpose(jnp.broadcast_to(own, (128, local)))
 
-        def soft_chunk(c, carry, r=r, seg_k=seg_k):
-            at = pl.multiple_of(c * 16, 16)
-            match = inner[pl.ds(at, 16), 0:1].astype(jnp.int32) == seg_k
+        def soft_chunk(c, carry):
+            at = pl.multiple_of(c * SC, SC)
+            match = inner[pl.ds(at, SC), 0:1].astype(jnp.int32) == seg_k
             for s in range(2):
-                sl = pl.ds(pl.multiple_of(s * local + at, 16), 16)
+                sl = pl.ds(pl.multiple_of(s * local + at, SC), SC)
                 sc_ = jnp.where(match, score[sl, :], NEG)
                 num = jnp.exp(sc_ - jnp.max(sc_, axis=-1, keepdims=True))
                 total = jnp.sum(num, axis=-1, keepdims=True)
-                prob[r, sl, :] = (num / total).astype(BF16)
+                prob[r, sl, :] = (num * (1.0 / total)).astype(BF16)
             return carry
 
-        lax.fori_loop(0, local // 16, soft_chunk, 0, unroll=2)
+        lax.fori_loop(0, local // SC, soft_chunk, 0, unroll=SU)
         ctx = jnp.zeros((2 * local, 128), F32)
         for m in range(nseq):
             ctx = ctx + mm(prob[r, :, m * local : (m + 1) * local], kvs[m][r])
         up2 = lax.broadcasted_iota(jnp.int32, ctx.shape, 1) >= 64
         ctx = jnp.where(up2, ctx, 0.0)
         ctx = ctx + pltpu.roll(ctx, 64, 1)
-        cd[0, r * local : (r + 1) * local, :] = ctx[:local]
-        cd[1, r * local : (r + 1) * local, :] = ctx[local:]
+        own_rows = pl.ds(pl.multiple_of(r * local, local), local)
+        cd[0, own_rows, :] = ctx[:local]
+        cd[1, own_rows, :] = ctx[local:]
+        return outer
+
+    lax.fori_loop(0, R, attend, 0, unroll=RU)
 
     @pl.when(step == 0)
     def _():
@@ -290,7 +299,7 @@
             ).astype(BF16)
         return carry
 
-    lax.fori_loop(0, nch, mix_chunk, 0)
+    lax.fori_loop(0, nch, mix_chunk, 0, unroll=UN)
     wide1[...] = mm(mix[...], wo[...])
 
     def mid_chunk(c, carry):
@@ -303,40 +312,39 @@
         n2[sl, :] = (xhat * gain2 + shift2).astype(BF16)
         return carry
 
-    lax.fori_loop(0, nch, mid_chunk, 0)
-
-    n2_t = jnp.transpose(n2[...])
-    cot_t = jnp.transpose(cot[...])
+    lax.fori_loop(0, nch, mid_chunk, 0, unroll=UN)
+
+    n2_t[...] = jnp.transpose(n2[...])
+    cot_t[...] = jnp.transpose(cot[...])
     width = hid.shape[2]
-    for j in range(wup.shape[1] // width):
-        k = j % 2
-        js = slice(j * width, (j + 1) * width)
-        hid[k] = mm(n2[...], wup[:, js])
-        gac[k] = mmt(cot[...], wdn[js, :])
+    wide1[...] = jnp.zeros_like(wide1)
+    wide2[...] = jnp.zeros_like(wide2)
+
+    def hidden_block(j, carry):
+        js = pl.ds(pl.multiple_of(j * width, width), width)
+        hid[0] = mm(n2[...], wup[:, js])
+        gac[0] = mmt(cot[...], wdn[js, :])
         bias = bup[0:1, js]
         total = jnp.zeros((8, width), F32)
-        for c in range(tile // 32):
-            sl = slice(c * 32, (c + 1) * 32)
-            h = hid[k, sl, :] + bias
+        for c in range(tile // FC):
+            sl = slice(c * FC, (c + 1) * FC)
+            h = hid[0, sl, :] + bias
             h2 = h * h
             t = jnp.tanh(h * (C0 + C1 * h2))
             hh = 0.5 * h
-            act[k, sl, :] = (hh + hh * t).astype(BF16)
+            act[0, sl, :] = (hh + hh * t).astype(BF16)
             slope = (0.5 + 0.5 * t) + hh * (1.0 - t * t) * (C0 + (3.0 * C1) * h2)
-            g = (gac[k, sl, :] * slope).astype(BF16)
-            ghd[k, sl, :] = g
+            g = (gac[0, sl, :] * slope).astype(BF16)
+            ghd[0, sl, :] = g
             total = total + fold8(g.astype(F32))
-        vacc[(7 + j) * 8 : (8 + j) * 8, :] += total
-        o = mm(act[k], wdn[js, :])
-        g2 = mmt(ghd[k], wup[:, js])
-        if j == 0:
-            wide1[...] = o
-            wide2[...] = g2
-        else:
-            wide1[...] += o
-            wide2[...] += g2
-        acc_up[:, js] += mm(n2_t, ghd[k])
-        acc_dn[:, js] += mm(cot_t, act[k])
+        vacc[pl.ds(pl.multiple_of((7 + j) * 8, 8), 8), :] += total
+        wide1[...] += mm(act[0], wdn[js, :])
+        wide2[...] += mmt(ghd[0], wup[:, js])
+        acc_up[:, js] += mm(n2_t[...], ghd[0])
+        acc_dn[:, js] += mm(cot_t[...], act[0])
+        return carry
+
+    lax.fori_loop(0, wup.shape[1] // width, hidden_block, 0, unroll=FU)
 
     def out_chunk(c, carry):
         sl = pl.ds(pl.multiple_of(c * ch, ch), ch)
@@ -354,7 +362,7 @@
         vacc[48:56, :] += fold8(ct)
         return carry
 
-    lax.fori_loop(0, nch, out_chunk, 0)
+    lax.fori_loop(0, nch, out_chunk, 0, unroll=UN)
 
     acc_wo[...] += mm(jnp.transpose(mix[...]), n2[...])
     wide1[...] = mmt(n2[...], wo[...])
@@ -397,23 +405,25 @@
         )
         return carry
 
-    lax.fori_loop(0, nch, gate_back_chunk, 0)
-
-    for r in range(R):
+    lax.fori_loop(0, nch, gate_back_chunk, 0, unroll=UN)
+
+    width = hid.shape[2]
+
+    def attend_back(r, outer):
         for m in range(nseq):
             score[:, m * local : (m + 1) * local] = mmt(dp[r], kvs[m][r])
         dsc = act
 
-        def score_chunk(c, carry, r=r):
-            at = pl.multiple_of(c * 16, 16)
-            sl = pl.ds(at, 16)
-            inn = inner[pl.ds(pl.multiple_of(r * 2 * local + at, 16), 16), 0:1]
+        def score_chunk(c, carry):
+            at = pl.multiple_of(c * SD, SD)
+            sl = pl.ds(at, SD)
+            inn = inner[pl.ds(pl.multiple_of(r * 2 * local + at, SD), SD), 0:1]
             for k in range(2):
                 ks = slice(k * width, (k + 1) * width)
                 dsc[k, sl, :] = (prob[r, sl, ks].astype(F32) * (score[sl, ks] - inn)).astype(BF16)
             return carry
 
-        lax.fori_loop(0, 2 * local // 16, score_chunk, 0, unroll=2)
+        lax.fori_loop(0, 2 * local // SD, score_chunk, 0, unroll=SV)
         q_t = jnp.transpose(qp[r])
         d_t = jnp.transpose(dp[r])
         dq = jnp.zeros((2 * local, 128), F32)
@@ -427,8 +437,12 @@
         up2 = lax.broadcasted_iota(jnp.int32, dq.shape, 1) >= 64
         dq = jnp.where(up2, 0.0, dq) * 0.125
         dq = dq + pltpu.roll(dq, 64, 1)
-        cd[0, r * local : (r + 1) * local, :] = dq[:local]
-        cd[1, r * local : (r + 1) * local, :] = dq[local:]
+        own_rows = pl.ds(pl.multiple_of(r * local, local), local)
+        cd[0, own_rows, :] = dq[:local]
+        cd[1, own_rows, :] = dq[local:]
+        return outer
+
+    lax.fori_loop(0, R, attend_back, 0, unroll=RU)
 
     def query_chunk(c, carry):
         sl = pl.ds(pl.multiple_of(c * ch, ch), ch)
@@ -444,10 +458,10 @@
             vacc[16:24, b * 128 : (b + 1) * 128] += fold8(low.astype(F32))
         return carry
 
-    lax.fori_loop(0, nch, query_chunk, 0)
+    lax.fori_loop(0, nch, query_chunk, 0, unroll=UN)
     xn_t = jnp.transpose(xn[...])
     acc_wq[...] += mm(xn_t, mix[...])
-    acc_r[...] += mm(xn_t, gl[...])
+    vacc[88:104, :] += mm(jnp.transpose(gl[...])[0:16], xn[...])
     wide1[...] = mmt(mix[...], can[:, 0:512]) + mmt(gl[...], can[:, 640:768])
 
     def part_chunk(c, carry):
@@ -459,24 +473,25 @@
         vacc[8:16, :] += fold8(g)
         return carry
 
-    lax.fori_loop(0, nch, part_chunk, 0)
+    lax.fori_loop(0, nch, part_chunk, 0, unroll=UN)
 
     if last:
 
         @pl.when(step == steps - 1)
         def _():
-            for b in range(nblk):
-                j = rel(gbits_u, me ^ b)
-                rows = slice(b * 16, (b + 1) * 16)
-                gu_ref[j, :, 0:2048] = acc_up[rows, :].astype(BF16)
-                gu_ref[j, :, 2048:2176] = acc_r[rows, :].astype(BF16)
-                j = rel(gbits_d, me ^ b)
-                gd_ref[j, 64:80, :] = acc_wo[rows, :].astype(BF16)
-                gd_ref[j, 80:96, :] = acc_wq[rows, :].astype(BF16)
-            for c in range(nblk // 2):
-                both = jnp.transpose(acc_dn[:, c * 128 : (c + 1) * 128]).astype(BF16)
-                gd_ref[rel(gbits_d, me ^ (2 * c)), 0:64, :] = both[:64]
-                gd_ref[rel(gbits_d, me ^ (2 * c + 1)), 0:64, :] = both[64:]
+            for c in range(wdn.shape[0] // 128):
+                cs = slice(c * 128, (c + 1) * 128)
+                wdn[cs, :] = jnp.transpose(acc_dn[:, cs].astype(BF16))
+            for j in range(nblk):
+                h, i = j // (nblk // 2), j % (nblk // 2)
+                b = me ^ sum((j >> dst & 1) << src for src, dst in gbits_u)
+                rows = pl.ds(pl.multiple_of(b * 16, 16), 16)
+                gu_refs[h][i, :, 0:2048] = acc_up[rows, :].astype(BF16)
+                gu_refs[h][i, :, 2048:2560] = acc_wq[rows, :].astype(BF16)
+                b = me ^ sum((j >> dst & 1) << src for src, dst in gbits_d)
+                gd_refs[h][i, 0:64, :] = wdn[pl.ds(pl.multiple_of(b * 64, 64), 64), :]
+                rows = pl.ds(pl.multiple_of(b * 16, 16), 16)
+                gd_refs[h][i, 64:80, :] = acc_wo[rows, :].astype(BF16)
 
 
 def kernel_e(cfg, *refs):
@@ -497,14 +512,14 @@
         take(1)
     (out_ref,) = take(1)
     if last:
-        (gs_ref,) = take(1)
+        gs_refs = take(2)
     acc_kv, acc_l = take(2)
-    wide, xh, xn, dk = refs
+    wide, xn, dk, small = refs
     me = sc[0]
     step = pl.program_id(0)
     tile = tok.shape[0]
     local = tile // R
-    ch = 64
+    ch = CH
     nch = tile // ch
     gain = vec[0:1, :]
     shift = vec[1:2, :]
@@ -535,7 +550,7 @@
         acc_l[8:16, :] += fold8(g)
         return carry
 
-    lax.fori_loop(0, nch, chunk, 0)
+    lax.fori_loop(0, nch, chunk, 0, unroll=UN)
     acc_kv[...] += mm(jnp.transpose(xn[...]), dk[...])
 
     if last:
@@ -549,20 +564,31 @@
                 if v < 2:
                     line = line + acc_l[v * 8 : (v + 1) * 8, :]
                 table = jnp.where(row == v, jnp.sum(line, axis=0, keepdims=True), table)
-            ex = spread_matrix()
-            pick = spread_rows()
-            ups = []
-            for b in range(4):
-                line = jnp.sum(vacc[(7 + b) * 8 : (8 + b) * 8, :], axis=0, keepdims=True)
-                ups.append(mmt(jnp.where(pick, line, 0.0).astype(BF16), ex))
-            table = table + jnp.concatenate(ups, axis=1)
-            table = jnp.concatenate([table, jnp.zeros((112, 512), F32)], axis=0)
-            cols = jnp.transpose(table)
+            router = vacc[88:104, :][0:8]
+            table = table + jnp.concatenate([jnp.zeros((8, 512), F32), router], axis=0)
+            ups = [
+                jnp.sum(vacc[(7 + b) * 8 : (8 + b) * 8, :], axis=0, keepdims=True)
+                for b in range(4)
+            ]
+            lane = lax.broadcasted_iota(jnp.int32, (16, 128), 1)
+            first_row = lax.broadcasted_iota(jnp.int32, (16, 128), 0) == 0
             for b in range(nblk):
-                j = rel(gbits, me ^ b)
-                rows = slice(b * 16, (b + 1) * 16)
-                gs_ref[j, :, 0:128] = acc_kv[rows, :].astype(BF16)
-                gs_ref[j, :, 128:256] = cols[rows, :].astype(BF16)
+                g, i = b // 8, b % 8
+                rows = table[:, g * 128 : (g + 1) * 128]
+                if i:
+                    rows = pltpu.roll(rows, 128 - i * 16, 1)
+                c = b * 64 // 512
+                at = (b * 64 % 512) // 128 * 128
+                line = jnp.broadcast_to(ups[c][:, at : at + 128], (16, 128))
+                line = pltpu.roll(line, 16 if b % 2 == 0 else 80, 1)
+                tail = jnp.where(
+                    lane < 16, rows, jnp.where(first_row & (lane < 80), line, 0.0)
+                )
+                small[b] = jnp.concatenate([acc_kv[b * 16 : (b + 1) * 16, :], tail], axis=1).astype(BF16)
+            for j in range(nblk):
+                h, i = j // (nblk // 2), j % (nblk // 2)
+                b = me ^ sum((j >> dst & 1) << src for src, dst in gbits)
+                gs_refs[h][i] = small[b]
 
 
 def swap(x, hop, sizes):
@@ -576,19 +602,145 @@
     return x, swap(x, order[-1], sizes)
 
 
-def narrow(x, order, sizes):
-    for n, hop in enumerate(order):
-        h = x.shape[0] // 2
-        got = swap(x[h:], hop, sizes)
-        x = x[:h].astype(F32) + got.astype(F32)
-        if n < len(order) - 1:
-            x = x.astype(BF16)
-    return x[0]
+def after(x, *deps):
+    return lax.optimization_barrier((x,) + deps)[0]
+
+
+def narrow_step(pair, hop, sizes):
+    low, high = pair
+    got = swap(high, hop, sizes)
+    h = low.shape[0] // 2
+
+    def add(sl):
+        return low[sl].astype(F32) + got[sl].astype(F32)
+
+    if h == 0:
+        return add(slice(None))
+    return add(slice(0, h)).astype(BF16), add(slice(h, 2 * h)).astype(BF16)
 
 
 def whole(shape):
     zeros = (0,) * len(shape)
     return pl.BlockSpec(shape, lambda i: zeros, pipeline_mode=pl.Buffered(1))
+
+
+def layer_calls(
+    sc, tok, cot, idx, seg, kv_all, can, vec, bup, u_own, u_got, d_own, d_got,
+    bits_u, bits_d, gbits_u, gbits_d, nblk, nseq, parts, moved=lambda dkv: None,
+):
+    d, ff, local = tok.shape[1], bup.shape[1], idx.shape[2]
+    flat = tok.shape
+    tile = R * local
+    smem = pl.BlockSpec(memory_space=pltpu.SMEM)
+    anywhere = pl.BlockSpec(memory_space=pl.ANY)
+    params = pltpu.CompilerParams(vmem_limit_bytes=VMEM_LIMIT)
+    shape = jax.ShapeDtypeStruct
+    acc_shapes = (
+        shape((d, ff), F32),
+        shape((d, ff), F32),
+        shape((d, d), F32),
+        shape((d, d), F32),
+    )
+    vacc_shape = shape((104, d), F32)
+    row0 = 0
+    acc = None
+    out = part = vacc = None
+    for p, count in enumerate(parts):
+        first, last = p == 0, p == len(parts) - 1
+        steps = count // R
+        base = row0 // R
+        rowspec = pl.BlockSpec((tile, d), lambda i, base=base: (base + i, 0))
+        kvspec = pl.BlockSpec((R, local, 128), lambda i: (i, 0, 0))
+        ins = [sc, tok, cot, idx, seg] + kv_all[p] + [can, vec, bup, u_own, u_got, d_own, d_got]
+        specs = [
+            smem,
+            rowspec,
+            rowspec,
+            pl.BlockSpec((R, 2, local), lambda i, base=base: (base + i, 0, 0)),
+            pl.BlockSpec((R, 1, local * nseq), lambda i, base=base: (base + i, 0, 0)),
+        ]
+        specs += [kvspec] * nseq
+        specs += [whole(can.shape), whole(vec.shape), whole(bup.shape)] + [anywhere] * 4
+        alias = {}
+        if not first:
+            ins += list(acc) + [vacc, out, part]
+            specs += [anywhere] * 7
+            alias = {len(ins) - 2: 0, len(ins) - 1: 1}
+        outs = [shape(flat, BF16), shape(flat, F32)]
+        outs += [shape((count, local, 128), BF16)] * nseq + [vacc_shape]
+        ospecs = [rowspec, rowspec] + [kvspec] * nseq + [whole(vacc_shape.shape)]
+        scratch = []
+        if last:
+            sh_u, sh_d = (nblk // 2, 16, ff + d), (nblk // 2, 80, d)
+            outs += [shape(sh_u, BF16)] * 2 + [shape(sh_d, BF16)] * 2
+            ospecs += [whole(sh_u)] * 2 + [whole(sh_d)] * 2
+            scratch += [pltpu.VMEM(a.shape, F32) for a in acc_shapes]
+        else:
+            outs += list(acc_shapes)
+            ospecs += [whole(a.shape) for a in acc_shapes]
+        wide = (tile, d)
+        scratch += [
+            pltpu.VMEM((d, ff), BF16),
+            pltpu.VMEM((ff, d), BF16),
+            pltpu.VMEM((d, d), BF16),
+            pltpu.VMEM(wide, BF16),
+            pltpu.VMEM(wide, F32),
+            pltpu.VMEM((R, 2 * local, 128), BF16),
+            pltpu.VMEM((R, 2 * local, 128), BF16),
+            pltpu.VMEM((2, tile, 128), jnp.int32),
+            pltpu.VMEM((2, tile, 128), F32),
+            pltpu.VMEM((2, tile, 128), F32),
+            pltpu.VMEM((2 * tile, 128), F32),
+            pltpu.VMEM((R, 2 * local, nseq * local), BF16),
+            pltpu.VMEM((2 * local, nseq * local), F32),
+            pltpu.VMEM(wide, F32),
+            pltpu.VMEM(wide, F32),
+            pltpu.VMEM(wide, F32),
+            pltpu.VMEM(wide, F32),
+            pltpu.VMEM((tile, 128), F32),
+            pltpu.VMEM(wide, BF16),
+            pltpu.VMEM(wide, BF16),
+            pltpu.VMEM((2, tile, 512), F32),
+            pltpu.VMEM((2, tile, 512), F32),
+            pltpu.VMEM((2, tile, 512), BF16),
+            pltpu.VMEM((2, tile, 512), BF16),
+            pltpu.VMEM((tile, 128), F32),
+            pltpu.VMEM((tile, 128), BF16),
+            pltpu.VMEM((d, tile), BF16),
+            pltpu.VMEM((d, tile), BF16),
+            pltpu.SemaphoreType.DMA((3,)),
+            pltpu.SemaphoreType.DMA((6,)),
+        ]
+        cfg = (
+            first,
+            last,
+            steps,
+            bits_u,
+            bits_d,
+            gbits_u,
+            gbits_d,
+            nblk,
+            nseq,
+        )
+        got = pl.pallas_call(
+            functools.partial(kernel_b, cfg),
+            grid=(steps,),
+            out_shape=tuple(outs),
+            in_specs=specs,
+            out_specs=tuple(ospecs),
+            scratch_shapes=scratch,
+            input_output_aliases=alias,
+            compiler_params=params,
+            name="layer",
+        )(*ins)
+        out, part = got[0], got[1]
+        dkv = got[2 : 2 + nseq]
+        moved(dkv)
+        vacc = got[2 + nseq]
+        acc = got[3 + nseq :]
+        row0 += count
+
+    return out, part, vacc, acc
 
 
 def body(
@@ -660,25 +812,39 @@
         return out
 
     order_a = zz[::-1] + xy + [core]
-    order_u = weave(zz[::-1], xy) + [core]
-    order_d = weave(xy, zz[::-1]) + [core]
+    order_u = zz[::-1] + xy + [core]
+    order_d = zz[::-1] + xy[::-1] + [core]
     back_u = [core] + xy[::-1] + zz
     back_d = [core] + xy + zz
     back_s = [core] + xy[::-1] + zz
 
-    cols = [near(v)[:, None] for v in (ln1_gain, ln1_bias, b_query, b_out, ln2_gain, ln2_bias, b_down)]
-    bu = jnp.transpose(near(b_up).reshape(-1, 16))
-    pad0 = jnp.zeros((16, 1), BF16)
-    pad1 = jnp.zeros((16, 128 - 20), BF16)
-    pack = jnp.concatenate(
-        [near(w_query), near(w_keyval), near(w_router)] + cols + [pad0, bu, pad1], axis=1
-    )[None]
-    own, got = widen(pack, order_a, sizes)
-    pack = jnp.concatenate([own, got], axis=0)
-    u_own, u_got = widen(near(w_up)[None], order_u, sizes)
-    d_own, d_got = widen(
-        jnp.concatenate([near(w_down), near(w_out)], axis=0)[None], order_d, sizes
+    def grow(x, hop):
+        return jnp.concatenate([x, swap(x, hop, sizes)], axis=0)
+
+    table = jnp.concatenate(
+        [
+            near(v)[None]
+            for v in (ln1_gain, ln1_bias, b_query, b_out, ln2_gain, ln2_bias, b_down, b_down)
+        ]
+        + [jnp.transpose(near(w_router))],
+        axis=0,
     )
+    tail = lax.pad(near(b_up)[None], jnp.zeros((), BF16), ((0, 15, 0), (0, 48, 0)))
+    pack = jnp.concatenate([near(w_query), near(w_keyval), table, tail], axis=1)[None]
+    u = near(w_up)[None]
+    dn = jnp.concatenate([near(w_down), near(w_out)], axis=0)[None]
+    nz = len(zz)
+    for n in range(nz):
+        pack = grow(pack, order_a[n])
+        u = grow(u, order_u[n])
+        dn = grow(dn, order_d[n])
+    for hop in order_a[nz:-1]:
+        pack = grow(pack, hop)
+    u = after(u, pack)
+    dn = after(dn, pack)
+    u = grow(u, order_u[nz])
+    dn = grow(dn, order_d[nz])
+    packs = [pack, swap(pack, core, sizes)]
 
     smem = pl.BlockSpec(memory_space=pltpu.SMEM)
     anywhere = pl.BlockSpec(memory_space=pl.ANY)
@@ -693,11 +859,12 @@
             shape((8, ff), F32),
         )
         + tuple(shape((n, local, 128), BF16) for n in PARTS),
-        in_specs=[smem, pl.BlockSpec(memory_space=pltpu.VMEM), pl.BlockSpec(memory_space=pltpu.VMEM)],
+        in_specs=[smem] + [pl.BlockSpec(memory_space=pltpu.VMEM)] * 3,
         out_specs=tuple(pl.BlockSpec(memory_space=pltpu.VMEM) for unused in range(3 + len(PARTS))),
+        scratch_shapes=[pltpu.VMEM((nblk, 16, 768), BF16)],
         compiler_params=params,
         name="project",
-    )(sc, pack, tokens)
+    )(sc, *packs, tokens)
 
     flat = (rows_dev * local, d)
     tok = tokens.reshape(flat)
@@ -706,118 +873,39 @@
     seg = segments[:, None, :]
     tile = R * local
 
-    kv_all = [
-        [kv] + [swap(kv, ("seq", m), sizes) for m in range(1, nseq)] for kv in kv_parts
-    ]
-    acc_shapes = (
-        shape((d, ff), F32),
-        shape((d, ff), F32),
-        shape((d, d), F32),
-        shape((d, d), F32),
-        shape((d, 128), F32),
+    kv_all = []
+
+    def gather_kv(kv):
+        kv_all.append([kv] + [swap(kv, ("seq", m), sizes) for m in range(1, nseq)])
+
+    gather_kv(kv_parts[0])
+    u = after(u, can)
+    dn = after(dn, can)
+    for n in range(nz + 1, len(order_u) - 1):
+        u = grow(u, order_u[n])
+        dn = grow(dn, order_d[n])
+    u = after(u, *kv_all[0])
+    dn = after(dn, *kv_all[0])
+    us = [u, swap(u, core, sizes)]
+    ds = [dn, swap(dn, core, sizes)]
+    for kv in kv_parts[1:]:
+        gather_kv(after(kv, *kv_all[-1]))
+    dkv_all = []
+
+    def moved(dkv):
+        dkv_all.append([dkv[0]] + [swap(dkv[m], ("seq", m), sizes) for m in range(1, nseq)])
+
+    out, part, vacc, acc = layer_calls(
+        sc, tok, cot, idx, seg, kv_all, can, vec, bup, *us, *ds,
+        gather_bits(order_u), gather_bits(order_d), scatter_bits(back_u), scatter_bits(back_d),
+        nblk, nseq, PARTS, moved,
     )
-    vacc_shape = shape((88, d), F32)
-    row0 = 0
-    acc = None
-    out = part = vacc = None
-    dkv_all = []
-    for p, count in enumerate(PARTS):
-        first, last = p == 0, p == len(PARTS) - 1
-        steps = count // R
-        base = row0 // R
-        rowspec = pl.BlockSpec((tile, d), lambda i, base=base: (base + i, 0))
-        kvspec = pl.BlockSpec((R, local, 128), lambda i: (i, 0, 0))
-        ins = [sc, tok, cot, idx, seg] + kv_all[p] + [can, vec, bup, u_own, u_got, d_own, d_got]
-        specs = [
-            smem,
-            rowspec,
-            rowspec,
-            pl.BlockSpec((R, 2, local), lambda i, base=base: (base + i, 0, 0)),
-            pl.BlockSpec((R, 1, local * nseq), lambda i, base=base: (base + i, 0, 0)),
-        ]
-        specs += [kvspec] * nseq
-        specs += [whole(can.shape), whole(vec.shape), whole(bup.shape)] + [anywhere] * 4
-        alias = {}
-        if not first:
-            ins += list(acc) + [vacc, out, part]
-            specs += [anywhere] * 8
-            alias = {len(ins) - 2: 0, len(ins) - 1: 1}
-        outs = [shape(flat, BF16), shape(flat, F32)]
-        outs += [shape((count, local, 128), BF16)] * nseq + [vacc_shape]
-        ospecs = [rowspec, rowspec] + [kvspec] * nseq + [whole(vacc_shape.shape)]
-        scratch = []
-        if last:
-            outs += [shape((nblk, 16, ff + 128), BF16), shape((nblk, 96, d), BF16)]
-            ospecs += [whole((nblk, 16, ff + 128)), whole((nblk, 96, d))]
-            scratch += [pltpu.VMEM(a.shape, F32) for a in acc_shapes]
-        else:
-            outs += list(acc_shapes)
-            ospecs += [whole(a.shape) for a in acc_shapes]
-        wide = (tile, d)
-        scratch += [
-            pltpu.VMEM((d, ff), BF16),
-            pltpu.VMEM((ff, d), BF16),
-            pltpu.VMEM((d, d), BF16),
-            pltpu.VMEM(wide, BF16),
-            pltpu.VMEM(wide, F32),
-            pltpu.VMEM((R, 2 * local, 128), BF16),
-            pltpu.VMEM((R, 2 * local, 128), BF16),
-            pltpu.VMEM((2, tile, 128), jnp.int32),
-            pltpu.VMEM((2, tile, 128), F32),
-            pltpu.VMEM((2, tile, 128), F32),
-            pltpu.VMEM((2 * tile, 128), F32),
-            pltpu.VMEM((R, 2 * local, nseq * local), BF16),
-            pltpu.VMEM((2 * local, nseq * local), F32),
-            pltpu.VMEM(wide, F32),
-            pltpu.VMEM(wide, F32),
-            pltpu.VMEM(wide, F32),
-            pltpu.VMEM(wide, F32),
-            pltpu.VMEM((tile, 128), F32),
-            pltpu.VMEM(wide, BF16),
-            pltpu.VMEM(wide, BF16),
-            pltpu.VMEM((2, tile, 512), F32),
-            pltpu.VMEM((2, tile, 512), F32),
-            pltpu.VMEM((2, tile, 512), BF16),
-            pltpu.VMEM((2, tile, 512), BF16),
-            pltpu.VMEM((tile, 128), F32),
-            pltpu.VMEM((tile, 128), BF16),
-            pltpu.SemaphoreType.DMA((3,)),
-            pltpu.SemaphoreType.DMA((6,)),
-        ]
-        cfg = (
-            first,
-            last,
-            steps,
-            gather_bits(order_u),
-            gather_bits(order_d),
-            scatter_bits(back_u),
-            scatter_bits(back_d),
-            nblk,
-            nseq,
-        )
-        got = pl.pallas_call(
-            functools.partial(kernel_b, cfg),
-            grid=(steps,),
-            out_shape=tuple(outs),
-            in_specs=specs,
-            out_specs=tuple(ospecs),
-            scratch_shapes=scratch,
-            input_output_aliases=alias,
-            compiler_params=params,
-            name="layer",
-        )(*ins)
-        out, part = got[0], got[1]
-        dkv = got[2 : 2 + nseq]
-        dkv_all.append(
-            [dkv[0]] + [swap(dkv[m], ("seq", m), sizes) for m in range(1, nseq)]
-        )
-        vacc = got[2 + nseq]
-        acc = got[3 + nseq :]
-        row0 += count
-
-    gu, gd = acc
-    gu = narrow(gu, back_u, sizes)
-    gd = narrow(gd, back_d, sizes)
+    gu, gd = acc[0:2], acc[2:4]
+    for n in range(len(PARTS) - 1):
+        dkv_all[n] = [sum(v.astype(F32) for v in dkv_all[n]).astype(BF16)]
+        gu, gd, dkv_all[n] = lax.optimization_barrier((gu, gd, dkv_all[n]))
+    gu = narrow_step(gu, back_u[0], sizes)
+    gd = narrow_step(gd, back_d[0], sizes)
 
     row0 = 0
     grad = None
@@ -828,8 +916,12 @@
         base = row0 // R
         rowspec = pl.BlockSpec((tile, d), lambda i, base=base: (base + i, 0))
         kvspec = pl.BlockSpec((R, local, 128), lambda i: (i, 0, 0))
-        ins = [sc, part, tok] + dkv_all[p] + [can, vec, vacc]
-        specs = [smem, rowspec, rowspec] + [kvspec] * nseq
+        if last:
+            gu = narrow_step(gu, back_u[1], sizes)
+            gd = narrow_step(gd, back_d[1], sizes)
+        part = after(part, gu, gd)
+        ins = [sc, part, tok] + list(dkv_all[p]) + [can, vec, vacc]
+        specs = [smem, rowspec, rowspec] + [kvspec] * len(dkv_all[p])
         specs += [whole(can.shape), whole(vec.shape), whole(vacc.shape)]
         alias = {}
         if not first:
@@ -840,19 +932,19 @@
         ospecs = [rowspec]
         scratch = []
         if last:
-            outs += [shape((nblk, 16, 256), BF16)]
-            ospecs += [whole((nblk, 16, 256))]
+            outs += [shape((nblk // 2, 16, 256), BF16)] * 2
+            ospecs += [whole((nblk // 2, 16, 256))] * 2
             scratch += [pltpu.VMEM((d, 128), F32), pltpu.VMEM((16, d), F32)]
         else:
             outs += [shape((d, 128), F32), shape((16, d), F32)]
             ospecs += [whole((d, 128)), whole((16, d))]
         scratch += [
             pltpu.VMEM((tile, d), F32),
-            pltpu.VMEM((8, 128), F32),
             pltpu.VMEM((tile, d), BF16),
             pltpu.VMEM((tile, 128), BF16),
+            pltpu.VMEM((nblk, 16, 256), BF16),
         ]
-        cfg = (first, last, steps, scatter_bits(back_s), nblk, nseq)
+        cfg = (first, last, steps, scatter_bits(back_s), nblk, len(dkv_all[p]))
         got = pl.pallas_call(
             functools.partial(kernel_e, cfg),
             grid=(steps,),
@@ -867,19 +959,25 @@
         grad = got[0]
         eacc = got[1:]
         row0 += count
-    gs = narrow(eacc[0], back_s, sizes)
+    gs = eacc
+    for n in range(len(back_s)):
+        gs = narrow_step(gs, back_s[n], sizes)
+        if n + 2 < len(back_u):
+            gu = narrow_step(gu, back_u[n + 2], sizes)
+            gd = narrow_step(gd, back_d[n + 2], sizes)
+        gs, gu, gd = lax.optimization_barrier((gs, gu, gd))
+    gs, gu, gd = gs[0], gu[0], gd[0]
 
     def vector(v):
-        return near_sum(gs[:, 128 + v])
-
-    grad_b_up = near_sum(jnp.transpose(gs[:, 136:140]).reshape(-1))
+        return near_sum(gs[v, 128:144])
+
     return (
         out.reshape(tokens.shape),
         grad.reshape(tokens.shape),
         vector(0),
         vector(1),
-        near_sum(gu[:, ff : ff + experts]),
-        near_sum(gd[80:96]),
+        near_sum(jnp.transpose(gs[8 : 8 + experts, 128:144])),
+        near_sum(gu[:, ff:]),
         vector(2),
         near_sum(gs[:, :128]),
         near_sum(gd[64:80]),
@@ -887,7 +985,7 @@
         vector(4),
         vector(5),
         near_sum(gu[:, :ff]),
-        grad_b_up,
+        near_sum(gs[0, 144:208]),
         near_sum(gd[:64]),
         vector(6),
     )

time: 385 us -> 264 us (0.69)
  waiting for transfers between devices: 134 us -> 78.4 us
  Pallas kernels: 159 us -> 115 us
  local copies, waits for them, and re-layouts: 27.9 us -> 11.3 us
    ppermute x36 -> x42, waiting for transfers between devices: 134 us -> 78.4 us  [swap(): return lax.ppermute(x, axis, [(i, i ^ mask) for i in range(sizes[axis])])]
    pallas_call x1 -> x2, Pallas kernels: 138 us -> 100 us  [layer_calls(): pl.pallas_call(functools.partial(kernel_b, cfg), grid=(steps,), out_shape...]
    unnamed x41 -> x35, local copies, waits for them, and re-layouts: 11.2 us -> 4.3 us
    pallas_call x1 -> x2, Pallas kernels: 15.8 us -> 10.1 us  [body(): pl.pallas_call(functools.partial(kernel_e, cfg), grid=(steps,), out_shape...]
    broadcast_in_dim x8 -> x0, local copies, waits for them, and re-layouts: 5.22 us -> none  [the longest x7 5.21 us: body(): near(v)[:, None]]
    ppermute x36 -> x42, starting transfers between devices: 54.3 us -> 51.5 us  [swap(): return lax.ppermute(x, axis, [(i, i ^ mask) for i in range(sizes[axis])])]
  transfers between devices with their start and end apart: 36 -> 42, of which waited for: 20 -> 20; matrix products, arithmetic and copies ran while one was open for 6% -> 2% of each run, Pallas kernels for 1% -> 41%
where the time goes in v2:
time: 264 us; the launch traced here: 266 us
  Pallas kernels  115 us (44%)
  waiting for transfers between devices  78.4 us (30%)
  starting transfers between devices  51.5 us (20%)
  local copies, waits for them, and re-layouts  11.3 us (4%)
  other arithmetic  7.72 us (3%)
    pallas_call x2, Pallas kernels, layer_calls(): pl.pallas_call(functools.partial(kernel_b, cfg), grid=(steps,), out_shape...  100 us
    ppermute x42, waiting for transfers between devices, swap(): return lax.ppermute(x, axis, [(i, i ^ mask) for i in range(sizes[axis])])  78.4 us
    ppermute x42, starting transfers between devices, swap(): return lax.ppermute(x, axis, [(i, i ^ mask) for i in range(sizes[axis])])  51.5 us
    pallas_call x2, Pallas kernels, body(): pl.pallas_call(functools.partial(kernel_e, cfg), grid=(steps,), out_shape...  10.1 us
  transfers between devices with their start and end apart: 42, of which 20 were waited for; matrix products, arithmetic and copies ran while one was open for 2% of the time, Pallas kernels for 41%

profile of v2, /device:TPU:0, one launch (start us, length us, event | category | flops | bytes accessed | tf_op | source)
XLA Modules:
  0.0 265.6 jit_solution(16293799511981454476)
XLA Ops:
  3.0 4.0 %collective-permute-start = (bf16[1,16,768]{2,1,0:T(8,128)(2,1)S(1)}, bf16[1,16,768]{2,1,0:T(8,128)(2,1)S(1)}, u32[]{:S(2)}, u32[]{:S(2)}) collective-permute-start(bf16[1,16,768]{2,1,0:T(8,128)(2,1)S(1)} %get-tuple-element.157), channel_id=1, source_target_pairs={{0,16},{8,24},{16,0},{24,8},{1,17},{9,25},{17,1},{25,9},{2,18},{10... | collective-permute-start | bytes 73736 | tf_op jit(solution)/shard_map/ppermute | solution.py:596
  7.9 2.9 %collective-permute-start.11 = (bf16[1,16,2048]{2,1,0:T(8,128)(2,1)}, bf16[1,16,2048]{2,1,0:T(8,128)(2,1)S(1)}, u32[]{:S(2)}, u32[]{:S(2)}) collective-permute-start(bf16[1,16,2048]{2,1,0:T(8,128)(2,1)} %bitcast.56), channel_id=1, source_target_pairs={{0,16},{8,24},{16,0},{24,8},{1,17},{9,25},{17,1},{25,9},{2,18},{10... | collective-permute-start | bytes 196616 | tf_op jit(solution)/shard_map/ppermute | solution.py:596
  10.8 1.6 collective-permute-start.1
  12.5 4.8 %collective-permute-done.11 = bf16[1,16,2048]{2,1,0:T(8,128)(2,1)S(1)} collective-permute-done((bf16[1,16,2048]{2,1,0:T(8,128)(2,1)}, bf16[1,16,2048]{2,1,0:T(8,128)(2,1)S(1)}, u32[]{:S(2)}, u32[]{:S(2)}) %collective-permute-start.11) | collective-permute-done | bytes 65568 | tf_op jit(solution)/shard_map/ppermute | solution.py:596
  19.8 2.1 collective-permute-start.17
  26.1 2.6 collective-permute-done.3
  32.5 6.4 %collective-permute-done.18 = bf16[4,80,512]{2,1,0:T(8,128)(2,1)S(1)} collective-permute-done((bf16[4,80,512]{2,1,0:T(8,128)(2,1)S(1)}, bf16[4,80,512]{2,1,0:T(8,128)(2,1)S(1)}, u32[]{:S(2)}, u32[]{:S(2)}) %collective-permute-start.18) | collective-permute-done | bytes 327712 | tf_op jit(solution)/shard_map/ppermute | solution.py:596
  39.7 4.8 %project.1 = (bf16[512,768]{1,0:T(8,128)(2,1)}, f32[16,512]{1,0:T(8,128)}, f32[8,2048]{1,0:T(8,128)}, bf16[4,256,128]{2,1,0:T(8,128)(2,1)}, bf16[4,256,128]{2,1,0:T(8,128)(2,1)}) custom-call(s32[2]{0:T(128)} %pad_add_fusion.sc.refs_0_, bf16[16,16,768]{2,1,0:T(8,128)(2,1)} %copy-done.6, bf16[16,16,768]{2,1,0:T(8,128)(2,1)} %copy-done.7, bf16[8,256,512]{2,1,0:T(8,128)(2,1)} %tok.1), custom_call_target="tpu_custom_call" | custom-call | tf_op jit(solution)/shard_map/project/pallas_call | solution.py:854
  47.6 2.0 collective-permute-start.5
  50.1 1.9 collective-permute-start.7
  52.0 8.8 %collective-permute-done.19 = bf16[8,80,512]{2,1,0:T(8,128)(2,1)S(1)} collective-permute-done((bf16[8,80,512]{2,1,0:T(8,128)(2,1)S(1)}, bf16[8,80,512]{2,1,0:T(8,128)(2,1)S(1)}, u32[]{:S(2)}, u32[]{:S(2)}) %collective-permute-start.19) | collective-permute-done | bytes 655392 | tf_op jit(solution)/shard_map/ppermute | solution.py:596
  61.0 10.2 %collective-permute-done.6.refs_7_ = bf16[4,256,128]{2,1,0:T(8,128)(2,1)S(1)} collective-permute-done((bf16[4,256,128]{2,1,0:T(8,128)(2,1)}, bf16[4,256,128]{2,1,0:T(8,128)(2,1)S(1)}, u32[]{:S(2)}, u32[]{:S(2)}) %collective-permute-start.6) | collective-permute-done | bytes 262176 | tf_op jit(solution)/shard_map/ppermute | solution.py:596
  72.7 1.8 collective-permute-start.10
  75.1 2.5 collective-permute-start.8
  80.2 43.0 %layer.2 = (bf16[2048,512]{1,0:T(8,128)(2,1)}, f32[2048,512]{1,0:T(8,128)}, bf16[4,256,128]{2,1,0:T(8,128)(2,1)}, bf16[4,256,128]{2,1,0:T(8,128)(2,1)}, bf16[4,2...) custom-call(s32[2]{0:T(128)} %pad_add_fusion.sc.refs_0_, ...), custom_call_target="tpu_custom_call" | custom-call | tf_op jit(solution)/shard_map/layer/pallas_call | solution.py:725
  123.2 2.1 collective-permute-start.21
  125.7 2.1 collective-permute-start.23
  127.8 57.4 %layer.3 = (bf16[2048,512]{1,0:T(8,128)(2,1)}, f32[2048,512]{1,0:T(8,128)}, bf16[4,256,128]{2,1,0:T(8,128)(2,1)}, bf16[4,256,128]{2,1,0:T(8,128)(2,1)}, bf16[4,2...) custom-call(s32[2]{0:T(128)} %pad_add_fusion.sc.refs_0_, ...), custom_call_target="tpu_custom_call", output_to_operand_aliasing={{0}: (21, {}), {1}: (22, {})} | custom-call | tf_op jit(solution)/shard_map/layer/pallas_call | solution.py:725
  186.7 2.7 %collective-permute-done.24 = bf16[16,16,2560]{2,1,0:T(8,128)(2,1)S(1)} collective-permute-done((bf16[16,16,2560]{2,1,0:T(8,128)(2,1)}, bf16[16,16,2560]{2,1,0:T(8,128)(2,1)S(1)}, u32[]{:S(2)}, u32[]{:S(2)}) %collective-permute-start.24) | collective-permute-done | bytes 1310752 | tf_op jit(solution)/shard_map/ppermute | solution.py:596
  192.7 2.1 collective-permute-start.30
  196.7 4.8 %finish.2 = (bf16[2048,512]{1,0:T(8,128)(2,1)}, f32[512,128]{1,0:T(8,128)}, f32[16,512]{1,0:T(8,128)}) custom-call(s32[2]{0:T(128)} %pad_add_fusion.sc.refs_0_, f32[2048,512]{1,0:T(8,128)} %get-tuple-element.120.refs_1_, bf16[2048,512]{1,0:T(8,128)(2,1)} %bitcast.48, bf16[4,256,128]{2,1,0:T(8,128)(2,1)} %add_convert_fusion.8.refs_3_, ...), custom_call_target="tpu_custom_call" | custom-call | tf_op jit(solution)/shard_map/finish/pallas_call | solution.py:948
  201.5 5.2 %collective-permute-done.26 = bf16[8,16,2560]{2,1,0:T(8,128)(2,1)S(1)} collective-permute-done((bf16[8,16,2560]{2,1,0:T(8,128)(2,1)S(1)}, bf16[8,16,2560]{2,1,0:T(8,128)(2,1)S(1)}, u32[]{:S(2)}, u32[]{:S(2)}) %collective-permute-start.26) | collective-permute-done | bytes 655392 | tf_op jit(solution)/shard_map/ppermute | solution.py:596
  206.8 5.2 %collective-permute-done.27 = bf16[8,80,512]{2,1,0:T(8,128)(2,1)S(1)} collective-permute-done((bf16[8,80,512]{2,1,0:T(8,128)(2,1)}, bf16[8,80,512]{2,1,0:T(8,128)(2,1)S(1)}, u32[]{:S(2)}, u32[]{:S(2)}) %collective-permute-start.27) | collective-permute-done | bytes 655392 | tf_op jit(solution)/shard_map/ppermute | solution.py:596
  213.8 5.3 %finish.3 = (bf16[2048,512]{1,0:T(8,128)(2,1)}, bf16[16,16,256]{2,1,0:T(8,128)(2,1)}, bf16[16,16,256]{2,1,0:T(8,128)(2,1)}) custom-call(s32[2]{0:T(128)} %pad_add_fusion.sc.refs_0_, f32[2048,512]{1,0:T(8,128)} %get-tuple-element.120.refs_1_, bf16[2048,512]{1,0:T(8,128)(2,1)} %bitcast.49, ...), custom_call_target="tpu_custom_call", output_to_operand_aliasing={{0}: (12, {})} | custom-call | tf_op jit(solution)/shard_map/finish/pallas_call | solution.py:948
  222.3 7.1 %collective-permute-done.33 = bf16[4,80,512]{2,1,0:T(8,128)(2,1)S(1)} collective-permute-done((bf16[4,80,512]{2,1,0:T(8,128)(2,1)S(1)}, bf16[4,80,512]{2,1,0:T(8,128)(2,1)S(1)}, u32[]{:S(2)}, u32[]{:S(2)}) %collective-permute-start.33) | collective-permute-done | bytes 327712 | tf_op jit(solution)/shard_map/ppermute | solution.py:596
  231.2 4.2 %collective-permute-start.36 = (bf16[2,80,512]{2,1,0:T(8,128)(2,1)S(1)}, bf16[2,80,512]{2,1,0:T(8,128)(2,1)S(1)}, u32[]{:S(2)}, u32[]{:S(2)}) collective-permute-start(bf16[2,80,512]{2,1,0:T(8,128)(2,1)S(1)} %get-tuple-element.138), channel_id=1, source_target_pairs={{0,8},{8,0},{16,24},{24,16},{1,9},{9,1},{17,25},{25,17},{2,10},{10... | collective-permute-start | bytes 491528 | tf_op jit(solution)/shard_map/ppermute | solution.py:596
  235.5 5.1 %collective-permute-done.36 = bf16[2,80,512]{2,1,0:T(8,128)(2,1)S(1)} collective-permute-done((bf16[2,80,512]{2,1,0:T(8,128)(2,1)S(1)}, bf16[2,80,512]{2,1,0:T(8,128)(2,1)S(1)}, u32[]{:S(2)}, u32[]{:S(2)}) %collective-permute-start.36) | collective-permute-done | bytes 163872 | tf_op jit(solution)/shard_map/ppermute | solution.py:596
  240.6 2.0 collective-permute-done.35
  243.2 2.0 collective-permute-start.39
  246.6 4.6 %collective-permute-done.39 = bf16[1,80,512]{2,1,0:T(8,128)(2,1)S(1)} collective-permute-done((bf16[1,80,512]{2,1,0:T(8,128)(2,1)S(1)}, bf16[1,80,512]{2,1,0:T(8,128)(2,1)S(1)}, u32[]{:S(2)}, u32[]{:S(2)}) %collective-permute-start.39) | collective-permute-done | bytes 81952 | tf_op jit(solution)/shard_map/ppermute | solution.py:596
  252.1 3.7 %collective-permute-done.40 = bf16[2,16,256]{2,1,0:T(8,128)(2,1)S(1)} collective-permute-done((bf16[2,16,256]{2,1,0:T(8,128)(2,1)S(1)}, bf16[2,16,256]{2,1,0:T(8,128)(2,1)S(1)}, u32[]{:S(2)}, u32[]{:S(2)}) %collective-permute-start.40) | collective-permute-done | bytes 16416 | tf_op jit(solution)/shard_map/ppermute | solution.py:596
  256.3 4.2 %collective-permute-done.41 = bf16[1,16,256]{2,1,0:T(8,128)(2,1)S(1)} collective-permute-done((bf16[1,16,256]{2,1,0:T(8,128)(2,1)S(1)}, bf16[1,16,256]{2,1,0:T(8,128)(2,1)S(1)}, u32[]{:S(2)}, u32[]{:S(2)}) %collective-permute-start.41) | collective-permute-done | bytes 8224 | tf_op jit(solution)/shard_map/ppermute | solution.py:596
  (133 shorter events, 45.2 us)
Async XLA Ops:
  3.0 7.8 %collective-permute-start = (bf16[1,16,768]{2,1,0:T(8,128)(2,1)S(1)}, bf16[1,16,768]{2,1,0:T(8,128)(2,1)S(1)}, u32[]{:S(2)}, u32[]{:S(2)}) collective-permute-start(bf16[1,16,768]{2,1,0:T(8,128)(2,1)S(1)} %get-tuple-element.157), channel_id=1, source_target_pairs={{0,16},{8,24},{16,0},{24,8},{1,17},{9,25},{17,1},{25,9},{2,18},{10... | collective-permute-start | bytes 73736 | tf_op jit(solution)/shard_map/ppermute | solution.py:596
  7.9 11.9 %collective-permute-start.16 = (bf16[1,80,512]{2,1,0:T(8,128)(2,1)S(1)}, bf16[1,80,512]{2,1,0:T(8,128)(2,1)S(1)}, u32[]{:S(2)}, u32[]{:S(2)}) collective-permute-start(bf16[1,80,512]{2,1,0:T(8,128)(2,1)S(1)} %maximum_bitcast_fusion), channel_id=1, source_target_pairs={{0,16},{8,24},{16,0},{24,8},{1,17},{9,25},{17,1},{25,9},{2,18},{10... | collective-permute-start | bytes 245768 | tf_op jit(solution)/shard_map/ppermute | solution.py:596
  7.9 9.4 %collective-permute-start.11 = (bf16[1,16,2048]{2,1,0:T(8,128)(2,1)}, bf16[1,16,2048]{2,1,0:T(8,128)(2,1)S(1)}, u32[]{:S(2)}, u32[]{:S(2)}) collective-permute-start(bf16[1,16,2048]{2,1,0:T(8,128)(2,1)} %bitcast.56), channel_id=1, source_target_pairs={{0,16},{8,24},{16,0},{24,8},{1,17},{9,25},{17,1},{25,9},{2,18},{10... | collective-permute-start | bytes 196616 | tf_op jit(solution)/shard_map/ppermute | solution.py:596
  10.8 7.4 %collective-permute-start.1 = (bf16[2,16,768]{2,1,0:T(8,128)(2,1)S(1)}, bf16[2,16,768]{2,1,0:T(8,128)(2,1)S(1)}, u32[]{:S(2)}, u32[]{:S(2)}) collective-permute-start(bf16[2,16,768]{2,1,0:T(8,128)(2,1)S(1)} %pad_maximum_fusion.10), channel_id=1, source_target_pairs={{0,8},{8,0},{16,24},{24,16},{1,9},{9,1},{17,25},{25,17},{2,10},{10... | collective-permute-start | bytes 147464 | tf_op jit(solution)/shard_map/ppermute | solution.py:596
  18.1 12.3 %collective-permute-start.12 = (bf16[2,16,2048]{2,1,0:T(8,128)(2,1)S(1)}, bf16[2,16,2048]{2,1,0:T(8,128)(2,1)S(1)}, u32[]{:S(2)}, u32[]{:S(2)}) collective-permute-start(bf16[2,16,2048]{2,1,0:T(8,128)(2,1)S(1)} %pad_maximum_fusion.8), channel_id=1, source_target_pairs={{0,8},{8,0},{16,24},{24,16},{1,9},{9,1},{17,25},{25,17},{2,10},{10... | collective-permute-start | bytes 393224 | tf_op jit(solution)/shard_map/ppermute | solution.py:596
  19.8 6.2 %collective-permute-start.17 = (bf16[2,80,512]{2,1,0:T(8,128)(2,1)S(1)}, bf16[2,80,512]{2,1,0:T(8,128)(2,1)S(1)}, u32[]{:S(2)}, u32[]{:S(2)}) collective-permute-start(bf16[2,80,512]{2,1,0:T(8,128)(2,1)S(1)} %pad_maximum_fusion.7), channel_id=1, source_target_pairs={{0,8},{8,0},{16,24},{24,16},{1,9},{9,1},{17,25},{25,17},{2,10},{10... | collective-permute-start | bytes 491528 | tf_op jit(solution)/shard_map/ppermute | solution.py:596
  28.7 10.3 %collective-permute-start.4 = (bf16[16,16,768]{2,1,0:T(8,128)(2,1)S(1)}, bf16[16,16,768]{2,1,0:T(8,128)(2,1)S(1)}, u32[]{:S(2)}, u32[]{:S(2)}) collective-permute-start(bf16[16,16,768]{2,1,0:T(8,128)(2,1)S(1)} %constant_dynamic-update-slice_fusion.own), channel_id=1, source_target_pairs={{0,1},{1,0},{2,3},{3,2},{4,5},{5,4},{6,7},{7,6},{8,9},{9,8},{10,11... | collective-permute-start | bytes 1179656 | tf_op jit(solution)/shard_map/ppermute | solution.py:596
  28.7 10.1 %collective-permute-start.18 = (bf16[4,80,512]{2,1,0:T(8,128)(2,1)S(1)}, bf16[4,80,512]{2,1,0:T(8,128)(2,1)S(1)}, u32[]{:S(2)}, u32[]{:S(2)}) collective-permute-start(bf16[4,80,512]{2,1,0:T(8,128)(2,1)S(1)} %pad_maximum_fusion.4), channel_id=1, source_target_pairs={{0,4},{1,5},{2,6},{3,7},{4,0},{5,1},{6,2},{7,3},{8,12},{9,13},{10,... | collective-permute-start | bytes 983048 | tf_op jit(solution)/shard_map/ppermute | solution.py:596
  30.4 15.6 %collective-permute-start.13 = (bf16[4,16,2048]{2,1,0:T(8,128)(2,1)S(1)}, bf16[4,16,2048]{2,1,0:T(8,128)(2,1)S(1)}, u32[]{:S(2)}, u32[]{:S(2)}) collective-permute-start(bf16[4,16,2048]{2,1,0:T(8,128)(2,1)S(1)} %pad_maximum_fusion.5), channel_id=1, source_target_pairs={{0,2},{1,3},{2,0},{3,1},{4,6},{5,7},{6,4},{7,5},{8,10},{9,11},{10,... | collective-permute-start | bytes 786440 | tf_op jit(solution)/shard_map/ppermute | solution.py:596
  44.5 16.3 %collective-permute-start.19 = (bf16[8,80,512]{2,1,0:T(8,128)(2,1)S(1)}, bf16[8,80,512]{2,1,0:T(8,128)(2,1)S(1)}, u32[]{:S(2)}, u32[]{:S(2)}) collective-permute-start(bf16[8,80,512]{2,1,0:T(8,128)(2,1)S(1)} %pad_maximum_fusion.2), channel_id=1, source_target_pairs={{0,2},{1,3},{2,0},{3,1},{4,6},{5,7},{6,4},{7,5},{8,10},{9,11},{10,... | collective-permute-start | bytes 1966088 | tf_op jit(solution)/shard_map/ppermute | solution.py:596
  46.1 25.9 %collective-permute-start.14 = (bf16[8,16,2048]{2,1,0:T(8,128)(2,1)S(1)}, bf16[8,16,2048]{2,1,0:T(8,128)(2,1)S(1)}, u32[]{:S(2)}, u32[]{:S(2)}) collective-permute-start(bf16[8,16,2048]{2,1,0:T(8,128)(2,1)S(1)} %pad_maximum_fusion.3), channel_id=1, source_target_pairs={{0,4},{1,5},{2,6},{3,7},{4,0},{5,1},{6,2},{7,3},{8,12},{9,13},{10,... | collective-permute-start | bytes 1572872 | tf_op jit(solution)/shard_map/ppermute | solution.py:596
  47.6 13.3 %collective-permute-start.5 = (bf16[4,256,128]{2,1,0:T(8,128)(2,1)}, bf16[4,256,128]{2,1,0:T(8,128)(2,1)S(1)}, u32[]{:S(2)}, u32[]{:S(2)}) collective-permute-start(bf16[4,256,128]{2,1,0:T(8,128)(2,1)} %get-tuple-element.87.refs_5_), channel_id=1, source_target_pairs={{0,8},{8,0},{16,24},{24,16},{1,9},{9,1},{17,25},{25,17},{2,10},{10... | collective-permute-start | bytes 786440 | tf_op jit(solution)/shard_map/ppermute | solution.py:596
  49.6 21.6 %collective-permute-start.6 = (bf16[4,256,128]{2,1,0:T(8,128)(2,1)}, bf16[4,256,128]{2,1,0:T(8,128)(2,1)S(1)}, u32[]{:S(2)}, u32[]{:S(2)}) collective-permute-start(bf16[4,256,128]{2,1,0:T(8,128)(2,1)} %get-tuple-element.87.refs_5_), channel_id=1, source_target_pairs={{0,16},{8,24},{16,0},{24,8},{1,17},{9,25},{17,1},{25,9},{2,18},{10... | collective-permute-start | bytes 786440 | tf_op jit(solution)/shard_map/ppermute | solution.py:596
  50.1 21.9 %collective-permute-start.7 = (bf16[4,256,128]{2,1,0:T(8,128)(2,1)}, bf16[4,256,128]{2,1,0:T(8,128)(2,1)}, u32[]{:S(2)}, u32[]{:S(2)}) collective-permute-start(bf16[4,256,128]{2,1,0:T(8,128)(2,1)} %get-tuple-element.87.refs_5_), channel_id=1, source_target_pairs={{0,24},{8,16},{16,8},{24,0},{1,25},{9,17},{17,9},{25,1},{2,26},{10... | collective-permute-start | bytes 786440 | tf_op jit(solution)/shard_map/ppermute | solution.py:596
  72.7 53.1 %collective-permute-start.10 = (bf16[4,256,128]{2,1,0:T(8,128)(2,1)S(1)}, bf16[4,256,128]{2,1,0:T(8,128)(2,1)}, u32[]{:S(2)}, u32[]{:S(2)}) collective-permute-start(bf16[4,256,128]{2,1,0:T(8,128)(2,1)S(1)} %copy-done.8), channel_id=1, source_target_pairs={{0,24},{8,16},{16,8},{24,0},{1,25},{9,17},{17,9},{25,1},{2,26},{10... | collective-permute-start | bytes 786440 | tf_op jit(solution)/shard_map/ppermute | solution.py:596
  75.1 52.7 %collective-permute-start.8 = (bf16[4,256,128]{2,1,0:T(8,128)(2,1)S(1)}, bf16[4,256,128]{2,1,0:T(8,128)(2,1)}, u32[]{:S(2)}, u32[]{:S(2)}) collective-permute-start(bf16[4,256,128]{2,1,0:T(8,128)(2,1)S(1)} %copy-done.8), channel_id=1, source_target_pairs={{0,8},{8,0},{16,24},{24,16},{1,9},{9,1},{17,25},{25,17},{2,10},{10... | collective-permute-start | bytes 786440 | tf_op jit(solution)/shard_map/ppermute | solution.py:596
  77.6 50.2 %collective-permute-start.9 = (bf16[4,256,128]{2,1,0:T(8,128)(2,1)S(1)}, bf16[4,256,128]{2,1,0:T(8,128)(2,1)}, u32[]{:S(2)}, u32[]{:S(2)}) collective-permute-start(bf16[4,256,128]{2,1,0:T(8,128)(2,1)S(1)} %copy-done.8), channel_id=1, source_target_pairs={{0,16},{8,24},{16,0},{24,8},{1,17},{9,25},{17,1},{25,9},{2,18},{10... | collective-permute-start | bytes 786440 | tf_op jit(solution)/shard_map/ppermute | solution.py:596
  123.2 62.0 %collective-permute-start.21 = (bf16[4,256,128]{2,1,0:T(8,128)(2,1)}, bf16[4,256,128]{2,1,0:T(8,128)(2,1)S(1)}, u32[]{:S(2)}, u32[]{:S(2)}) collective-permute-start(bf16[4,256,128]{2,1,0:T(8,128)(2,1)} %get-tuple-element.112), channel_id=1, source_target_pairs={{0,8},{8,0},{16,24},{24,16},{1,9},{9,1},{17,25},{25,17},{2,10},{10... | collective-permute-start | bytes 786440 | tf_op jit(solution)/shard_map/ppermute | solution.py:596
  125.3 59.9 %collective-permute-start.22 = (bf16[4,256,128]{2,1,0:T(8,128)(2,1)}, bf16[4,256,128]{2,1,0:T(8,128)(2,1)S(1)}, u32[]{:S(2)}, u32[]{:S(2)}) collective-permute-start(bf16[4,256,128]{2,1,0:T(8,128)(2,1)} %get-tuple-element.113), channel_id=1, source_target_pairs={{0,16},{8,24},{16,0},{24,8},{1,17},{9,25},{17,1},{25,9},{2,18},{10... | collective-permute-start | bytes 786440 | tf_op jit(solution)/shard_map/ppermute | solution.py:596
  125.7 59.6 %collective-permute-start.23 = (bf16[4,256,128]{2,1,0:T(8,128)(2,1)}, bf16[4,256,128]{2,1,0:T(8,128)(2,1)S(1)}, u32[]{:S(2)}, u32[]{:S(2)}) collective-permute-start(bf16[4,256,128]{2,1,0:T(8,128)(2,1)} %get-tuple-element.114), channel_id=1, source_target_pairs={{0,24},{8,16},{16,8},{24,0},{1,25},{9,17},{17,9},{25,1},{2,26},{10... | collective-permute-start | bytes 786440 | tf_op jit(solution)/shard_map/ppermute | solution.py:596
  186.2 8.6 %collective-permute-start.25 = (bf16[16,80,512]{2,1,0:T(8,128)(2,1)}, bf16[16,80,512]{2,1,0:T(8,128)(2,1)S(1)}, u32[]{:S(2)}, u32[]{:S(2)}) collective-permute-start(bf16[16,80,512]{2,1,0:T(8,128)(2,1)} %get-tuple-element.118), channel_id=1, source_target_pairs={{0,1},{1,0},{2,3},{3,2},{4,5},{5,4},{6,7},{7,6},{8,9},{9,8},{10,11... | collective-permute-start | bytes 3932168 | tf_op jit(solution)/shard_map/ppermute | solution.py:596
  189.8 16.8 %collective-permute-start.26 = (bf16[8,16,2560]{2,1,0:T(8,128)(2,1)S(1)}, bf16[8,16,2560]{2,1,0:T(8,128)(2,1)S(1)}, u32[]{:S(2)}, u32[]{:S(2)}) collective-permute-start(bf16[8,16,2560]{2,1,0:T(8,128)(2,1)S(1)} %get-tuple-element.160), channel_id=1, source_target_pairs={{0,4},{1,5},{2,6},{3,7},{4,0},{5,1},{6,2},{7,3},{8,12},{9,13},{10,... | collective-permute-start | bytes 1966088 | tf_op jit(solution)/shard_map/ppermute | solution.py:596
  190.4 21.8 %collective-permute-start.28 = (bf16[4,256,128]{2,1,0:T(8,128)(2,1)}, bf16[4,256,128]{2,1,0:T(8,128)(2,1)S(1)}, u32[]{:S(2)}, u32[]{:S(2)}) collective-permute-start(bf16[4,256,128]{2,1,0:T(8,128)(2,1)} %get-tuple-element.122), channel_id=1, source_target_pairs={{0,8},{8,0},{16,24},{24,16},{1,9},{9,1},{17,25},{25,17},{2,10},{10... | collective-permute-start | bytes 786440 | tf_op jit(solution)/shard_map/ppermute | solution.py:596
  191.5 21.6 %collective-permute-start.29 = (bf16[4,256,128]{2,1,0:T(8,128)(2,1)}, bf16[4,256,128]{2,1,0:T(8,128)(2,1)S(1)}, u32[]{:S(2)}, u32[]{:S(2)}) collective-permute-start(bf16[4,256,128]{2,1,0:T(8,128)(2,1)} %get-tuple-element.123), channel_id=1, source_target_pairs={{0,16},{8,24},{16,0},{24,8},{1,17},{9,25},{17,1},{25,9},{2,18},{10... | collective-permute-start | bytes 786440 | tf_op jit(solution)/shard_map/ppermute | solution.py:596
  192.7 20.3 %collective-permute-start.30 = (bf16[4,256,128]{2,1,0:T(8,128)(2,1)}, bf16[4,256,128]{2,1,0:T(8,128)(2,1)}, u32[]{:S(2)}, u32[]{:S(2)}) collective-permute-start(bf16[4,256,128]{2,1,0:T(8,128)(2,1)} %get-tuple-element.124), channel_id=1, source_target_pairs={{0,24},{8,16},{16,8},{24,0},{1,25},{9,17},{17,9},{25,1},{2,26},{10... | collective-permute-start | bytes 786440 | tf_op jit(solution)/shard_map/ppermute | solution.py:596
  196.1 15.9 %collective-permute-start.27 = (bf16[8,80,512]{2,1,0:T(8,128)(2,1)}, bf16[8,80,512]{2,1,0:T(8,128)(2,1)S(1)}, u32[]{:S(2)}, u32[]{:S(2)}) collective-permute-start(bf16[8,80,512]{2,1,0:T(8,128)(2,1)} %get-tuple-element.158), channel_id=1, source_target_pairs={{0,2},{1,3},{2,0},{3,1},{4,6},{5,7},{6,4},{7,5},{8,10},{9,11},{10,... | collective-permute-start | bytes 1966088 | tf_op jit(solution)/shard_map/ppermute | solution.py:596
  219.2 10.1 %collective-permute-start.33 = (bf16[4,80,512]{2,1,0:T(8,128)(2,1)S(1)}, bf16[4,80,512]{2,1,0:T(8,128)(2,1)S(1)}, u32[]{:S(2)}, u32[]{:S(2)}) collective-permute-start(bf16[4,80,512]{2,1,0:T(8,128)(2,1)S(1)} %get-tuple-element.162), channel_id=1, source_target_pairs={{0,4},{1,5},{2,6},{3,7},{4,0},{5,1},{6,2},{7,3},{8,12},{9,13},{10,... | collective-permute-start | bytes 983048 | tf_op jit(solution)/shard_map/ppermute | solution.py:596
  220.8 9.8 %collective-permute-start.32 = (bf16[4,16,2560]{2,1,0:T(8,128)(2,1)S(1)}, bf16[4,16,2560]{2,1,0:T(8,128)(2,1)S(1)}, u32[]{:S(2)}, u32[]{:S(2)}) collective-permute-start(bf16[4,16,2560]{2,1,0:T(8,128)(2,1)S(1)} %get-tuple-element.164), channel_id=1, source_target_pairs={{0,2},{1,3},{2,0},{3,1},{4,6},{5,7},{6,4},{7,5},{8,10},{9,11},{10,... | collective-permute-start | bytes 983048 | tf_op jit(solution)/shard_map/ppermute | solution.py:596
  231.2 9.3 %collective-permute-start.36 = (bf16[2,80,512]{2,1,0:T(8,128)(2,1)S(1)}, bf16[2,80,512]{2,1,0:T(8,128)(2,1)S(1)}, u32[]{:S(2)}, u32[]{:S(2)}) collective-permute-start(bf16[2,80,512]{2,1,0:T(8,128)(2,1)S(1)} %get-tuple-element.138), channel_id=1, source_target_pairs={{0,8},{8,0},{16,24},{24,16},{1,9},{9,1},{17,25},{25,17},{2,10},{10... | collective-permute-start | bytes 491528 | tf_op jit(solution)/shard_map/ppermute | solution.py:596
  235.4 7.1 %collective-permute-start.35 = (bf16[2,16,2560]{2,1,0:T(8,128)(2,1)S(1)}, bf16[2,16,2560]{2,1,0:T(8,128)(2,1)S(1)}, u32[]{:S(2)}, u32[]{:S(2)}) collective-permute-start(bf16[2,16,2560]{2,1,0:T(8,128)(2,1)S(1)} %get-tuple-element.136), channel_id=1, source_target_pairs={{0,8},{8,0},{16,24},{24,16},{1,9},{9,1},{17,25},{25,17},{2,10},{10... | collective-permute-start | bytes 491528 | tf_op jit(solution)/shard_map/ppermute | solution.py:596
  243.2 8.0 %collective-permute-start.39 = (bf16[1,80,512]{2,1,0:T(8,128)(2,1)S(1)}, bf16[1,80,512]{2,1,0:T(8,128)(2,1)S(1)}, u32[]{:S(2)}, u32[]{:S(2)}) collective-permute-start(bf16[1,80,512]{2,1,0:T(8,128)(2,1)S(1)} %get-tuple-element.144), channel_id=1, source_target_pairs={{0,16},{8,24},{16,0},{24,8},{1,17},{9,25},{17,1},{25,9},{2,18},{10... | collective-permute-start | bytes 245768 | tf_op jit(solution)/shard_map/ppermute | solution.py:596
  245.2 6.8 %collective-permute-start.38 = (bf16[1,16,2560]{2,1,0:T(8,128)(2,1)S(1)}, bf16[1,16,2560]{2,1,0:T(8,128)(2,1)S(1)}, u32[]{:S(2)}, u32[]{:S(2)}) collective-permute-start(bf16[1,16,2560]{2,1,0:T(8,128)(2,1)S(1)} %get-tuple-element.142), channel_id=1, source_target_pairs={{0,16},{8,24},{16,0},{24,8},{1,17},{9,25},{17,1},{25,9},{2,18},{10... | collective-permute-start | bytes 245768 | tf_op jit(solution)/shard_map/ppermute | solution.py:596
  (26 other events, 212.1 us)

commit v3 on v2

--- a/solution.py
+++ b/solution.py
@@ -12,6 +12,8 @@
 C0 = 0.7978845608028654
 C1 = 0.7978845608028654 * 0.044715
 PARTS = (4, 4)
+LAG = 2
+GSW = 1
 R = 2
 FC = 32
 FU = 4
@@ -21,8 +23,9 @@
 SC = 64
 SU = 4
 SD = 64
-SV = 4
-VMEM_LIMIT = 60 * 1024 * 1024
+SV = 8
+VMEM_LIMIT = 52 * 1024 * 1024
+SMALL_LIMIT = 24 * 1024 * 1024
 F32 = jnp.float32
 BF16 = jnp.bfloat16
 
@@ -243,7 +246,7 @@
 
     def attend(r, outer):
         for m in range(nseq):
-            score[:, m * local : (m + 1) * local] = mmt(qp[r], kvs[m][r])
+            score[r, :, m * local : (m + 1) * local] = mmt(qp[r], kvs[m][r])
         seg_k = jnp.concatenate(
             [
                 seg[r, :, pl.ds(pl.multiple_of((place ^ m) * local, 128), local)]
@@ -252,14 +255,17 @@
             axis=1,
         )
         own = seg[r, :, pl.ds(pl.multiple_of(place * local, 128), local)].astype(F32)
-        inner[0:local, :] = jnp.transpose(jnp.broadcast_to(own, (128, local)))
+        inner[pl.ds(pl.multiple_of(r * local, local), local), :] = jnp.transpose(
+            jnp.broadcast_to(own, (128, local))
+        )
 
         def soft_chunk(c, carry):
             at = pl.multiple_of(c * SC, SC)
-            match = inner[pl.ds(at, SC), 0:1].astype(jnp.int32) == seg_k
+            mine = pl.ds(pl.multiple_of(r * local + at, SC), SC)
+            match = inner[mine, 0:1].astype(jnp.int32) == seg_k
             for s in range(2):
                 sl = pl.ds(pl.multiple_of(s * local + at, SC), SC)
-                sc_ = jnp.where(match, score[sl, :], NEG)
+                sc_ = jnp.where(match, score[r, sl, :], NEG)
                 num = jnp.exp(sc_ - jnp.max(sc_, axis=-1, keepdims=True))
                 total = jnp.sum(num, axis=-1, keepdims=True)
                 prob[r, sl, :] = (num * (1.0 / total)).astype(BF16)
@@ -277,7 +283,8 @@
         cd[1, own_rows, :] = ctx[local:]
         return outer
 
-    lax.fori_loop(0, R, attend, 0, unroll=RU)
+    for r in range(R):
+        attend(r, 0)
 
     @pl.when(step == 0)
     def _():
@@ -321,30 +328,32 @@
     wide2[...] = jnp.zeros_like(wide2)
 
     def hidden_block(j, carry):
-        js = pl.ds(pl.multiple_of(j * width, width), width)
-        hid[0] = mm(n2[...], wup[:, js])
-        gac[0] = mmt(cot[...], wdn[js, :])
+        js = slice(j * width, (j + 1) * width)
+        k = j % 2
+        hid[k] = mm(n2[...], wup[:, js])
+        gac[k] = mmt(cot[...], wdn[js, :])
         bias = bup[0:1, js]
         total = jnp.zeros((8, width), F32)
         for c in range(tile // FC):
             sl = slice(c * FC, (c + 1) * FC)
-            h = hid[0, sl, :] + bias
+            h = hid[k, sl, :] + bias
             h2 = h * h
             t = jnp.tanh(h * (C0 + C1 * h2))
             hh = 0.5 * h
-            act[0, sl, :] = (hh + hh * t).astype(BF16)
+            act[k, sl, :] = (hh + hh * t).astype(BF16)
             slope = (0.5 + 0.5 * t) + hh * (1.0 - t * t) * (C0 + (3.0 * C1) * h2)
-            g = (gac[0, sl, :] * slope).astype(BF16)
-            ghd[0, sl, :] = g
+            g = (gac[k, sl, :] * slope).astype(BF16)
+            ghd[k, sl, :] = g
             total = total + fold8(g.astype(F32))
-        vacc[pl.ds(pl.multiple_of((7 + j) * 8, 8), 8), :] += total
-        wide1[...] += mm(act[0], wdn[js, :])
-        wide2[...] += mmt(ghd[0], wup[:, js])
-        acc_up[:, js] += mm(n2_t[...], ghd[0])
-        acc_dn[:, js] += mm(cot_t[...], act[0])
+        vacc[(7 + j) * 8 : (8 + j) * 8, :] += total
+        wide1[...] += mm(act[k], wdn[js, :])
+        wide2[...] += mmt(ghd[k], wup[:, js])
+        acc_up[:, js] += mm(n2_t[...], ghd[k])
+        acc_dn[:, js] += mm(cot_t[...], act[k])
         return carry
 
-    lax.fori_loop(0, wup.shape[1] // width, hidden_block, 0, unroll=FU)
+    for j in range(wup.shape[1] // width):
+        hidden_block(j, 0)
 
     def out_chunk(c, carry):
         sl = pl.ds(pl.multiple_of(c * ch, ch), ch)
@@ -411,8 +420,8 @@
 
     def attend_back(r, outer):
         for m in range(nseq):
-            score[:, m * local : (m + 1) * local] = mmt(dp[r], kvs[m][r])
-        dsc = act
+            score[r, :, m * local : (m + 1) * local] = mmt(dp[r], kvs[m][r])
+        dsc = (act, ghd)[r % 2]
 
         def score_chunk(c, carry):
             at = pl.multiple_of(c * SD, SD)
@@ -420,7 +429,7 @@
             inn = inner[pl.ds(pl.multiple_of(r * 2 * local + at, SD), SD), 0:1]
             for k in range(2):
                 ks = slice(k * width, (k + 1) * width)
-                dsc[k, sl, :] = (prob[r, sl, ks].astype(F32) * (score[sl, ks] - inn)).astype(BF16)
+                dsc[k, sl, :] = (prob[r, sl, ks].astype(F32) * (score[r, sl, ks] - inn)).astype(BF16)
             return carry
 
         lax.fori_loop(0, 2 * local // SD, score_chunk, 0, unroll=SV)
@@ -442,7 +451,8 @@
         cd[1, own_rows, :] = dq[local:]
         return outer
 
-    lax.fori_loop(0, R, attend_back, 0, unroll=RU)
+    for r in range(R):
+        attend_back(r, 0)
 
     def query_chunk(c, carry):
         sl = pl.ds(pl.multiple_of(c * ch, ch), ch)
@@ -692,7 +702,7 @@
             pltpu.VMEM((2, tile, 128), F32),
             pltpu.VMEM((2 * tile, 128), F32),
             pltpu.VMEM((R, 2 * local, nseq * local), BF16),
-            pltpu.VMEM((2 * local, nseq * local), F32),
+            pltpu.VMEM((R, 2 * local, nseq * local), F32),
             pltpu.VMEM(wide, F32),
             pltpu.VMEM(wide, F32),
             pltpu.VMEM(wide, F32),
@@ -816,6 +826,10 @@
     order_d = zz[::-1] + xy[::-1] + [core]
     back_u = [core] + xy[::-1] + zz
     back_d = [core] + xy + zz
+    if GSW == 1:
+        back_u = [core] + xy[::-1][:1] + zz[:1] + xy[::-1][1:] + zz[1:]
+    if GSW == 2:
+        back_u = [core] + xy[::-1][:1] + zz[:1] + zz[1:] + xy[::-1][1:]
     back_s = [core] + xy[::-1] + zz
 
     def grow(x, hop):
@@ -840,15 +854,13 @@
         dn = grow(dn, order_d[n])
     for hop in order_a[nz:-1]:
         pack = grow(pack, hop)
-    u = after(u, pack)
-    dn = after(dn, pack)
-    u = grow(u, order_u[nz])
-    dn = grow(dn, order_d[nz])
+    u = grow(after(u, pack), order_u[nz])
+    dn = grow(after(dn, pack), order_d[nz])
     packs = [pack, swap(pack, core, sizes)]
 
     smem = pl.BlockSpec(memory_space=pltpu.SMEM)
     anywhere = pl.BlockSpec(memory_space=pl.ANY)
-    params = pltpu.CompilerParams(vmem_limit_bytes=VMEM_LIMIT)
+    params = pltpu.CompilerParams(vmem_limit_bytes=SMALL_LIMIT)
     shape = jax.ShapeDtypeStruct
 
     can, vec, bup, *kv_parts = pl.pallas_call(
@@ -879,8 +891,8 @@
         kv_all.append([kv] + [swap(kv, ("seq", m), sizes) for m in range(1, nseq)])
 
     gather_kv(kv_parts[0])
-    u = after(u, can)
-    dn = after(dn, can)
+    u = after(u, kv_all[0][1])
+    dn = after(dn, kv_all[0][1])
     for n in range(nz + 1, len(order_u) - 1):
         u = grow(u, order_u[n])
         dn = grow(dn, order_d[n])
@@ -960,12 +972,16 @@
         eacc = got[1:]
         row0 += count
     gs = eacc
+    gu, gd, unused = lax.optimization_barrier((gu, gd, dkv_all[-1]))
+    later = [(gu, gd)]
+    for n in range(2, len(back_u)):
+        gu = narrow_step(gu, back_u[n], sizes)
+        gd = narrow_step(gd, back_d[n], sizes)
+        later.append((gu, gd))
     for n in range(len(back_s)):
+        if 0 < n - LAG < len(later):
+            gs = after(gs, later[n - LAG])
         gs = narrow_step(gs, back_s[n], sizes)
-        if n + 2 < len(back_u):
-            gu = narrow_step(gu, back_u[n + 2], sizes)
-            gd = narrow_step(gd, back_d[n + 2], sizes)
-        gs, gu, gd = lax.optimization_barrier((gs, gu, gd))
     gs, gu, gd = gs[0], gu[0], gd[0]
 
     def vector(v):

time: 264 us -> 250 us (0.947)
  starting transfers between devices: 51.5 us -> 65.5 us
  waiting for transfers between devices: 78.4 us -> 66.9 us
  Pallas kernels: 115 us -> 104 us
  local copies, waits for them, and re-layouts: 11.3 us -> 8.63 us
    ppermute x42, starting transfers between devices: 51.5 us -> 65.5 us  [swap(): return lax.ppermute(x, axis, [(i, i ^ mask) for i in range(sizes[axis])])]
    ppermute x42, waiting for transfers between devices: 78.4 us -> 66.9 us  [swap(): return lax.ppermute(x, axis, [(i, i ^ mask) for i in range(sizes[axis])])]
    pallas_call x2, Pallas kernels: 100 us -> 94.4 us  [layer_calls(): pl.pallas_call(functools.partial(kernel_b, cfg), grid=(steps,), out_shape...]
    pallas_call x2, Pallas kernels: 10.1 us -> 7.19 us  [body(): pl.pallas_call(functools.partial(kernel_e, cfg), grid=(steps,), out_shape...]
  transfers between devices with their start and end apart: 42 -> 42, of which waited for: 20 -> 20; matrix products, arithmetic and copies ran while one was open for 2% -> 3% of each run, Pallas kernels for 41% -> 40%
where the time goes in v3:
time: 250 us; the launch traced here: 252 us
  Pallas kernels  104 us (42%)
  waiting for transfers between devices  66.9 us (27%)
  starting transfers between devices  65.5 us (26%)
  local copies, waits for them, and re-layouts  8.63 us (3%)
  other arithmetic  5.33 us (2%)
    pallas_call x2, Pallas kernels, layer_calls(): pl.pallas_call(functools.partial(kernel_b, cfg), grid=(steps,), out_shape...  94.4 us
    ppermute x42, waiting for transfers between devices, swap(): return lax.ppermute(x, axis, [(i, i ^ mask) for i in range(sizes[axis])])  66.9 us
    ppermute x42, starting transfers between devices, swap(): return lax.ppermute(x, axis, [(i, i ^ mask) for i in range(sizes[axis])])  65.5 us
    pallas_call x2, Pallas kernels, body(): pl.pallas_call(functools.partial(kernel_e, cfg), grid=(steps,), out_shape...  7.19 us
  transfers between devices with their start and end apart: 42, of which 20 were waited for; matrix products, arithmetic and copies ran while one was open for 3% of the time, Pallas kernels for 40%

profile of v3, /device:TPU:0, one launch (start us, length us, event | category | flops | bytes accessed | tf_op | source)
XLA Modules:
  0.0 251.7 jit_solution(12837617807191704964)
XLA Ops:
  3.0 4.0 %collective-permute-start = (bf16[1,16,768]{2,1,0:T(8,128)(2,1)S(1)}, bf16[1,16,768]{2,1,0:T(8,128)(2,1)S(1)}, u32[]{:S(2)}, u32[]{:S(2)}) collective-permute-start(bf16[1,16,768]{2,1,0:T(8,128)(2,1)S(1)} %get-tuple-element.131), channel_id=1, source_target_pairs={{0,16},{8,24},{16,0},{24,8},{1,17},{9,25},{17,1},{25,9},{2,18},{10... | collective-permute-start | bytes 73736 | tf_op jit(solution)/shard_map/ppermute | solution.py:606
  7.9 2.9 %collective-permute-start.11 = (bf16[1,16,2048]{2,1,0:T(8,128)(2,1)}, bf16[1,16,2048]{2,1,0:T(8,128)(2,1)S(1)}, u32[]{:S(2)}, u32[]{:S(2)}) collective-permute-start(bf16[1,16,2048]{2,1,0:T(8,128)(2,1)} %bitcast.58), channel_id=1, source_target_pairs={{0,16},{8,24},{16,0},{24,8},{1,17},{9,25},{17,1},{25,9},{2,18},{10... | collective-permute-start | bytes 196616 | tf_op jit(solution)/shard_map/ppermute | solution.py:606
  12.5 2.7 %collective-permute-done.1 = bf16[2,16,768]{2,1,0:T(8,128)(2,1)S(1)} collective-permute-done((bf16[2,16,768]{2,1,0:T(8,128)(2,1)S(1)}, bf16[2,16,768]{2,1,0:T(8,128)(2,1)S(1)}, u32[]{:S(2)}, u32[]{:S(2)}) %collective-permute-start.1) | collective-permute-done | bytes 49184 | tf_op jit(solution)/shard_map/ppermute | solution.py:606
  16.7 3.1 %collective-permute-done.2 = bf16[4,16,768]{2,1,0:T(8,128)(2,1)S(1)} collective-permute-done((bf16[4,16,768]{2,1,0:T(8,128)(2,1)S(1)}, bf16[4,16,768]{2,1,0:T(8,128)(2,1)S(1)}, u32[]{:S(2)}, u32[]{:S(2)}) %collective-permute-start.2) | collective-permute-done | bytes 98336 | tf_op jit(solution)/shard_map/ppermute | solution.py:606
  23.0 2.6 %collective-permute-done.3 = bf16[8,16,768]{2,1,0:T(8,128)(2,1)S(1)} collective-permute-done((bf16[8,16,768]{2,1,0:T(8,128)(2,1)S(1)}, bf16[8,16,768]{2,1,0:T(8,128)(2,1)S(1)}, u32[]{:S(2)}, u32[]{:S(2)}) %collective-permute-start.3) | collective-permute-done | bytes 196640 | tf_op jit(solution)/shard_map/ppermute | solution.py:606
  29.0 2.5 project.1
  33.8 3.4 %collective-permute-done.18 = bf16[4,80,512]{2,1,0:T(8,128)(2,1)S(1)} collective-permute-done((bf16[4,80,512]{2,1,0:T(8,128)(2,1)S(1)}, bf16[4,80,512]{2,1,0:T(8,128)(2,1)S(1)}, u32[]{:S(2)}, u32[]{:S(2)}) %collective-permute-start.18) | collective-permute-done | bytes 327712 | tf_op jit(solution)/shard_map/ppermute | solution.py:606
  37.2 2.5 collective-permute-done.5.refs_6_
  41.8 3.6 %collective-permute-start.6 = (bf16[4,256,128]{2,1,0:T(8,128)(2,1)S(1)}, bf16[4,256,128]{2,1,0:T(8,128)(2,1)S(1)}, u32[]{:S(2)}, u32[]{:S(2)}) collective-permute-start(bf16[4,256,128]{2,1,0:T(8,128)(2,1)S(1)} %get-tuple-element.72.refs_5_), channel_id=1, source_target_pairs={{0,16},{8,24},{16,0},{24,8},{1,17},{9,25},{17,1},{25,9},{2,18},{10... | collective-permute-start | bytes 786440 | tf_op jit(solution)/shard_map/ppermute | solution.py:606
  46.0 9.4 %collective-permute-done.19 = bf16[8,80,512]{2,1,0:T(8,128)(2,1)S(1)} collective-permute-done((bf16[8,80,512]{2,1,0:T(8,128)(2,1)S(1)}, bf16[8,80,512]{2,1,0:T(8,128)(2,1)S(1)}, u32[]{:S(2)}, u32[]{:S(2)}) %collective-permute-start.19) | collective-permute-done | bytes 655392 | tf_op jit(solution)/shard_map/ppermute | solution.py:606
  55.5 6.9 %collective-permute-done.6.refs_7_ = bf16[4,256,128]{2,1,0:T(8,128)(2,1)S(1)} collective-permute-done((bf16[4,256,128]{2,1,0:T(8,128)(2,1)S(1)}, bf16[4,256,128]{2,1,0:T(8,128)(2,1)S(1)}, u32[]{:S(2)}, u32[]{:S(2)}) %collective-permute-start.6) | collective-permute-done | bytes 262176 | tf_op jit(solution)/shard_map/ppermute | solution.py:606
  63.2 2.9 %collective-permute-start.10 = (bf16[4,256,128]{2,1,0:T(8,128)(2,1)S(1)}, bf16[4,256,128]{2,1,0:T(8,128)(2,1)S(1)}, u32[]{:S(2)}, u32[]{:S(2)}) collective-permute-start(bf16[4,256,128]{2,1,0:T(8,128)(2,1)S(1)} %get-tuple-element.73.refs_5_), channel_id=1, source_target_pairs={{0,24},{8,16},{16,8},{24,0},{1,25},{9,17},{17,9},{25,1},{2,26},{10... | collective-permute-start | bytes 786440 | tf_op jit(solution)/shard_map/ppermute | solution.py:606
  66.1 4.9 %collective-permute-start.8 = (bf16[4,256,128]{2,1,0:T(8,128)(2,1)S(1)}, bf16[4,256,128]{2,1,0:T(8,128)(2,1)S(1)}, u32[]{:S(2)}, u32[]{:S(2)}) collective-permute-start(bf16[4,256,128]{2,1,0:T(8,128)(2,1)S(1)} %get-tuple-element.73.refs_5_), channel_id=1, source_target_pairs={{0,8},{8,0},{16,24},{24,16},{1,9},{9,1},{17,25},{25,17},{2,10},{10... | collective-permute-start | bytes 786440 | tf_op jit(solution)/shard_map/ppermute | solution.py:606
  72.4 40.8 %layer.2 = (bf16[2048,512]{1,0:T(8,128)(2,1)}, f32[2048,512]{1,0:T(8,128)}, bf16[4,256,128]{2,1,0:T(8,128)(2,1)S(1)}, bf16[4,256,128]{2,1,0:T(8,128)(2,1)S(1)}, ...) custom-call(s32[2]{0:T(128)S(1)} %pad_add_fusion.sc.refs_0_, ...), custom_call_target="tpu_custom_call" | custom-call | tf_op jit(solution)/shard_map/layer/pallas_call | solution.py:735
  114.7 1.8 collective-permute-start.22
  118.8 53.6 %layer.3 = (bf16[2048,512]{1,0:T(8,128)(2,1)}, f32[2048,512]{1,0:T(8,128)}, bf16[4,256,128]{2,1,0:T(8,128)(2,1)S(1)}, bf16[4,256,128]{2,1,0:T(8,128)(2,1)S(1)}, ...) custom-call(s32[2]{0:T(128)S(1)} %pad_add_fusion.sc.refs_0_, ...), custom_call_target="tpu_custom_call", output_to_operand_aliasing={{0}: (21, {}), {1}: (22, {})} | custom-call | tf_op jit(solution)/shard_map/layer/pallas_call | solution.py:735
  173.1 2.7 %collective-permute-done.24 = bf16[16,16,2560]{2,1,0:T(8,128)(2,1)S(1)} collective-permute-done((bf16[16,16,2560]{2,1,0:T(8,128)(2,1)}, bf16[16,16,2560]{2,1,0:T(8,128)(2,1)S(1)}, u32[]{:S(2)}, u32[]{:S(2)}) %collective-permute-start.24) | collective-permute-done | bytes 1310752 | tf_op jit(solution)/shard_map/ppermute | solution.py:606
  175.9 1.9 add_convert_fusion.2
  177.7 6.3 %collective-permute-start.26 = (bf16[8,16,2560]{2,1,0:T(8,128)(2,1)S(1)}, bf16[8,16,2560]{2,1,0:T(8,128)(2,1)S(1)}, u32[]{:S(2)}, u32[]{:S(2)}) collective-permute-start(bf16[8,16,2560]{2,1,0:T(8,128)(2,1)S(1)} %get-tuple-element.134), channel_id=1, source_target_pairs={{0,4},{1,5},{2,6},{3,7},{4,0},{5,1},{6,2},{7,3},{8,12},{9,13},{10,... | collective-permute-start | bytes 1966088 | tf_op jit(solution)/shard_map/ppermute | solution.py:606
  186.0 2.4 collective-permute-start.30
  190.4 3.5 %finish.2 = (bf16[2048,512]{1,0:T(8,128)(2,1)}, f32[512,128]{1,0:T(8,128)S(1)}, f32[16,512]{1,0:T(8,128)S(1)}) custom-call(s32[2]{0:T(128)S(1)} %pad_add_fusion.sc.refs_0_, f32[2048,512]{1,0:T(8,128)S(1)} %copy-done.2, bf16[2048,512]{1,0:T(8,128)(2,1)S(1)} %bitcast.50, bf16[4,256,128]{2,1,0:T(8,128)(2,1)S(1)} %add_convert_fusion.8.refs_3_, ...), custom_call_target="tpu_custom_call" | custom-call | tf_op jit(solution)/shard_map/finish/pallas_call | solution.py:960
  193.9 5.1 %collective-permute-done.26 = bf16[8,16,2560]{2,1,0:T(8,128)(2,1)S(1)} collective-permute-done((bf16[8,16,2560]{2,1,0:T(8,128)(2,1)S(1)}, bf16[8,16,2560]{2,1,0:T(8,128)(2,1)S(1)}, u32[]{:S(2)}, u32[]{:S(2)}) %collective-permute-start.26) | collective-permute-done | bytes 655392 | tf_op jit(solution)/shard_map/ppermute | solution.py:606
  199.2 5.4 %collective-permute-done.27 = bf16[8,80,512]{2,1,0:T(8,128)(2,1)S(1)} collective-permute-done((bf16[8,80,512]{2,1,0:T(8,128)(2,1)S(1)}, bf16[8,80,512]{2,1,0:T(8,128)(2,1)S(1)}, u32[]{:S(2)}, u32[]{:S(2)}) %collective-permute-start.27) | collective-permute-done | bytes 655392 | tf_op jit(solution)/shard_map/ppermute | solution.py:606
  206.4 3.7 %finish.3 = (bf16[2048,512]{1,0:T(8,128)(2,1)}, bf16[16,16,256]{2,1,0:T(8,128)(2,1)S(1)}, bf16[16,16,256]{2,1,0:T(8,128)(2,1)S(1)}) custom-call(s32[2]{0:T(128)S(1)} %pad_add_fusion.sc.refs_0_, f32[2048,512]{1,0:T(8,128)S(1)} %copy-done.2, bf16[2048,512]{1,0:T(8,128)(2,1)S(1)} %bitcast.51, ...), custom_call_target="tpu_custom_call", output_to_operand_aliasing={{0}: (12, {})} | custom-call | tf_op jit(solution)/shard_map/finish/pallas_call | solution.py:960
  211.6 2.0 collective-permute-start.35
  213.6 2.9 %collective-permute-done.32 = bf16[8,16,256]{2,1,0:T(8,128)(2,1)S(1)} collective-permute-done((bf16[8,16,256]{2,1,0:T(8,128)(2,1)S(1)}, bf16[8,16,256]{2,1,0:T(8,128)(2,1)S(1)}, u32[]{:S(2)}, u32[]{:S(2)}) %collective-permute-start.32) | collective-permute-done | bytes 65568 | tf_op jit(solution)/shard_map/ppermute | solution.py:606
  217.7 4.8 %collective-permute-start.34 = (bf16[4,16,2560]{2,1,0:T(8,128)(2,1)S(1)}, bf16[4,16,2560]{2,1,0:T(8,128)(2,1)S(1)}, u32[]{:S(2)}, u32[]{:S(2)}) collective-permute-start(bf16[4,16,2560]{2,1,0:T(8,128)(2,1)S(1)} %get-tuple-element.119), channel_id=1, source_target_pairs={{0,8},{8,0},{16,24},{24,16},{1,9},{9,1},{17,25},{25,17},{2,10},{10... | collective-permute-start | bytes 983048 | tf_op jit(solution)/shard_map/ppermute | solution.py:606
  222.9 5.5 %collective-permute-done.34 = bf16[4,16,2560]{2,1,0:T(8,128)(2,1)S(1)} collective-permute-done((bf16[4,16,2560]{2,1,0:T(8,128)(2,1)S(1)}, bf16[4,16,2560]{2,1,0:T(8,128)(2,1)S(1)}, u32[]{:S(2)}, u32[]{:S(2)}) %collective-permute-start.34) | collective-permute-done | bytes 327712 | tf_op jit(solution)/shard_map/ppermute | solution.py:606
  228.5 1.8 collective-permute-start.36
  232.3 4.2 %collective-permute-done.38 = bf16[2,80,512]{2,1,0:T(8,128)(2,1)S(1)} collective-permute-done((bf16[2,80,512]{2,1,0:T(8,128)(2,1)S(1)}, bf16[2,80,512]{2,1,0:T(8,128)(2,1)S(1)}, u32[]{:S(2)}, u32[]{:S(2)}) %collective-permute-start.38) | collective-permute-done | bytes 163872 | tf_op jit(solution)/shard_map/ppermute | solution.py:606
  239.6 2.4 collective-permute-done.41
  247.1 2.1 collective-permute-done.39
  (137 shorter events, 46.1 us)
Async XLA Ops:
  3.0 7.8 %collective-permute-start = (bf16[1,16,768]{2,1,0:T(8,128)(2,1)S(1)}, bf16[1,16,768]{2,1,0:T(8,128)(2,1)S(1)}, u32[]{:S(2)}, u32[]{:S(2)}) collective-permute-start(bf16[1,16,768]{2,1,0:T(8,128)(2,1)S(1)} %get-tuple-element.131), channel_id=1, source_target_pairs={{0,16},{8,24},{16,0},{24,8},{1,17},{9,25},{17,1},{25,9},{2,18},{10... | collective-permute-start | bytes 73736 | tf_op jit(solution)/shard_map/ppermute | solution.py:606
  7.9 13.6 %collective-permute-start.16 = (bf16[1,80,512]{2,1,0:T(8,128)(2,1)S(1)}, bf16[1,80,512]{2,1,0:T(8,128)(2,1)S(1)}, u32[]{:S(2)}, u32[]{:S(2)}) collective-permute-start(bf16[1,80,512]{2,1,0:T(8,128)(2,1)S(1)} %maximum_bitcast_fusion), channel_id=1, source_target_pairs={{0,16},{8,24},{16,0},{24,8},{1,17},{9,25},{17,1},{25,9},{2,18},{10... | collective-permute-start | bytes 245768 | tf_op jit(solution)/shard_map/ppermute | solution.py:606
  7.9 17.8 %collective-permute-start.11 = (bf16[1,16,2048]{2,1,0:T(8,128)(2,1)}, bf16[1,16,2048]{2,1,0:T(8,128)(2,1)S(1)}, u32[]{:S(2)}, u32[]{:S(2)}) collective-permute-start(bf16[1,16,2048]{2,1,0:T(8,128)(2,1)} %bitcast.58), channel_id=1, source_target_pairs={{0,16},{8,24},{16,0},{24,8},{1,17},{9,25},{17,1},{25,9},{2,18},{10... | collective-permute-start | bytes 196616 | tf_op jit(solution)/shard_map/ppermute | solution.py:606
  21.5 5.8 %collective-permute-start.17 = (bf16[2,80,512]{2,1,0:T(8,128)(2,1)S(1)}, bf16[2,80,512]{2,1,0:T(8,128)(2,1)S(1)}, u32[]{:S(2)}, u32[]{:S(2)}) collective-permute-start(bf16[2,80,512]{2,1,0:T(8,128)(2,1)S(1)} %pad_maximum_fusion.7), channel_id=1, source_target_pairs={{0,8},{8,0},{16,24},{24,16},{1,9},{9,1},{17,25},{25,17},{2,10},{10... | collective-permute-start | bytes 491528 | tf_op jit(solution)/shard_map/ppermute | solution.py:606
  25.8 6.4 %collective-permute-start.12 = (bf16[2,16,2048]{2,1,0:T(8,128)(2,1)S(1)}, bf16[2,16,2048]{2,1,0:T(8,128)(2,1)S(1)}, u32[]{:S(2)}, u32[]{:S(2)}) collective-permute-start(bf16[2,16,2048]{2,1,0:T(8,128)(2,1)S(1)} %pad_maximum_fusion.8), channel_id=1, source_target_pairs={{0,8},{8,0},{16,24},{24,16},{1,9},{9,1},{17,25},{25,17},{2,10},{10... | collective-permute-start | bytes 393224 | tf_op jit(solution)/shard_map/ppermute | solution.py:606
  27.3 9.9 %collective-permute-start.18 = (bf16[4,80,512]{2,1,0:T(8,128)(2,1)S(1)}, bf16[4,80,512]{2,1,0:T(8,128)(2,1)S(1)}, u32[]{:S(2)}, u32[]{:S(2)}) collective-permute-start(bf16[4,80,512]{2,1,0:T(8,128)(2,1)S(1)} %pad_maximum_fusion.4), channel_id=1, source_target_pairs={{0,4},{1,5},{2,6},{3,7},{4,0},{5,1},{6,2},{7,3},{8,12},{9,13},{10,... | collective-permute-start | bytes 983048 | tf_op jit(solution)/shard_map/ppermute | solution.py:606
  31.5 8.2 %collective-permute-start.5 = (bf16[4,256,128]{2,1,0:T(8,128)(2,1)S(1)}, bf16[4,256,128]{2,1,0:T(8,128)(2,1)S(1)}, u32[]{:S(2)}, u32[]{:S(2)}) collective-permute-start(bf16[4,256,128]{2,1,0:T(8,128)(2,1)S(1)} %get-tuple-element.72.refs_5_), channel_id=1, source_target_pairs={{0,8},{8,0},{16,24},{24,16},{1,9},{9,1},{17,25},{25,17},{2,10},{10... | collective-permute-start | bytes 786440 | tf_op jit(solution)/shard_map/ppermute | solution.py:606
  32.2 9.0 %collective-permute-start.13 = (bf16[4,16,2048]{2,1,0:T(8,128)(2,1)S(1)}, bf16[4,16,2048]{2,1,0:T(8,128)(2,1)S(1)}, u32[]{:S(2)}, u32[]{:S(2)}) collective-permute-start(bf16[4,16,2048]{2,1,0:T(8,128)(2,1)S(1)} %pad_maximum_fusion.5), channel_id=1, source_target_pairs={{0,2},{1,3},{2,0},{3,1},{4,6},{5,7},{6,4},{7,5},{8,10},{9,11},{10,... | collective-permute-start | bytes 786440 | tf_op jit(solution)/shard_map/ppermute | solution.py:606
  39.7 15.7 %collective-permute-start.19 = (bf16[8,80,512]{2,1,0:T(8,128)(2,1)S(1)}, bf16[8,80,512]{2,1,0:T(8,128)(2,1)S(1)}, u32[]{:S(2)}, u32[]{:S(2)}) collective-permute-start(bf16[8,80,512]{2,1,0:T(8,128)(2,1)S(1)} %pad_maximum_fusion.2), channel_id=1, source_target_pairs={{0,2},{1,3},{2,0},{3,1},{4,6},{5,7},{6,4},{7,5},{8,10},{9,11},{10,... | collective-permute-start | bytes 1966088 | tf_op jit(solution)/shard_map/ppermute | solution.py:606
  41.2 21.3 %collective-permute-start.14 = (bf16[8,16,2048]{2,1,0:T(8,128)(2,1)S(1)}, bf16[8,16,2048]{2,1,0:T(8,128)(2,1)S(1)}, u32[]{:S(2)}, u32[]{:S(2)}) collective-permute-start(bf16[8,16,2048]{2,1,0:T(8,128)(2,1)S(1)} %pad_maximum_fusion.3), channel_id=1, source_target_pairs={{0,4},{1,5},{2,6},{3,7},{4,0},{5,1},{6,2},{7,3},{8,12},{9,13},{10,... | collective-permute-start | bytes 1572872 | tf_op jit(solution)/shard_map/ppermute | solution.py:606
  41.8 20.6 %collective-permute-start.6 = (bf16[4,256,128]{2,1,0:T(8,128)(2,1)S(1)}, bf16[4,256,128]{2,1,0:T(8,128)(2,1)S(1)}, u32[]{:S(2)}, u32[]{:S(2)}) collective-permute-start(bf16[4,256,128]{2,1,0:T(8,128)(2,1)S(1)} %get-tuple-element.72.refs_5_), channel_id=1, source_target_pairs={{0,16},{8,24},{16,0},{24,8},{1,17},{9,25},{17,1},{25,9},{2,18},{10... | collective-permute-start | bytes 786440 | tf_op jit(solution)/shard_map/ppermute | solution.py:606
  45.4 17.0 %collective-permute-start.7 = (bf16[4,256,128]{2,1,0:T(8,128)(2,1)S(1)}, bf16[4,256,128]{2,1,0:T(8,128)(2,1)S(1)}, u32[]{:S(2)}, u32[]{:S(2)}) collective-permute-start(bf16[4,256,128]{2,1,0:T(8,128)(2,1)S(1)} %get-tuple-element.72.refs_5_), channel_id=1, source_target_pairs={{0,24},{8,16},{16,8},{24,0},{1,25},{9,17},{17,9},{25,1},{2,26},{10... | collective-permute-start | bytes 786440 | tf_op jit(solution)/shard_map/ppermute | solution.py:606
  62.4 8.6 %collective-permute-start.20 = (bf16[16,80,512]{2,1,0:T(8,128)(2,1)S(1)}, bf16[16,80,512]{2,1,0:T(8,128)(2,1)S(1)}, u32[]{:S(2)}, u32[]{:S(2)}) collective-permute-start(bf16[16,80,512]{2,1,0:T(8,128)(2,1)S(1)} %pad_maximum_fusion.refs_14_), channel_id=1, source_target_pairs={{0,1},{1,0},{2,3},{3,2},{4,5},{5,4},{6,7},{7,6},{8,9},{9,8},{10,11... | collective-permute-start | bytes 3932168 | tf_op jit(solution)/shard_map/ppermute | solution.py:606
  62.6 8.3 %collective-permute-start.15 = (bf16[16,16,2048]{2,1,0:T(8,128)(2,1)S(1)}, bf16[16,16,2048]{2,1,0:T(8,128)(2,1)S(1)}, u32[]{:S(2)}, u32[]{:S(2)}) collective-permute-start(bf16[16,16,2048]{2,1,0:T(8,128)(2,1)S(1)} %pad_maximum_fusion.1.refs_12_), channel_id=1, source_target_pairs={{0,1},{1,0},{2,3},{3,2},{4,5},{5,4},{6,7},{7,6},{8,9},{9,8},{10,11... | collective-permute-start | bytes 3145736 | tf_op jit(solution)/shard_map/ppermute | solution.py:606
  63.2 53.3 %collective-permute-start.10 = (bf16[4,256,128]{2,1,0:T(8,128)(2,1)S(1)}, bf16[4,256,128]{2,1,0:T(8,128)(2,1)S(1)}, u32[]{:S(2)}, u32[]{:S(2)}) collective-permute-start(bf16[4,256,128]{2,1,0:T(8,128)(2,1)S(1)} %get-tuple-element.73.refs_5_), channel_id=1, source_target_pairs={{0,24},{8,16},{16,8},{24,0},{1,25},{9,17},{17,9},{25,1},{2,26},{10... | collective-permute-start | bytes 786440 | tf_op jit(solution)/shard_map/ppermute | solution.py:606
  66.1 51.9 %collective-permute-start.8 = (bf16[4,256,128]{2,1,0:T(8,128)(2,1)S(1)}, bf16[4,256,128]{2,1,0:T(8,128)(2,1)S(1)}, u32[]{:S(2)}, u32[]{:S(2)}) collective-permute-start(bf16[4,256,128]{2,1,0:T(8,128)(2,1)S(1)} %get-tuple-element.73.refs_5_), channel_id=1, source_target_pairs={{0,8},{8,0},{16,24},{24,16},{1,9},{9,1},{17,25},{25,17},{2,10},{10... | collective-permute-start | bytes 786440 | tf_op jit(solution)/shard_map/ppermute | solution.py:606
  71.0 47.0 %collective-permute-start.9 = (bf16[4,256,128]{2,1,0:T(8,128)(2,1)S(1)}, bf16[4,256,128]{2,1,0:T(8,128)(2,1)S(1)}, u32[]{:S(2)}, u32[]{:S(2)}) collective-permute-start(bf16[4,256,128]{2,1,0:T(8,128)(2,1)S(1)} %get-tuple-element.73.refs_5_), channel_id=1, source_target_pairs={{0,16},{8,24},{16,0},{24,8},{1,17},{9,25},{17,1},{25,9},{2,18},{10... | collective-permute-start | bytes 786440 | tf_op jit(solution)/shard_map/ppermute | solution.py:606
  113.2 59.2 %collective-permute-start.21 = (bf16[4,256,128]{2,1,0:T(8,128)(2,1)S(1)}, bf16[4,256,128]{2,1,0:T(8,128)(2,1)S(1)}, u32[]{:S(2)}, u32[]{:S(2)}) collective-permute-start(bf16[4,256,128]{2,1,0:T(8,128)(2,1)S(1)} %get-tuple-element.97), channel_id=1, source_target_pairs={{0,8},{8,0},{16,24},{24,16},{1,9},{9,1},{17,25},{25,17},{2,10},{10... | collective-permute-start | bytes 786440 | tf_op jit(solution)/shard_map/ppermute | solution.py:606
  114.7 57.7 %collective-permute-start.22 = (bf16[4,256,128]{2,1,0:T(8,128)(2,1)S(1)}, bf16[4,256,128]{2,1,0:T(8,128)(2,1)S(1)}, u32[]{:S(2)}, u32[]{:S(2)}) collective-permute-start(bf16[4,256,128]{2,1,0:T(8,128)(2,1)S(1)} %get-tuple-element.98), channel_id=1, source_target_pairs={{0,16},{8,24},{16,0},{24,8},{1,17},{9,25},{17,1},{25,9},{2,18},{10... | collective-permute-start | bytes 786440 | tf_op jit(solution)/shard_map/ppermute | solution.py:606
  116.5 55.9 %collective-permute-start.23 = (bf16[4,256,128]{2,1,0:T(8,128)(2,1)S(1)}, bf16[4,256,128]{2,1,0:T(8,128)(2,1)S(1)}, u32[]{:S(2)}, u32[]{:S(2)}) collective-permute-start(bf16[4,256,128]{2,1,0:T(8,128)(2,1)S(1)} %get-tuple-element.99), channel_id=1, source_target_pairs={{0,24},{8,16},{16,8},{24,0},{1,25},{9,17},{17,9},{25,1},{2,26},{10... | collective-permute-start | bytes 786440 | tf_op jit(solution)/shard_map/ppermute | solution.py:606
  172.6 15.8 %collective-permute-start.25 = (bf16[16,80,512]{2,1,0:T(8,128)(2,1)}, bf16[16,80,512]{2,1,0:T(8,128)(2,1)S(1)}, u32[]{:S(2)}, u32[]{:S(2)}) collective-permute-start(bf16[16,80,512]{2,1,0:T(8,128)(2,1)} %get-tuple-element.103), channel_id=1, source_target_pairs={{0,1},{1,0},{2,3},{3,2},{4,5},{5,4},{6,7},{7,6},{8,9},{9,8},{10,11... | collective-permute-start | bytes 3932168 | tf_op jit(solution)/shard_map/ppermute | solution.py:606
  177.7 21.3 %collective-permute-start.26 = (bf16[8,16,2560]{2,1,0:T(8,128)(2,1)S(1)}, bf16[8,16,2560]{2,1,0:T(8,128)(2,1)S(1)}, u32[]{:S(2)}, u32[]{:S(2)}) collective-permute-start(bf16[8,16,2560]{2,1,0:T(8,128)(2,1)S(1)} %get-tuple-element.134), channel_id=1, source_target_pairs={{0,4},{1,5},{2,6},{3,7},{4,0},{5,1},{6,2},{7,3},{8,12},{9,13},{10,... | collective-permute-start | bytes 1966088 | tf_op jit(solution)/shard_map/ppermute | solution.py:606
  184.0 20.8 %collective-permute-start.28 = (bf16[4,256,128]{2,1,0:T(8,128)(2,1)S(1)}, bf16[4,256,128]{2,1,0:T(8,128)(2,1)S(1)}, u32[]{:S(2)}, u32[]{:S(2)}) collective-permute-start(bf16[4,256,128]{2,1,0:T(8,128)(2,1)S(1)} %get-tuple-element.107), channel_id=1, source_target_pairs={{0,8},{8,0},{16,24},{24,16},{1,9},{9,1},{17,25},{25,17},{2,10},{10... | collective-permute-start | bytes 786440 | tf_op jit(solution)/shard_map/ppermute | solution.py:606
  185.0 21.4 %collective-permute-start.29 = (bf16[4,256,128]{2,1,0:T(8,128)(2,1)S(1)}, bf16[4,256,128]{2,1,0:T(8,128)(2,1)S(1)}, u32[]{:S(2)}, u32[]{:S(2)}) collective-permute-start(bf16[4,256,128]{2,1,0:T(8,128)(2,1)S(1)} %get-tuple-element.108), channel_id=1, source_target_pairs={{0,16},{8,24},{16,0},{24,8},{1,17},{9,25},{17,1},{25,9},{2,18},{10... | collective-permute-start | bytes 786440 | tf_op jit(solution)/shard_map/ppermute | solution.py:606
  186.0 20.4 %collective-permute-start.30 = (bf16[4,256,128]{2,1,0:T(8,128)(2,1)S(1)}, bf16[4,256,128]{2,1,0:T(8,128)(2,1)S(1)}, u32[]{:S(2)}, u32[]{:S(2)}) collective-permute-start(bf16[4,256,128]{2,1,0:T(8,128)(2,1)S(1)} %get-tuple-element.109), channel_id=1, source_target_pairs={{0,24},{8,16},{16,8},{24,0},{1,25},{9,17},{17,9},{25,1},{2,26},{10... | collective-permute-start | bytes 786440 | tf_op jit(solution)/shard_map/ppermute | solution.py:606
  188.9 15.7 %collective-permute-start.27 = (bf16[8,80,512]{2,1,0:T(8,128)(2,1)S(1)}, bf16[8,80,512]{2,1,0:T(8,128)(2,1)S(1)}, u32[]{:S(2)}, u32[]{:S(2)}) collective-permute-start(bf16[8,80,512]{2,1,0:T(8,128)(2,1)S(1)} %get-tuple-element.132), channel_id=1, source_target_pairs={{0,2},{1,3},{2,0},{3,1},{4,6},{5,7},{6,4},{7,5},{8,10},{9,11},{10,... | collective-permute-start | bytes 1966088 | tf_op jit(solution)/shard_map/ppermute | solution.py:606
  211.6 11.1 %collective-permute-start.35 = (bf16[4,80,512]{2,1,0:T(8,128)(2,1)S(1)}, bf16[4,80,512]{2,1,0:T(8,128)(2,1)S(1)}, u32[]{:S(2)}, u32[]{:S(2)}) collective-permute-start(bf16[4,80,512]{2,1,0:T(8,128)(2,1)S(1)} %get-tuple-element.121), channel_id=1, source_target_pairs={{0,4},{1,5},{2,6},{3,7},{4,0},{5,1},{6,2},{7,3},{8,12},{9,13},{10,... | collective-permute-start | bytes 983048 | tf_op jit(solution)/shard_map/ppermute | solution.py:606
  216.6 5.9 %collective-permute-start.33 = (bf16[4,16,256]{2,1,0:T(8,128)(2,1)S(1)}, bf16[4,16,256]{2,1,0:T(8,128)(2,1)S(1)}, u32[]{:S(2)}, u32[]{:S(2)}) collective-permute-start(bf16[4,16,256]{2,1,0:T(8,128)(2,1)S(1)} %get-tuple-element.147), channel_id=1, source_target_pairs={{0,2},{1,3},{2,0},{3,1},{4,6},{5,7},{6,4},{7,5},{8,10},{9,11},{10,... | collective-permute-start | bytes 98312 | tf_op jit(solution)/shard_map/ppermute | solution.py:606
  217.7 10.7 %collective-permute-start.34 = (bf16[4,16,2560]{2,1,0:T(8,128)(2,1)S(1)}, bf16[4,16,2560]{2,1,0:T(8,128)(2,1)S(1)}, u32[]{:S(2)}, u32[]{:S(2)}) collective-permute-start(bf16[4,16,2560]{2,1,0:T(8,128)(2,1)S(1)} %get-tuple-element.119), channel_id=1, source_target_pairs={{0,8},{8,0},{16,24},{24,16},{1,9},{9,1},{17,25},{25,17},{2,10},{10... | collective-permute-start | bytes 983048 | tf_op jit(solution)/shard_map/ppermute | solution.py:606
  230.3 6.2 %collective-permute-start.38 = (bf16[2,80,512]{2,1,0:T(8,128)(2,1)S(1)}, bf16[2,80,512]{2,1,0:T(8,128)(2,1)S(1)}, u32[]{:S(2)}, u32[]{:S(2)}) collective-permute-start(bf16[2,80,512]{2,1,0:T(8,128)(2,1)S(1)} %get-tuple-element.140), channel_id=1, source_target_pairs={{0,8},{8,0},{16,24},{24,16},{1,9},{9,1},{17,25},{25,17},{2,10},{10... | collective-permute-start | bytes 491528 | tf_op jit(solution)/shard_map/ppermute | solution.py:606
  230.6 7.6 %collective-permute-start.37 = (bf16[2,16,2560]{2,1,0:T(8,128)(2,1)S(1)}, bf16[2,16,2560]{2,1,0:T(8,128)(2,1)S(1)}, u32[]{:S(2)}, u32[]{:S(2)}) collective-permute-start(bf16[2,16,2560]{2,1,0:T(8,128)(2,1)S(1)} %get-tuple-element.142), channel_id=1, source_target_pairs={{0,2},{1,3},{2,0},{3,1},{4,6},{5,7},{6,4},{7,5},{8,10},{9,11},{10,... | collective-permute-start | bytes 491528 | tf_op jit(solution)/shard_map/ppermute | solution.py:606
  238.2 6.3 %collective-permute-start.40 = (bf16[1,16,2560]{2,1,0:T(8,128)(2,1)S(1)}, bf16[1,16,2560]{2,1,0:T(8,128)(2,1)S(1)}, u32[]{:S(2)}, u32[]{:S(2)}) collective-permute-start(bf16[1,16,2560]{2,1,0:T(8,128)(2,1)S(1)} %add_convert_fusion.15), channel_id=1, source_target_pairs={{0,16},{8,24},{16,0},{24,8},{1,17},{9,25},{17,1},{25,9},{2,18},{10... | collective-permute-start | bytes 245768 | tf_op jit(solution)/shard_map/ppermute | solution.py:606
  (28 other events, 207.9 us)

commit v4 on v3

--- a/solution.py
+++ b/solution.py
@@ -13,6 +13,7 @@
 C1 = 0.7978845608028654 * 0.044715
 PARTS = (4, 4)
 LAG = 2
+KVT = 3
 GSW = 1
 R = 2
 FC = 32
@@ -901,7 +902,7 @@
     us = [u, swap(u, core, sizes)]
     ds = [dn, swap(dn, core, sizes)]
     for kv in kv_parts[1:]:
-        gather_kv(after(kv, *kv_all[-1]))
+        gather_kv(after(kv, *kv_all[-1][:KVT]))
     dkv_all = []
 
     def moved(dkv):

time: 250 us -> 245 us (0.980)
  starting transfers between devices: 65.5 us -> 60.9 us
    ppermute x42, starting transfers between devices: 65.5 us -> 60.9 us  [swap(): return lax.ppermute(x, axis, [(i, i ^ mask) for i in range(sizes[axis])])]
  transfers between devices with their start and end apart: 42 -> 42, of which waited for: 20 -> 19; matrix products, arithmetic and copies ran while one was open for 3% -> 3% of each run, Pallas kernels for 40% -> 41%
where the time goes in v4:
time: 245 us; the launch traced here: 246 us
  Pallas kernels  104 us (42%)
  waiting for transfers between devices  65.9 us (27%)
  starting transfers between devices  60.9 us (25%)
  local copies, waits for them, and re-layouts  8.68 us (4%)
  other arithmetic  5.33 us (2%)
    pallas_call x2, Pallas kernels, layer_calls(): pl.pallas_call(functools.partial(kernel_b, cfg), grid=(steps,), out_shape...  94.4 us
    ppermute x42, waiting for transfers between devices, swap(): return lax.ppermute(x, axis, [(i, i ^ mask) for i in range(sizes[axis])])  65.9 us
    ppermute x42, starting transfers between devices, swap(): return lax.ppermute(x, axis, [(i, i ^ mask) for i in range(sizes[axis])])  60.9 us
    pallas_call x2, Pallas kernels, body(): pl.pallas_call(functools.partial(kernel_e, cfg), grid=(steps,), out_shape...  7.19 us
  transfers between devices with their start and end apart: 42, of which 19 were waited for; matrix products, arithmetic and copies ran while one was open for 3% of the time, Pallas kernels for 41%

profile of v4, /device:TPU:0, one launch (start us, length us, event | category | flops | bytes accessed | tf_op | source)
XLA Modules:
  0.0 246.2 jit_solution(12238735187814373417)
XLA Ops:
  3.0 4.0 %collective-permute-start = (bf16[1,16,768]{2,1,0:T(8,128)(2,1)S(1)}, bf16[1,16,768]{2,1,0:T(8,128)(2,1)S(1)}, u32[]{:S(2)}, u32[]{:S(2)}) collective-permute-start(bf16[1,16,768]{2,1,0:T(8,128)(2,1)S(1)} %get-tuple-element.131), channel_id=1, source_target_pairs={{0,16},{8,24},{16,0},{24,8},{1,17},{9,25},{17,1},{25,9},{2,18},{10... | collective-permute-start | bytes 73736 | tf_op jit(solution)/shard_map/ppermute | solution.py:607
  7.9 2.9 %collective-permute-start.10 = (bf16[1,16,2048]{2,1,0:T(8,128)(2,1)}, bf16[1,16,2048]{2,1,0:T(8,128)(2,1)S(1)}, u32[]{:S(2)}, u32[]{:S(2)}) collective-permute-start(bf16[1,16,2048]{2,1,0:T(8,128)(2,1)} %bitcast.58), channel_id=1, source_target_pairs={{0,16},{8,24},{16,0},{24,8},{1,17},{9,25},{17,1},{25,9},{2,18},{10... | collective-permute-start | bytes 196616 | tf_op jit(solution)/shard_map/ppermute | solution.py:607
  10.9 1.6 collective-permute-start.1
  12.5 2.7 %collective-permute-done.1 = bf16[2,16,768]{2,1,0:T(8,128)(2,1)S(1)} collective-permute-done((bf16[2,16,768]{2,1,0:T(8,128)(2,1)S(1)}, bf16[2,16,768]{2,1,0:T(8,128)(2,1)S(1)}, u32[]{:S(2)}, u32[]{:S(2)}) %collective-permute-start.1) | collective-permute-done | bytes 49184 | tf_op jit(solution)/shard_map/ppermute | solution.py:607
  16.7 3.1 %collective-permute-done.2 = bf16[4,16,768]{2,1,0:T(8,128)(2,1)S(1)} collective-permute-done((bf16[4,16,768]{2,1,0:T(8,128)(2,1)S(1)}, bf16[4,16,768]{2,1,0:T(8,128)(2,1)S(1)}, u32[]{:S(2)}, u32[]{:S(2)}) %collective-permute-start.2) | collective-permute-done | bytes 98336 | tf_op jit(solution)/shard_map/ppermute | solution.py:607
  23.0 2.6 %collective-permute-done.3 = bf16[8,16,768]{2,1,0:T(8,128)(2,1)S(1)} collective-permute-done((bf16[8,16,768]{2,1,0:T(8,128)(2,1)S(1)}, bf16[8,16,768]{2,1,0:T(8,128)(2,1)S(1)}, u32[]{:S(2)}, u32[]{:S(2)}) %collective-permute-start.3) | collective-permute-done | bytes 196640 | tf_op jit(solution)/shard_map/ppermute | solution.py:607
  29.0 2.5 %project.1 = (bf16[512,768]{1,0:T(8,128)(2,1)S(1)}, f32[16,512]{1,0:T(8,128)S(1)}, f32[8,2048]{1,0:T(8,128)S(1)}, bf16[4,256,128]{2,1,0:T(8,128)(2,1)S(1)}, bf16[4,256,128]{2,1,0:T(8,128)(2,1)S(1)}) custom-call(s32[2]{0:T(128)S(1)} %pad_add_fusion.sc.refs_0_, bf16[16,16,768]{2,1,0:T(8,128)(2,1)S(1)} %constant_dynamic-update-slice_fusion.own, ...), custom_call_target="tpu_custom_call" | custom-call | tf_op jit(solution)/shard_map/project/pallas_call | solution.py:867
  33.8 3.4 %collective-permute-done.18 = bf16[4,80,512]{2,1,0:T(8,128)(2,1)S(1)} collective-permute-done((bf16[4,80,512]{2,1,0:T(8,128)(2,1)S(1)}, bf16[4,80,512]{2,1,0:T(8,128)(2,1)S(1)}, u32[]{:S(2)}, u32[]{:S(2)}) %collective-permute-start.18) | collective-permute-done | bytes 327712 | tf_op jit(solution)/shard_map/ppermute | solution.py:607
  37.2 2.5 collective-permute-done.5.refs_6_
  41.8 3.6 %collective-permute-start.6 = (bf16[4,256,128]{2,1,0:T(8,128)(2,1)S(1)}, bf16[4,256,128]{2,1,0:T(8,128)(2,1)S(1)}, u32[]{:S(2)}, u32[]{:S(2)}) collective-permute-start(bf16[4,256,128]{2,1,0:T(8,128)(2,1)S(1)} %get-tuple-element.72.refs_5_), channel_id=1, source_target_pairs={{0,16},{8,24},{16,0},{24,8},{1,17},{9,25},{17,1},{25,9},{2,18},{10... | collective-permute-start | bytes 786440 | tf_op jit(solution)/shard_map/ppermute | solution.py:607
  46.0 9.4 %collective-permute-done.19 = bf16[8,80,512]{2,1,0:T(8,128)(2,1)S(1)} collective-permute-done((bf16[8,80,512]{2,1,0:T(8,128)(2,1)S(1)}, bf16[8,80,512]{2,1,0:T(8,128)(2,1)S(1)}, u32[]{:S(2)}, u32[]{:S(2)}) %collective-permute-start.19) | collective-permute-done | bytes 655392 | tf_op jit(solution)/shard_map/ppermute | solution.py:607
  55.5 6.9 %collective-permute-done.6.refs_7_ = bf16[4,256,128]{2,1,0:T(8,128)(2,1)S(1)} collective-permute-done((bf16[4,256,128]{2,1,0:T(8,128)(2,1)S(1)}, bf16[4,256,128]{2,1,0:T(8,128)(2,1)S(1)}, u32[]{:S(2)}, u32[]{:S(2)}) %collective-permute-start.6) | collective-permute-done | bytes 262176 | tf_op jit(solution)/shard_map/ppermute | solution.py:607
  63.2 5.3 %collective-permute-start.7 = (bf16[4,256,128]{2,1,0:T(8,128)(2,1)S(1)}, bf16[4,256,128]{2,1,0:T(8,128)(2,1)S(1)}, u32[]{:S(2)}, u32[]{:S(2)}) collective-permute-start(bf16[4,256,128]{2,1,0:T(8,128)(2,1)S(1)} %get-tuple-element.73.refs_5_), channel_id=1, source_target_pairs={{0,8},{8,0},{16,24},{24,16},{1,9},{9,1},{17,25},{25,17},{2,10},{10... | collective-permute-start | bytes 786440 | tf_op jit(solution)/shard_map/ppermute | solution.py:607
  68.5 1.9 collective-permute-start.8
  73.3 40.8 %layer.2 = (bf16[2048,512]{1,0:T(8,128)(2,1)}, f32[2048,512]{1,0:T(8,128)}, bf16[4,256,128]{2,1,0:T(8,128)(2,1)S(1)}, bf16[4,256,128]{2,1,0:T(8,128)(2,1)S(1)}, ...) custom-call(s32[2]{0:T(128)S(1)} %pad_add_fusion.sc.refs_0_, ...), custom_call_target="tpu_custom_call" | custom-call | tf_op jit(solution)/shard_map/layer/pallas_call | solution.py:736
  114.7 2.4 collective-permute-start.22
  119.5 53.6 %layer.3 = (bf16[2048,512]{1,0:T(8,128)(2,1)}, f32[2048,512]{1,0:T(8,128)}, bf16[4,256,128]{2,1,0:T(8,128)(2,1)S(1)}, bf16[4,256,128]{2,1,0:T(8,128)(2,1)S(1)}, ...) custom-call(s32[2]{0:T(128)S(1)} %pad_add_fusion.sc.refs_0_, ...), custom_call_target="tpu_custom_call", output_to_operand_aliasing={{0}: (21, {}), {1}: (22, {})} | custom-call | tf_op jit(solution)/shard_map/layer/pallas_call | solution.py:736
  173.8 2.7 %collective-permute-done.24 = bf16[16,16,2560]{2,1,0:T(8,128)(2,1)S(1)} collective-permute-done((bf16[16,16,2560]{2,1,0:T(8,128)(2,1)}, bf16[16,16,2560]{2,1,0:T(8,128)(2,1)S(1)}, u32[]{:S(2)}, u32[]{:S(2)}) %collective-permute-start.24) | collective-permute-done | bytes 1310752 | tf_op jit(solution)/shard_map/ppermute | solution.py:607
  176.5 1.9 add_convert_fusion.2
  179.5 2.8 %collective-permute-start.29 = (bf16[4,256,128]{2,1,0:T(8,128)(2,1)S(1)}, bf16[4,256,128]{2,1,0:T(8,128)(2,1)S(1)}, u32[]{:S(2)}, u32[]{:S(2)}) collective-permute-start(bf16[4,256,128]{2,1,0:T(8,128)(2,1)S(1)} %get-tuple-element.108), channel_id=1, source_target_pairs={{0,16},{8,24},{16,0},{24,8},{1,17},{9,25},{17,1},{25,9},{2,18},{10... | collective-permute-start | bytes 786440 | tf_op jit(solution)/shard_map/ppermute | solution.py:607
  185.5 3.5 %finish.2 = (bf16[2048,512]{1,0:T(8,128)(2,1)}, f32[512,128]{1,0:T(8,128)S(1)}, f32[16,512]{1,0:T(8,128)S(1)}) custom-call(s32[2]{0:T(128)S(1)} %pad_add_fusion.sc.refs_0_, f32[2048,512]{1,0:T(8,128)S(1)} %copy-done.2, bf16[2048,512]{1,0:T(8,128)(2,1)S(1)} %bitcast.50, bf16[4,256,128]{2,1,0:T(8,128)(2,1)S(1)} %add_convert_fusion.8.refs_3_, ...), custom_call_target="tpu_custom_call" | custom-call | tf_op jit(solution)/shard_map/finish/pallas_call | solution.py:961
  189.0 6.3 %collective-permute-done.26 = bf16[8,16,2560]{2,1,0:T(8,128)(2,1)S(1)} collective-permute-done((bf16[8,16,2560]{2,1,0:T(8,128)(2,1)S(1)}, bf16[8,16,2560]{2,1,0:T(8,128)(2,1)S(1)}, u32[]{:S(2)}, u32[]{:S(2)}) %collective-permute-start.26) | collective-permute-done | bytes 655392 | tf_op jit(solution)/shard_map/ppermute | solution.py:607
  195.4 4.6 %collective-permute-done.27 = bf16[8,80,512]{2,1,0:T(8,128)(2,1)S(1)} collective-permute-done((bf16[8,80,512]{2,1,0:T(8,128)(2,1)S(1)}, bf16[8,80,512]{2,1,0:T(8,128)(2,1)S(1)}, u32[]{:S(2)}, u32[]{:S(2)}) %collective-permute-start.27) | collective-permute-done | bytes 655392 | tf_op jit(solution)/shard_map/ppermute | solution.py:607
  200.8 3.7 %finish.3 = (bf16[2048,512]{1,0:T(8,128)(2,1)}, bf16[16,16,256]{2,1,0:T(8,128)(2,1)S(1)}, bf16[16,16,256]{2,1,0:T(8,128)(2,1)S(1)}) custom-call(s32[2]{0:T(128)S(1)} %pad_add_fusion.sc.refs_0_, f32[2048,512]{1,0:T(8,128)S(1)} %copy-done.2, bf16[2048,512]{1,0:T(8,128)(2,1)S(1)} %bitcast.51, ...), custom_call_target="tpu_custom_call", output_to_operand_aliasing={{0}: (12, {})} | custom-call | tf_op jit(solution)/shard_map/finish/pallas_call | solution.py:961
  208.0 2.9 %collective-permute-done.32 = bf16[8,16,256]{2,1,0:T(8,128)(2,1)S(1)} collective-permute-done((bf16[8,16,256]{2,1,0:T(8,128)(2,1)S(1)}, bf16[8,16,256]{2,1,0:T(8,128)(2,1)S(1)}, u32[]{:S(2)}, u32[]{:S(2)}) %collective-permute-start.32) | collective-permute-done | bytes 65568 | tf_op jit(solution)/shard_map/ppermute | solution.py:607
  212.1 5.1 %collective-permute-start.34 = (bf16[4,16,2560]{2,1,0:T(8,128)(2,1)S(1)}, bf16[4,16,2560]{2,1,0:T(8,128)(2,1)S(1)}, u32[]{:S(2)}, u32[]{:S(2)}) collective-permute-start(bf16[4,16,2560]{2,1,0:T(8,128)(2,1)S(1)} %get-tuple-element.119), channel_id=1, source_target_pairs={{0,8},{8,0},{16,24},{24,16},{1,9},{9,1},{17,25},{25,17},{2,10},{10... | collective-permute-start | bytes 983048 | tf_op jit(solution)/shard_map/ppermute | solution.py:607
  217.3 5.8 %collective-permute-done.34 = bf16[4,16,2560]{2,1,0:T(8,128)(2,1)S(1)} collective-permute-done((bf16[4,16,2560]{2,1,0:T(8,128)(2,1)S(1)}, bf16[4,16,2560]{2,1,0:T(8,128)(2,1)S(1)}, u32[]{:S(2)}, u32[]{:S(2)}) %collective-permute-start.34) | collective-permute-done | bytes 327712 | tf_op jit(solution)/shard_map/ppermute | solution.py:607
  223.2 1.9 collective-permute-start.36
  227.0 4.1 %collective-permute-done.38 = bf16[2,80,512]{2,1,0:T(8,128)(2,1)S(1)} collective-permute-done((bf16[2,80,512]{2,1,0:T(8,128)(2,1)S(1)}, bf16[2,80,512]{2,1,0:T(8,128)(2,1)S(1)}, u32[]{:S(2)}, u32[]{:S(2)}) %collective-permute-start.38) | collective-permute-done | bytes 163872 | tf_op jit(solution)/shard_map/ppermute | solution.py:607
  232.7 1.6 collective-permute-start.40
  234.3 2.6 %collective-permute-done.41 = bf16[1,80,512]{2,1,0:T(8,128)(2,1)S(1)} collective-permute-done((bf16[1,80,512]{2,1,0:T(8,128)(2,1)S(1)}, bf16[1,80,512]{2,1,0:T(8,128)(2,1)S(1)}, u32[]{:S(2)}, u32[]{:S(2)}) %collective-permute-start.41) | collective-permute-done | bytes 81952 | tf_op jit(solution)/shard_map/ppermute | solution.py:607
  241.7 1.9 collective-permute-done.39
  (137 shorter events, 44.4 us)
Async XLA Ops:
  3.0 7.8 %collective-permute-start = (bf16[1,16,768]{2,1,0:T(8,128)(2,1)S(1)}, bf16[1,16,768]{2,1,0:T(8,128)(2,1)S(1)}, u32[]{:S(2)}, u32[]{:S(2)}) collective-permute-start(bf16[1,16,768]{2,1,0:T(8,128)(2,1)S(1)} %get-tuple-element.131), channel_id=1, source_target_pairs={{0,16},{8,24},{16,0},{24,8},{1,17},{9,25},{17,1},{25,9},{2,18},{10... | collective-permute-start | bytes 73736 | tf_op jit(solution)/shard_map/ppermute | solution.py:607
  7.9 13.6 %collective-permute-start.16 = (bf16[1,80,512]{2,1,0:T(8,128)(2,1)S(1)}, bf16[1,80,512]{2,1,0:T(8,128)(2,1)S(1)}, u32[]{:S(2)}, u32[]{:S(2)}) collective-permute-start(bf16[1,80,512]{2,1,0:T(8,128)(2,1)S(1)} %maximum_bitcast_fusion), channel_id=1, source_target_pairs={{0,16},{8,24},{16,0},{24,8},{1,17},{9,25},{17,1},{25,9},{2,18},{10... | collective-permute-start | bytes 245768 | tf_op jit(solution)/shard_map/ppermute | solution.py:607
  7.9 17.8 %collective-permute-start.10 = (bf16[1,16,2048]{2,1,0:T(8,128)(2,1)}, bf16[1,16,2048]{2,1,0:T(8,128)(2,1)S(1)}, u32[]{:S(2)}, u32[]{:S(2)}) collective-permute-start(bf16[1,16,2048]{2,1,0:T(8,128)(2,1)} %bitcast.58), channel_id=1, source_target_pairs={{0,16},{8,24},{16,0},{24,8},{1,17},{9,25},{17,1},{25,9},{2,18},{10... | collective-permute-start | bytes 196616 | tf_op jit(solution)/shard_map/ppermute | solution.py:607
  21.5 5.8 %collective-permute-start.17 = (bf16[2,80,512]{2,1,0:T(8,128)(2,1)S(1)}, bf16[2,80,512]{2,1,0:T(8,128)(2,1)S(1)}, u32[]{:S(2)}, u32[]{:S(2)}) collective-permute-start(bf16[2,80,512]{2,1,0:T(8,128)(2,1)S(1)} %pad_maximum_fusion.7), channel_id=1, source_target_pairs={{0,8},{8,0},{16,24},{24,16},{1,9},{9,1},{17,25},{25,17},{2,10},{10... | collective-permute-start | bytes 491528 | tf_op jit(solution)/shard_map/ppermute | solution.py:607
  25.8 6.4 %collective-permute-start.11 = (bf16[2,16,2048]{2,1,0:T(8,128)(2,1)S(1)}, bf16[2,16,2048]{2,1,0:T(8,128)(2,1)S(1)}, u32[]{:S(2)}, u32[]{:S(2)}) collective-permute-start(bf16[2,16,2048]{2,1,0:T(8,128)(2,1)S(1)} %pad_maximum_fusion.8), channel_id=1, source_target_pairs={{0,8},{8,0},{16,24},{24,16},{1,9},{9,1},{17,25},{25,17},{2,10},{10... | collective-permute-start | bytes 393224 | tf_op jit(solution)/shard_map/ppermute | solution.py:607
  27.3 9.9 %collective-permute-start.18 = (bf16[4,80,512]{2,1,0:T(8,128)(2,1)S(1)}, bf16[4,80,512]{2,1,0:T(8,128)(2,1)S(1)}, u32[]{:S(2)}, u32[]{:S(2)}) collective-permute-start(bf16[4,80,512]{2,1,0:T(8,128)(2,1)S(1)} %pad_maximum_fusion.4), channel_id=1, source_target_pairs={{0,4},{1,5},{2,6},{3,7},{4,0},{5,1},{6,2},{7,3},{8,12},{9,13},{10,... | collective-permute-start | bytes 983048 | tf_op jit(solution)/shard_map/ppermute | solution.py:607
  31.5 8.2 %collective-permute-start.5 = (bf16[4,256,128]{2,1,0:T(8,128)(2,1)S(1)}, bf16[4,256,128]{2,1,0:T(8,128)(2,1)S(1)}, u32[]{:S(2)}, u32[]{:S(2)}) collective-permute-start(bf16[4,256,128]{2,1,0:T(8,128)(2,1)S(1)} %get-tuple-element.72.refs_5_), channel_id=1, source_target_pairs={{0,8},{8,0},{16,24},{24,16},{1,9},{9,1},{17,25},{25,17},{2,10},{10... | collective-permute-start | bytes 786440 | tf_op jit(solution)/shard_map/ppermute | solution.py:607
  32.2 9.0 %collective-permute-start.12 = (bf16[4,16,2048]{2,1,0:T(8,128)(2,1)S(1)}, bf16[4,16,2048]{2,1,0:T(8,128)(2,1)S(1)}, u32[]{:S(2)}, u32[]{:S(2)}) collective-permute-start(bf16[4,16,2048]{2,1,0:T(8,128)(2,1)S(1)} %pad_maximum_fusion.5), channel_id=1, source_target_pairs={{0,2},{1,3},{2,0},{3,1},{4,6},{5,7},{6,4},{7,5},{8,10},{9,11},{10,... | collective-permute-start | bytes 786440 | tf_op jit(solution)/shard_map/ppermute | solution.py:607
  39.7 15.7 %collective-permute-start.19 = (bf16[8,80,512]{2,1,0:T(8,128)(2,1)S(1)}, bf16[8,80,512]{2,1,0:T(8,128)(2,1)S(1)}, u32[]{:S(2)}, u32[]{:S(2)}) collective-permute-start(bf16[8,80,512]{2,1,0:T(8,128)(2,1)S(1)} %pad_maximum_fusion.2), channel_id=1, source_target_pairs={{0,2},{1,3},{2,0},{3,1},{4,6},{5,7},{6,4},{7,5},{8,10},{9,11},{10,... | collective-permute-start | bytes 1966088 | tf_op jit(solution)/shard_map/ppermute | solution.py:607
  41.2 21.3 %collective-permute-start.13 = (bf16[8,16,2048]{2,1,0:T(8,128)(2,1)S(1)}, bf16[8,16,2048]{2,1,0:T(8,128)(2,1)S(1)}, u32[]{:S(2)}, u32[]{:S(2)}) collective-permute-start(bf16[8,16,2048]{2,1,0:T(8,128)(2,1)S(1)} %pad_maximum_fusion.3), channel_id=1, source_target_pairs={{0,4},{1,5},{2,6},{3,7},{4,0},{5,1},{6,2},{7,3},{8,12},{9,13},{10,... | collective-permute-start | bytes 1572872 | tf_op jit(solution)/shard_map/ppermute | solution.py:607
  41.8 20.6 %collective-permute-start.6 = (bf16[4,256,128]{2,1,0:T(8,128)(2,1)S(1)}, bf16[4,256,128]{2,1,0:T(8,128)(2,1)S(1)}, u32[]{:S(2)}, u32[]{:S(2)}) collective-permute-start(bf16[4,256,128]{2,1,0:T(8,128)(2,1)S(1)} %get-tuple-element.72.refs_5_), channel_id=1, source_target_pairs={{0,16},{8,24},{16,0},{24,8},{1,17},{9,25},{17,1},{25,9},{2,18},{10... | collective-permute-start | bytes 786440 | tf_op jit(solution)/shard_map/ppermute | solution.py:607
  45.4 17.0 %collective-permute-start.14 = (bf16[4,256,128]{2,1,0:T(8,128)(2,1)S(1)}, bf16[4,256,128]{2,1,0:T(8,128)(2,1)S(1)}, u32[]{:S(2)}, u32[]{:S(2)}) collective-permute-start(bf16[4,256,128]{2,1,0:T(8,128)(2,1)S(1)} %get-tuple-element.72.refs_5_), channel_id=1, source_target_pairs={{0,24},{8,16},{16,8},{24,0},{1,25},{9,17},{17,9},{25,1},{2,26},{10... | collective-permute-start | bytes 786440 | tf_op jit(solution)/shard_map/ppermute | solution.py:607
  62.4 9.5 %collective-permute-start.20 = (bf16[16,80,512]{2,1,0:T(8,128)(2,1)S(1)}, bf16[16,80,512]{2,1,0:T(8,128)(2,1)S(1)}, u32[]{:S(2)}, u32[]{:S(2)}) collective-permute-start(bf16[16,80,512]{2,1,0:T(8,128)(2,1)S(1)} %pad_maximum_fusion.refs_14_), channel_id=1, source_target_pairs={{0,1},{1,0},{2,3},{3,2},{4,5},{5,4},{6,7},{7,6},{8,9},{9,8},{10,11... | collective-permute-start | bytes 3932168 | tf_op jit(solution)/shard_map/ppermute | solution.py:607
  62.6 9.3 %collective-permute-start.15 = (bf16[16,16,2048]{2,1,0:T(8,128)(2,1)S(1)}, bf16[16,16,2048]{2,1,0:T(8,128)(2,1)S(1)}, u32[]{:S(2)}, u32[]{:S(2)}) collective-permute-start(bf16[16,16,2048]{2,1,0:T(8,128)(2,1)S(1)} %pad_maximum_fusion.1.refs_12_), channel_id=1, source_target_pairs={{0,1},{1,0},{2,3},{3,2},{4,5},{5,4},{6,7},{7,6},{8,9},{9,8},{10,11... | collective-permute-start | bytes 3145736 | tf_op jit(solution)/shard_map/ppermute | solution.py:607
  63.2 53.9 %collective-permute-start.7 = (bf16[4,256,128]{2,1,0:T(8,128)(2,1)S(1)}, bf16[4,256,128]{2,1,0:T(8,128)(2,1)S(1)}, u32[]{:S(2)}, u32[]{:S(2)}) collective-permute-start(bf16[4,256,128]{2,1,0:T(8,128)(2,1)S(1)} %get-tuple-element.73.refs_5_), channel_id=1, source_target_pairs={{0,8},{8,0},{16,24},{24,16},{1,9},{9,1},{17,25},{25,17},{2,10},{10... | collective-permute-start | bytes 786440 | tf_op jit(solution)/shard_map/ppermute | solution.py:607
  68.5 50.1 %collective-permute-start.8 = (bf16[4,256,128]{2,1,0:T(8,128)(2,1)S(1)}, bf16[4,256,128]{2,1,0:T(8,128)(2,1)S(1)}, u32[]{:S(2)}, u32[]{:S(2)}) collective-permute-start(bf16[4,256,128]{2,1,0:T(8,128)(2,1)S(1)} %get-tuple-element.73.refs_5_), channel_id=1, source_target_pairs={{0,16},{8,24},{16,0},{24,8},{1,17},{9,25},{17,1},{25,9},{2,18},{10... | collective-permute-start | bytes 786440 | tf_op jit(solution)/shard_map/ppermute | solution.py:607
  70.4 48.2 %collective-permute-start.9 = (bf16[4,256,128]{2,1,0:T(8,128)(2,1)S(1)}, bf16[4,256,128]{2,1,0:T(8,128)(2,1)S(1)}, u32[]{:S(2)}, u32[]{:S(2)}) collective-permute-start(bf16[4,256,128]{2,1,0:T(8,128)(2,1)S(1)} %get-tuple-element.73.refs_5_), channel_id=1, source_target_pairs={{0,24},{8,16},{16,8},{24,0},{1,25},{9,17},{17,9},{25,1},{2,26},{10... | collective-permute-start | bytes 786440 | tf_op jit(solution)/shard_map/ppermute | solution.py:607
  114.1 58.9 %collective-permute-start.21 = (bf16[4,256,128]{2,1,0:T(8,128)(2,1)S(1)}, bf16[4,256,128]{2,1,0:T(8,128)(2,1)S(1)}, u32[]{:S(2)}, u32[]{:S(2)}) collective-permute-start(bf16[4,256,128]{2,1,0:T(8,128)(2,1)S(1)} %get-tuple-element.97), channel_id=1, source_target_pairs={{0,8},{8,0},{16,24},{24,16},{1,9},{9,1},{17,25},{25,17},{2,10},{10... | collective-permute-start | bytes 786440 | tf_op jit(solution)/shard_map/ppermute | solution.py:607
  114.7 58.4 %collective-permute-start.22 = (bf16[4,256,128]{2,1,0:T(8,128)(2,1)S(1)}, bf16[4,256,128]{2,1,0:T(8,128)(2,1)S(1)}, u32[]{:S(2)}, u32[]{:S(2)}) collective-permute-start(bf16[4,256,128]{2,1,0:T(8,128)(2,1)S(1)} %get-tuple-element.98), channel_id=1, source_target_pairs={{0,16},{8,24},{16,0},{24,8},{1,17},{9,25},{17,1},{25,9},{2,18},{10... | collective-permute-start | bytes 786440 | tf_op jit(solution)/shard_map/ppermute | solution.py:607
  117.1 56.0 %collective-permute-start.23 = (bf16[4,256,128]{2,1,0:T(8,128)(2,1)S(1)}, bf16[4,256,128]{2,1,0:T(8,128)(2,1)S(1)}, u32[]{:S(2)}, u32[]{:S(2)}) collective-permute-start(bf16[4,256,128]{2,1,0:T(8,128)(2,1)S(1)} %get-tuple-element.99), channel_id=1, source_target_pairs={{0,24},{8,16},{16,8},{24,0},{1,25},{9,17},{17,9},{25,1},{2,26},{10... | collective-permute-start | bytes 786440 | tf_op jit(solution)/shard_map/ppermute | solution.py:607
  173.3 10.5 %collective-permute-start.25 = (bf16[16,80,512]{2,1,0:T(8,128)(2,1)}, bf16[16,80,512]{2,1,0:T(8,128)(2,1)S(1)}, u32[]{:S(2)}, u32[]{:S(2)}) collective-permute-start(bf16[16,80,512]{2,1,0:T(8,128)(2,1)} %get-tuple-element.103), channel_id=1, source_target_pairs={{0,1},{1,0},{2,3},{3,2},{4,5},{5,4},{6,7},{7,6},{8,9},{9,8},{10,11... | collective-permute-start | bytes 3932168 | tf_op jit(solution)/shard_map/ppermute | solution.py:607
  178.4 16.8 %collective-permute-start.26 = (bf16[8,16,2560]{2,1,0:T(8,128)(2,1)S(1)}, bf16[8,16,2560]{2,1,0:T(8,128)(2,1)S(1)}, u32[]{:S(2)}, u32[]{:S(2)}) collective-permute-start(bf16[8,16,2560]{2,1,0:T(8,128)(2,1)S(1)} %get-tuple-element.134), channel_id=1, source_target_pairs={{0,4},{1,5},{2,6},{3,7},{4,0},{5,1},{6,2},{7,3},{8,12},{9,13},{10,... | collective-permute-start | bytes 1966088 | tf_op jit(solution)/shard_map/ppermute | solution.py:607
  179.4 20.8 %collective-permute-start.28 = (bf16[4,256,128]{2,1,0:T(8,128)(2,1)S(1)}, bf16[4,256,128]{2,1,0:T(8,128)(2,1)S(1)}, u32[]{:S(2)}, u32[]{:S(2)}) collective-permute-start(bf16[4,256,128]{2,1,0:T(8,128)(2,1)S(1)} %get-tuple-element.107), channel_id=1, source_target_pairs={{0,8},{8,0},{16,24},{24,16},{1,9},{9,1},{17,25},{25,17},{2,10},{10... | collective-permute-start | bytes 786440 | tf_op jit(solution)/shard_map/ppermute | solution.py:607
  179.5 21.3 %collective-permute-start.29 = (bf16[4,256,128]{2,1,0:T(8,128)(2,1)S(1)}, bf16[4,256,128]{2,1,0:T(8,128)(2,1)S(1)}, u32[]{:S(2)}, u32[]{:S(2)}) collective-permute-start(bf16[4,256,128]{2,1,0:T(8,128)(2,1)S(1)} %get-tuple-element.108), channel_id=1, source_target_pairs={{0,16},{8,24},{16,0},{24,8},{1,17},{9,25},{17,1},{25,9},{2,18},{10... | collective-permute-start | bytes 786440 | tf_op jit(solution)/shard_map/ppermute | solution.py:607
  182.2 18.6 %collective-permute-start.30 = (bf16[4,256,128]{2,1,0:T(8,128)(2,1)S(1)}, bf16[4,256,128]{2,1,0:T(8,128)(2,1)S(1)}, u32[]{:S(2)}, u32[]{:S(2)}) collective-permute-start(bf16[4,256,128]{2,1,0:T(8,128)(2,1)S(1)} %get-tuple-element.109), channel_id=1, source_target_pairs={{0,24},{8,16},{16,8},{24,0},{1,25},{9,17},{17,9},{25,1},{2,26},{10... | collective-permute-start | bytes 786440 | tf_op jit(solution)/shard_map/ppermute | solution.py:607
  184.2 15.7 %collective-permute-start.27 = (bf16[8,80,512]{2,1,0:T(8,128)(2,1)S(1)}, bf16[8,80,512]{2,1,0:T(8,128)(2,1)S(1)}, u32[]{:S(2)}, u32[]{:S(2)}) collective-permute-start(bf16[8,80,512]{2,1,0:T(8,128)(2,1)S(1)} %get-tuple-element.132), channel_id=1, source_target_pairs={{0,2},{1,3},{2,0},{3,1},{4,6},{5,7},{6,4},{7,5},{8,10},{9,11},{10,... | collective-permute-start | bytes 1966088 | tf_op jit(solution)/shard_map/ppermute | solution.py:607
  207.0 10.2 %collective-permute-start.35 = (bf16[4,80,512]{2,1,0:T(8,128)(2,1)S(1)}, bf16[4,80,512]{2,1,0:T(8,128)(2,1)S(1)}, u32[]{:S(2)}, u32[]{:S(2)}) collective-permute-start(bf16[4,80,512]{2,1,0:T(8,128)(2,1)S(1)} %get-tuple-element.121), channel_id=1, source_target_pairs={{0,4},{1,5},{2,6},{3,7},{4,0},{5,1},{6,2},{7,3},{8,12},{9,13},{10,... | collective-permute-start | bytes 983048 | tf_op jit(solution)/shard_map/ppermute | solution.py:607
  211.0 6.2 %collective-permute-start.33 = (bf16[4,16,256]{2,1,0:T(8,128)(2,1)S(1)}, bf16[4,16,256]{2,1,0:T(8,128)(2,1)S(1)}, u32[]{:S(2)}, u32[]{:S(2)}) collective-permute-start(bf16[4,16,256]{2,1,0:T(8,128)(2,1)S(1)} %get-tuple-element.147), channel_id=1, source_target_pairs={{0,2},{1,3},{2,0},{3,1},{4,6},{5,7},{6,4},{7,5},{8,10},{9,11},{10,... | collective-permute-start | bytes 98312 | tf_op jit(solution)/shard_map/ppermute | solution.py:607
  212.1 11.0 %collective-permute-start.34 = (bf16[4,16,2560]{2,1,0:T(8,128)(2,1)S(1)}, bf16[4,16,2560]{2,1,0:T(8,128)(2,1)S(1)}, u32[]{:S(2)}, u32[]{:S(2)}) collective-permute-start(bf16[4,16,2560]{2,1,0:T(8,128)(2,1)S(1)} %get-tuple-element.119), channel_id=1, source_target_pairs={{0,8},{8,0},{16,24},{24,16},{1,9},{9,1},{17,25},{25,17},{2,10},{10... | collective-permute-start | bytes 983048 | tf_op jit(solution)/shard_map/ppermute | solution.py:607
  225.1 6.1 %collective-permute-start.38 = (bf16[2,80,512]{2,1,0:T(8,128)(2,1)S(1)}, bf16[2,80,512]{2,1,0:T(8,128)(2,1)S(1)}, u32[]{:S(2)}, u32[]{:S(2)}) collective-permute-start(bf16[2,80,512]{2,1,0:T(8,128)(2,1)S(1)} %get-tuple-element.140), channel_id=1, source_target_pairs={{0,8},{8,0},{16,24},{24,16},{1,9},{9,1},{17,25},{25,17},{2,10},{10... | collective-permute-start | bytes 491528 | tf_op jit(solution)/shard_map/ppermute | solution.py:607
  225.3 7.3 %collective-permute-start.37 = (bf16[2,16,2560]{2,1,0:T(8,128)(2,1)S(1)}, bf16[2,16,2560]{2,1,0:T(8,128)(2,1)S(1)}, u32[]{:S(2)}, u32[]{:S(2)}) collective-permute-start(bf16[2,16,2560]{2,1,0:T(8,128)(2,1)S(1)} %get-tuple-element.142), channel_id=1, source_target_pairs={{0,2},{1,3},{2,0},{3,1},{4,6},{5,7},{6,4},{7,5},{8,10},{9,11},{10,... | collective-permute-start | bytes 491528 | tf_op jit(solution)/shard_map/ppermute | solution.py:607
  232.7 6.3 %collective-permute-start.40 = (bf16[1,16,2560]{2,1,0:T(8,128)(2,1)S(1)}, bf16[1,16,2560]{2,1,0:T(8,128)(2,1)S(1)}, u32[]{:S(2)}, u32[]{:S(2)}) collective-permute-start(bf16[1,16,2560]{2,1,0:T(8,128)(2,1)S(1)} %add_convert_fusion.15), channel_id=1, source_target_pairs={{0,16},{8,24},{16,0},{24,8},{1,17},{9,25},{17,1},{25,9},{2,18},{10... | collective-permute-start | bytes 245768 | tf_op jit(solution)/shard_map/ppermute | solution.py:607
  (28 other events, 202.3 us)
